TPU v7x, 256 devices: a whole 4x4x8 slice. The times are simulated.
256 devices in a mesh: red: 32 (over y, x, core), rep: 8 (over z).
Axes of the slice: x: 4, y: 4, z: 8, core: 2. Of those that a mesh axis runs over, the one named last changes fastest.
Arguments:
- amplitudes: bfloat16 [1024, 524288], P('red', 'rep'), may hold values from -6 to 6
- integrals: bfloat16 [524288, 2048], P(('red', 'rep')), may hold values from -0.03125 to 0.03125
- tile_perm: int32 [8, 32], P('rep'), may hold values from 0 to 31, each once within a row
- occ_index: int32 [4, 2, 16], replicated, may hold values from 0 to 124
- occ_energy: float32 [125], replicated, may hold values from -2 to -0.3
- block_sizes: int32 [8], replicated, may hold values from 64 to 832, as said below
- slab_irrep: int32 [1], replicated, may hold values from 0 to 7
- virt_energy: float32 [2048], replicated, may hold values from 0.2 to 4
Outputs:
- update: float32 [1024, 2048], P('red', 'rep')
Inputs may be any that keep to these rules, and one draw needn't show every extreme that they name: `block_sizes`: each a multiple of 64, together 2048. `tile_perm`: each row is a permutation.
All inputs are finite; a program needn't handle non-finite values.
Results may differ from a plain program's by a relative error of at most 0.0003.
Values may be sent and summed in bfloat16 or wider, within the bound.
No kernel may reach another device: no remote copies, remote signals or barrier semaphores. Data moves between devices by JAX's collectives and lax.ppermute only.
A program may use at most 64 MiB of HBM per device.

v0:
```python
import jax
import jax.numpy as jnp
from jax import lax
from jax.sharding import PartitionSpec as P

SUB = 64
A_SLAB = 32


def body(
    amplitudes, integrals, tile_perm, occ_index, occ_energy, block_sizes, slab_irrep, virt_energy
):
    n_red = lax.axis_size("red")
    rows = amplitudes.shape[0]
    tile = integrals.shape[0]
    pieces = amplitudes.reshape(rows, n_red, tile)
    ordered = jnp.take(pieces, tile_perm[0], axis=1)
    received = lax.all_to_all(ordered, "red", split_axis=1, concat_axis=0, tiled=True)
    local_amp = received.reshape(rows * n_red, tile)
    row_part = lax.psum_scatter(
        jnp.dot(local_amp, integrals, preferred_element_type=jnp.float32),
        "red",
        scatter_dimension=0,
        tiled=True,
    )
    ladder = lax.psum_scatter(row_part, "rep", scatter_dimension=1, tiled=True)
    n_occ = occ_energy.shape[0]
    matches = occ_index[:, :, :, None] == jnp.arange(n_occ, dtype=jnp.int32)[None, None, None, :]
    orbital_e = jnp.sum(jnp.where(matches, occ_energy[None, None, None, :], 0.0), axis=-1)
    pair_energy = (orbital_e[:, 0, :, None] + orbital_e[:, 1, None, :]).reshape(-1)
    row_energy = lax.dynamic_slice_in_dim(pair_energy, lax.axis_index("red") * rows, rows, 0)
    irreps = jnp.arange(block_sizes.shape[0], dtype=jnp.int32)
    start = jnp.sum(jnp.where(irreps < slab_irrep[0], block_sizes, 0))
    e_a = lax.dynamic_slice(virt_energy, (start,), (A_SLAB,))
    e_b = lax.dynamic_slice(virt_energy, (start,), (SUB,))
    slab_energy = (e_a[:, None] + e_b[None, :]).reshape(-1)
    columns = ladder.shape[1]
    col_energy = lax.dynamic_slice_in_dim(slab_energy, lax.axis_index("rep") * columns, columns, 0)
    return ladder / (row_energy[:, None] - col_energy[None, :])


def solution(mesh):
    placed = (P("red", "rep"), P(("red", "rep"), None), P("rep", None), P(), P(), P(), P(), P())
    return jax.shard_map(
        body, mesh=mesh, in_specs=placed, out_specs=P("red", "rep"), check_vma=False
    )
```

profile of v0, /device:TPU:2, one launch (start us, length us, event | category | flops | bytes accessed | tf_op | source)
XLA Modules:
  0.0 236.9 jit_solution(16223539452344610566)
XLA Ops:
  6.5 0.0 reduce-scatter.3.cloned.1.call-start
  6.5 0.7 fusion.1
  7.2 0.7 compare_and_fusion
  7.9 4.7 %copy.13 = bf16[4,32,8,2048]{3,2,0,1:T(8,128)(2,1)} copy(bf16[4,32,8,2048]{3,2,1,0:T(8,128)(2,1)} %bitcast.24) | data formatting | bytes 8388608 | tf_op jit(solution)/shard_map/reshape | solution.py:16
  12.6 5.0 %gather_fusion = bf16[32,32,2048]{2,1,0:T(8,128)(2,1)} fusion(bf16[32,32,2048]{2,0,1:T(8,128)(2,1)} %bitcast.23, s32[1024]{0:T(1024)S(1)} %pad_clamp_fusion), kind=kCustom, calls=%fused_computation | custom fusion | bytes 8388736 | tf_op jit(solution)/shard_map/jit(_take)/gather | solution.py:17
  17.5 0.0 slice-start
  17.5 2.8 %select_bitcast_fusion = bf16[32,32,2048]{2,0,1:T(8,128)(2,1)S(1)} fusion(bf16[32,32,2048]{2,1,0:T(8,128)(2,1)} %gather_fusion, pred[32]{0:T(512)(128)(4,1)S(1)} %compare_and_fusion), kind=kLoop, calls=%fused_computation.2 | loop fusion | flops 2097152 | bytes 8388640 | tf_op jit(solution)/shard_map/jit(_take)/select_n | solution.py:17
  20.4 0.0 slice-start.1
  20.4 57.5 %all_to_all.15 = bf16[32,32,2048]{2,0,1:T(8,128)(2,1)S(1)} all-to-all(bf16[32,32,2048]{2,0,1:T(8,128)(2,1)S(1)} %select_bitcast_fusion), channel_id=1, replica_groups=mesh['red'=32,'rep'=8] {'red'}, dimensions={1} | all-to-all | bytes 8388608 | tf_op jit(solution)/shard_map/all_to_all | solution.py:18
  77.9 0.0 slice-done
  77.9 0.0 slice-done.1
  77.9 11.1 %fusion.3 = f32[1024,2048]{1,0:T(8,128)} fusion(bf16[1024,2048]{1,0:T(8,128)(2,1)S(1)} %bitcast.25, bf16[2048,2048]{1,0:T(8,128)(2,1)S(1)} %bitcast.29), kind=kOutput, calls=%fused_computation.16 | convolution fusion | flops 8589934592 | bytes 20971520 | tf_op jit(solution)/shard_map/dot_general | solution.py:21
  89.0 0.0 copy-start.2
  89.0 0.0 copy-start
  89.0 0.0 copy-start.1
  89.0 0.0 reduce-scatter.3.cloned.1.call-update
  89.0 0.0 reduce-scatter.5.cloned.1.call-start
  89.7 0.0 copy-done.2
  89.7 0.6 fusion
  92.0 0.8 dynamic_slice.14
  92.8 0.8 dynamic_slice.13
  93.5 0.1 broadcast_add_fusion.1
  93.6 0.1 add.88
  93.7 95.8 %reduce-scatter.3.cloned.1.call-done = f32[32,2048]{1,0:T(8,128)} async-done(((f32[1024,2048]{1,0:T(8,128)}), f32[32,2048]{1,0:T(8,128)}) %reduce-scatter.3.cloned.1.call-update) | async-done | bytes 262160 | tf_op jit(solution)/shard_map/reduce_scatter | solution.py:20
  189.5 0.0 reduce-scatter.5.cloned.1.call-update
  189.5 0.0 copy-done
  189.5 0.0 copy-done.1
  189.5 0.2 select_reduce_fusion
  189.7 0.1 broadcast_add_fusion
  189.8 0.1 add.82
  189.9 0.1 dynamic_slice.15
  189.9 0.1 dynamic_slice.12
  190.0 38.6 %reduce-scatter.5.cloned.1.call-done = f32[32,256]{1,0:T(8,128)} async-done(((f32[32,2048]{1,0:T(8,128)}), f32[32,256]{1,0:T(8,128)}) %reduce-scatter.5.cloned.1.call-update) | async-done | bytes 32784 | tf_op jit(solution)/shard_map/reduce_scatter | solution.py:26
  228.6 1.5 subtract_divide_fusion
  (3 shorter events, 0.0 us)
Async XLA Ops:
  6.5 182.9 %reduce-scatter.3.cloned.1.call-start = ((), (), s32[]{:S(2)}) async-start(), calls=%async_computation.3 | async-start | bytes 8650752 | tf_op jit(solution)/shard_map/reduce_scatter | solution.py:20
  17.5 60.3 %slice-start = ((s8[8388608]{0:T(1024)(128)(4,1)}), s8[4194304]{0:T(1024)(128)(4,1)S(1)}, s32[]{:S(2)}) async-start(s8[8388608]{0:T(1024)(128)(4,1)} %bitcast.28), calls=%async_computation.5 | async-start | bytes 8388608
  20.4 57.5 %slice-start.1 = ((s8[8388608]{0:T(1024)(128)(4,1)}), s8[4194304]{0:T(1024)(128)(4,1)S(1)}, s32[]{:S(2)}) async-start(s8[8388608]{0:T(1024)(128)(4,1)} %bitcast.28), calls=%async_computation.6 | async-start | bytes 8388608
  89.0 0.7 copy-start.2
  89.0 100.5 %copy-start = (s32[4,2,16]{2,1,0:T(2,128)S(1)}, s32[4,2,16]{2,1,0:T(2,128)}, u32[]{:S(2)}) copy-start(s32[4,2,16]{2,1,0:T(2,128)} %param.11) | copy-start | bytes 1540
  89.0 100.5 %copy-start.1 = (f32[125]{0:T(128)S(1)}, f32[125]{0:T(128)}, u32[]{:S(2)}) copy-start(f32[125]{0:T(128)} %param.12) | copy-start | bytes 1504
  89.0 139.6 %reduce-scatter.5.cloned.1.call-start = ((), (), s32[]{:S(2)}) async-start(), calls=%async_computation.4 | async-start | bytes 294912 | tf_op jit(solution)/shard_map/reduce_scatter | solution.py:26
Sparse Core Ops, SparseCore 0:
  89.1 100.2 reduce-scatter.2
  192.1 36.4 reduce-scatter.4
where the time goes:
time: 237 us
  waiting for transfers between devices  134 us (57%)
  blocking collectives  57.5 us (24%)
  between operations  15.8 us (7%)
  local copies, waits for them, and re-layouts  11.6 us (5%)
  matrix products  11.1 us (5%)
  other arithmetic  6.5 us (3%)
    reduce_scatter x1, waiting for transfers between devices, body(): lax.psum_scatter(jnp.dot(local_amp, integrals, preferred_element_type=jnp...  95.8 us
    all_to_all x1, blocking collectives, body(): lax.all_to_all(ordered, 'red', split_axis=1, concat_axis=0, tiled=True)  57.5 us
    reduce_scatter x1, waiting for transfers between devices, body(): ladder = lax.psum_scatter(row_part, 'rep', scatter_dimension=1, tiled=True)  38.6 us
    dot_general x1, matrix products, body(): jnp.dot(local_amp, integrals, preferred_element_type=jnp.float32)  11.1 us
    gather x1, local copies, waits for them, and re-layouts, body(): ordered = jnp.take(pieces, tile_perm[0], axis=1)  4.97 us
  transfers between devices with their start and end apart: 2, of which 2 were waited for; matrix products, arithmetic and copies ran while one was open for 1% of the time, Pallas kernels for 0%

commit v1 on v0

v1 whole, which is shorter than its diff:
```python
import jax
import jax.numpy as jnp
from jax import lax
from jax.experimental import pallas as pl
from jax.experimental.pallas import tpu as pltpu
from jax.sharding import Mesh, PartitionSpec as P

SUB = 64
A_SLAB = 32
N_Y, N_X, N_CORE, N_REP = 4, 4, 2, 8
N_RED = N_Y * N_X * N_CORE
RED = ("y", "x", "core")
STEPS = (("x", 1), ("y", 1), ("x", 3), ("y", 3))
PIECES = 4


def step_bits(axis, mask):
    return mask * (N_CORE if axis == "x" else N_CORE * N_X)


def piece_steps(piece):
    return tuple(STEPS[(piece + k) % 4] for k in range(4))


def offsets(piece):
    steps = piece_steps(piece)
    out = []
    for pos in range(16):
        off = 0
        for k in range(4):
            if (pos >> (3 - k)) & 1:
                off ^= step_bits(*steps[k])
        out.append(off)
    return out


def swap(x, axis, mask, size):
    return lax.ppermute(x, axis, [(i, i ^ mask) for i in range(size)])


def pack_kernel(perm_ref, amp_ref, out_ref, sems):
    tile = out_ref.shape[2]

    def copy(r):
        cols = pl.ds(pl.multiple_of(perm_ref[0, r] * tile, tile), tile)
        return pltpu.make_async_copy(amp_ref.at[:, cols], out_ref.at[r], sems.at[r])

    for r in range(N_RED):
        copy(r).start()
    for r in range(N_RED):
        copy(r).wait()


def pack(amplitudes, tile_perm, tile):
    rows = amplitudes.shape[0]
    return pl.pallas_call(
        pack_kernel,
        out_shape=jax.ShapeDtypeStruct((N_RED, rows, tile), amplitudes.dtype),
        in_specs=[pl.BlockSpec(memory_space=pltpu.SMEM), pl.BlockSpec(memory_space=pl.ANY)],
        out_specs=pl.BlockSpec(memory_space=pl.ANY),
        scratch_shapes=[pltpu.SemaphoreType.DMA((N_RED,))],
        cost_estimate=pl.CostEstimate(
            flops=0, bytes_accessed=4 * amplitudes.size, transcendentals=0
        ),
    )(tile_perm, amplitudes)


def dot_kernel(half, where_ref, amp_ref, b_ref, out_ref, lhs, sems):
    rows = amp_ref.shape[1]
    step = pl.program_id(0)

    def copy(piece, pos):
        block = where_ref[0] ^ (offsets(piece)[pos] | half)
        return pltpu.make_async_copy(
            amp_ref.at[block],
            lhs.at[piece % 2, pl.ds(pos * rows, rows), :],
            sems.at[piece % 2, pos],
        )

    for piece in range(PIECES):

        @pl.when(step == 2 * piece)
        def _():
            if piece == 0:
                for pos in range(16):
                    copy(0, pos).start()
            if piece + 1 < PIECES:
                for pos in range(16):
                    copy(piece + 1, pos).start()
            for pos in range(16):
                copy(piece, pos).wait()

    slot = lax.rem(step // 2, 2)
    out_ref[0] = jnp.dot(lhs[slot], b_ref[...], preferred_element_type=jnp.float32)


def dot_half(half, where, amp, b):
    n_red, rows, tile = amp.shape
    width = b.shape[1] // N_REP
    m = rows * 16
    return pl.pallas_call(
        lambda *refs: dot_kernel(half, *refs),
        out_shape=jax.ShapeDtypeStruct((PIECES, m, 2 * width), jnp.float32),
        grid_spec=pltpu.PrefetchScalarGridSpec(
            num_scalar_prefetch=1,
            grid=(2 * PIECES,),
            in_specs=[
                pl.BlockSpec(memory_space=pl.ANY),
                pl.BlockSpec((tile, width), lambda s, w: (0, s ^ w[1])),
            ],
            out_specs=pl.BlockSpec((1, m, width), lambda s, w: (s // 2, 0, s % 2)),
            scratch_shapes=[
                pltpu.VMEM((2, m, tile), amp.dtype),
                pltpu.SemaphoreType.DMA((2, 16)),
            ],
        ),
        compiler_params=pltpu.CompilerParams(vmem_limit_bytes=24 * 1024 * 1024),
        cost_estimate=pl.CostEstimate(
            flops=2 * m * tile * b.shape[1],
            bytes_accessed=2 * tile * b.shape[1] + 2 * m * tile + 4 * m * b.shape[1],
            transcendentals=0,
        ),
    )(where, amp, b)


def body(
    amplitudes, integrals, tile_perm, occ_index, occ_energy, block_sizes, slab_irrep, virt_energy
):
    rows = amplitudes.shape[0]
    tile = integrals.shape[0]
    columns = integrals.shape[1] // N_REP
    red = (lax.axis_index("y") * N_X + lax.axis_index("x")) * N_CORE + lax.axis_index("core")
    rep = lax.axis_index("rep")
    where = jnp.stack([red, rep]).astype(jnp.int32)
    ordered = pack(amplitudes, tile_perm, tile)
    received = lax.all_to_all(ordered, RED, split_axis=0, concat_axis=0, tiled=True)
    away = dot_half(1, where, received, integrals)
    arrived = swap(away, "core", 1, 2)
    home = dot_half(0, where, received, integrals)

    terms = [[home[p], arrived[p]] for p in range(PIECES)]
    n = 16 * rows
    for k in range(4):
        n //= 2
        sent = [sum(t[n : 2 * n] for t in terms[p][1:]) + terms[p][0][n : 2 * n] for p in range(PIECES)]
        for p in range(PIECES):
            axis, mask = piece_steps(p)[k]
            got = swap(sent[p], axis, mask, 4)
            terms[p] = [t[:n] for t in terms[p]] + [got]
    pieces = []
    for p in range(PIECES):
        total = terms[p][-1]
        for t in terms[p][:-1]:
            total = total + t
        pieces.append(total)
    got = swap(jnp.concatenate([pieces[2], pieces[3]], axis=1), "rep", 4, N_REP)
    pieces = [pieces[0] + got[:, : 2 * columns], pieces[1] + got[:, 2 * columns :]]
    got = swap(pieces[1], "rep", 2, N_REP)
    near = pieces[0] + got
    got = swap(near[:, columns:], "rep", 1, N_REP)
    ladder = near[:, :columns] + got

    n_occ = occ_energy.shape[0]
    matches = occ_index[:, :, :, None] == jnp.arange(n_occ, dtype=jnp.int32)[None, None, None, :]
    orbital_e = jnp.sum(jnp.where(matches, occ_energy[None, None, None, :], 0.0), axis=-1)
    pair_energy = (orbital_e[:, 0, :, None] + orbital_e[:, 1, None, :]).reshape(-1)
    row_energy = lax.dynamic_slice_in_dim(pair_energy, red * rows, rows, 0)
    irreps = jnp.arange(block_sizes.shape[0], dtype=jnp.int32)
    start = jnp.sum(jnp.where(irreps < slab_irrep[0], block_sizes, 0))
    e_a = lax.dynamic_slice(virt_energy, (start,), (A_SLAB,))
    e_b = lax.dynamic_slice(virt_energy, (start,), (SUB,))
    slab_energy = (e_a[:, None] + e_b[None, :]).reshape(-1)
    col_energy = lax.dynamic_slice_in_dim(slab_energy, rep * columns, columns, 0)
    return ladder / (row_energy[:, None] - col_energy[None, :])


def solution(mesh):
    grid = Mesh(mesh.devices.reshape(N_Y, N_X, N_CORE, N_REP), RED + ("rep",))
    placed = (P(RED, "rep"), P(RED + ("rep",), None), P("rep", None), P(), P(), P(), P(), P())
    return jax.shard_map(
        body, mesh=grid, in_specs=placed, out_specs=P(RED, "rep"), check_vma=False
    )
```

time: 237 us -> 280 us (1.18)
  Pallas kernels: 0 us -> 150 us
  blocking collectives: 57.5 us -> 0 us
  waiting for transfers between devices: 134 us -> 80.9 us
  starting transfers between devices: 0.04 us -> 37.4 us
  between operations: 15.8 us -> 2.75 us
  matrix products: 11.1 us -> 0 us
  local copies, waits for them, and re-layouts: 11.6 us -> 5.24 us
    pallas_call x0 -> x3, Pallas kernels: none -> 150 us  [the longest x1 129 us: pack(): pl.pallas_call(pack_kernel, out_shape=jax.ShapeDtypeStruct((N_RED, rows,...]
    reduce_scatter x2 -> x0, waiting for transfers between devices: 134 us -> none  [the longest x1 95.8 us: body(): lax.psum_scatter(jnp.dot(local_amp, integrals, preferred_element_type=jnp...]
    all_to_all x1 -> x0, blocking collectives: 57.5 us -> none  [body(): lax.all_to_all(ordered, 'red', split_axis=1, concat_axis=0, tiled=True)]
    all_to_all x0 -> x1, waiting for transfers between devices: none -> 51.3 us  [body(): lax.all_to_all(ordered, RED, split_axis=0, concat_axis=0, tiled=True)]
    ppermute x0 -> x20, starting transfers between devices: none -> 29.7 us  [swap(): return lax.ppermute(x, axis, [(i, i ^ mask) for i in range(size)])]
    ppermute x0 -> x20, waiting for transfers between devices: none -> 29.6 us  [swap(): return lax.ppermute(x, axis, [(i, i ^ mask) for i in range(size)])]
    dot_general x1 -> x0, matrix products: 11.1 us -> none  [body(): jnp.dot(local_amp, integrals, preferred_element_type=jnp.float32)]
    all_to_all x0 -> x1, starting transfers between devices: none -> 7.69 us  [body(): lax.all_to_all(ordered, RED, split_axis=0, concat_axis=0, tiled=True)]
  transfers between devices with their start and end apart: 2 -> 21, of which waited for: 2 -> 14; matrix products, arithmetic and copies ran while one was open for 1% -> 1% of each run, Pallas kernels for 0% -> 4%
where the time goes in v1:
time: 280 us
  Pallas kernels  150 us (54%)
  waiting for transfers between devices  80.9 us (29%)
  starting transfers between devices  37.4 us (13%)
  local copies, waits for them, and re-layouts  5.24 us (2%)
  other arithmetic  3.95 us (1%)
    pallas_call x1, Pallas kernels, pack(): pl.pallas_call(pack_kernel, out_shape=jax.ShapeDtypeStruct((N_RED, rows,...  129 us
    all_to_all x1, waiting for transfers between devices, body(): lax.all_to_all(ordered, RED, split_axis=0, concat_axis=0, tiled=True)  51.3 us
    ppermute x20, starting transfers between devices, swap(): return lax.ppermute(x, axis, [(i, i ^ mask) for i in range(size)])  29.7 us
    ppermute x20, waiting for transfers between devices, swap(): return lax.ppermute(x, axis, [(i, i ^ mask) for i in range(size)])  29.6 us
    pallas_call x2, Pallas kernels, dot_half(): pl.pallas_call(lambda *refs: dot_kernel(half, *refs), out_shape=jax.Shape...  20.6 us
    all_to_all x1, starting transfers between devices, body(): lax.all_to_all(ordered, RED, split_axis=0, concat_axis=0, tiled=True)  7.69 us
  transfers between devices with their start and end apart: 21, of which 14 were waited for; matrix products, arithmetic and copies ran while one was open for 1% of the time, Pallas kernels for 4%

profile of v1, /device:TPU:2, one launch (start us, length us, event | category | flops | bytes accessed | tf_op | source)
XLA Modules:
  0.0 279.9 jit_solution(12297332404827378536)
XLA Ops:
  0.0 129.1 %shard_map.82 = bf16[32,32,2048]{2,1,0:T(8,128)(2,1)} custom-call(s32[1,32]{1,0:T(1,128)} %perm_ref.1, bf16[32,65536]{1,0:T(8,128)(2,1)} %amp_ref.1), custom_call_target="tpu_custom_call" | custom-call | bytes 8388608 | tf_op jit(solution)/shard_map/pallas_call | solution.py:56
  129.1 7.7 %all-to-all-start = ((bf16[32,32,2048]{2,1,0:T(8,128)(2,1)}), bf16[32,32,2048]{2,1,0:T(8,128)(2,1)}, u32[]{:S(2)}, u32[]{:S(2)}) async-start(bf16[32,32,2048]{2,1,0:T(8,128)(2,1)} %shard_map.82), calls=%async_computation | async-start | bytes 8388608 | tf_op jit(solution)/shard_map/all_to_all | solution.py:136
  136.8 0.1 pad_add_fusion.refs_0_
  136.9 51.3 %all-to-all-done.refs_1_ = bf16[32,32,2048]{2,1,0:T(8,128)(2,1)} async-done(((bf16[32,32,2048]{2,1,0:T(8,128)(2,1)}), bf16[32,32,2048]{2,1,0:T(8,128)(2,1)}, u32[]{:S(2)}, u32[]{:S(2)}) %all-to-all-start) | async-done | bytes 4194336 | tf_op jit(solution)/shard_map/all_to_all | solution.py:136
  188.2 3.4 %copy-done = bf16[2048,2048]{1,0:T(8,128)(2,1)S(1)} copy-done((bf16[2048,2048]{1,0:T(8,128)(2,1)S(1)}, bf16[2048,2048]{1,0:T(8,128)(2,1)}, u32[]{:S(2)}) %copy-start) | copy-done | bytes 8388632
  191.6 10.3 %shard_map.83 = f32[4,512,512]{2,1,0:T(8,128)S(1)} custom-call(s32[2]{0:T(128)S(1)} %pad_add_fusion.refs_0_, bf16[32,32,2048]{2,1,0:T(8,128)(2,1)} %all-to-all-done.refs_1_, bf16[2048,2048]{1,0:T(8,128)(2,1)S(1)} %copy-done), custom_call_target="tpu_custom_call" | custom-call | flops 4294967296 | bytes 14680064 | tf_op jit(solution)/shard_map/pallas_call | solution.py:101
  201.8 0.1 collective-permute-start
  201.9 10.3 %shard_map.84 = f32[4,512,512]{2,1,0:T(8,128)S(1)} custom-call(s32[2]{0:T(128)S(1)} %pad_add_fusion.refs_0_, bf16[32,32,2048]{2,1,0:T(8,128)(2,1)} %all-to-all-done.refs_1_, bf16[2048,2048]{1,0:T(8,128)(2,1)S(1)} %copy-done), custom_call_target="tpu_custom_call" | custom-call | flops 4294967296 | bytes 14680064 | tf_op jit(solution)/shard_map/pallas_call | solution.py:101
  212.3 0.5 fusion.3
  212.8 2.5 collective-permute-start.1
  215.3 1.6 collective-permute-start.9
  216.9 10.9 %collective-permute-done.1 = f32[256,512]{1,0:T(8,128)S(1)} collective-permute-done((f32[256,512]{1,0:T(8,128)S(1)}, f32[256,512]{1,0:T(8,128)S(1)}, u32[]{:S(2)}, u32[]{:S(2)}) %collective-permute-start.1) | collective-permute-done | bytes 524320 | tf_op jit(solution)/shard_map/ppermute | solution.py:38
  227.9 1.5 collective-permute-done.14
  229.3 1.2 collective-permute-done.9
  230.5 0.4 fusion.7
  230.9 0.6 collective-permute-start.2
  231.5 0.3 collective-permute-start.15
  231.8 1.8 collective-permute-start.10
  233.6 2.3 collective-permute-start.6
  235.9 2.6 collective-permute-done.2
  238.6 0.1 collective-permute-done.15
  238.7 0.1 collective-permute-done.10
  238.8 2.4 collective-permute-done.6
  241.2 0.2 fusion.11
  241.4 0.4 collective-permute-start.11
  241.8 0.6 collective-permute-start.7
  242.4 0.2 select_reduce_fusion
  242.6 2.5 collective-permute-start.16
  245.1 1.4 collective-permute-done.11
  246.5 0.3 collective-permute-done.7
  246.8 2.6 collective-permute-start.12
  249.4 1.4 collective-permute-start.8
  250.8 0.1 collective-permute-start.3
  250.9 0.8 collective-permute-done.12
  251.7 2.0 collective-permute-done.8
  253.7 0.1 fusion.14
  253.8 7.3 %collective-permute-start.13 = (f32[32,1024]{1,0:T(8,128)S(1)}, f32[32,1024]{1,0:T(8,128)S(1)}, u32[]{:S(2)}, u32[]{:S(2)}) collective-permute-start(f32[32,1024]{1,0:T(8,128)S(1)} %pad_maximum_fusion), channel_id=1, source_target_pairs={{0,4},{1,5},{2,6},{3,7},{4,0},{5,1},{6,2},{7,3},{8,12},{9,13},{10,... | collective-permute-start | bytes 393224 | tf_op jit(solution)/shard_map/ppermute | solution.py:38
  261.1 0.4 collective-permute-start.17
  262.3 3.1 %collective-permute-done.17 = f32[32,512]{1,0:T(8,128)S(1)} collective-permute-done((f32[32,512]{1,0:T(8,128)S(1)}, f32[32,512]{1,0:T(8,128)S(1)}, u32[]{:S(2)}, u32[]{:S(2)}) %collective-permute-start.17) | collective-permute-done | bytes 65568 | tf_op jit(solution)/shard_map/ppermute | solution.py:38
  265.4 2.9 %collective-permute-start.18 = (f32[32,512]{1,0:T(8,128)S(1)}, f32[32,512]{1,0:T(8,128)S(1)}, u32[]{:S(2)}, u32[]{:S(2)}) collective-permute-start(f32[32,512]{1,0:T(8,128)S(1)} %get-tuple-element.6), channel_id=1, source_target_pairs={{0,2},{1,3},{2,0},{3,1},{4,6},{5,7},{6,4},{7,5},{8,10},{9,11},{10,... | collective-permute-start | bytes 196616 | tf_op jit(solution)/shard_map/ppermute | solution.py:38
  268.3 1.8 collective-permute-start.4
  270.2 0.7 fusion.26
  272.8 0.8 dynamic_slice.14
  273.5 0.8 dynamic_slice.13
  274.3 0.9 fusion.15
  275.2 0.5 collective-permute-start.19
  276.1 3.1 %collective-permute-done.19 = f32[32,256]{1,0:T(8,128)S(1)} collective-permute-done((f32[32,256]{1,0:T(8,128)S(1)}, f32[32,256]{1,0:T(8,128)S(1)}, u32[]{:S(2)}, u32[]{:S(2)}) %collective-permute-start.19) | collective-permute-done | bytes 32800 | tf_op jit(solution)/shard_map/ppermute | solution.py:38
  279.2 0.7 fusion.25
  (31 shorter events, 0.6 us)
Async XLA Ops:
  129.1 59.1 %all-to-all-start = ((bf16[32,32,2048]{2,1,0:T(8,128)(2,1)}), bf16[32,32,2048]{2,1,0:T(8,128)(2,1)}, u32[]{:S(2)}, u32[]{:S(2)}) async-start(bf16[32,32,2048]{2,1,0:T(8,128)(2,1)} %shard_map.82), calls=%async_computation | async-start | bytes 8388608 | tf_op jit(solution)/shard_map/all_to_all | solution.py:136
  188.2 3.4 %copy-start = (bf16[2048,2048]{1,0:T(8,128)(2,1)S(1)}, bf16[2048,2048]{1,0:T(8,128)(2,1)}, u32[]{:S(2)}) copy-start(bf16[2048,2048]{1,0:T(8,128)(2,1)} %refs_2_.3) | copy-start | bytes 25165828
  201.8 10.4 %collective-permute-start = (f32[4,512,512]{2,1,0:T(8,128)S(1)}, f32[4,512,512]{2,1,0:T(8,128)S(1)}, u32[]{:S(2)}, u32[]{:S(2)}) collective-permute-start(f32[4,512,512]{2,1,0:T(8,128)S(1)} %shard_map.83), channel_id=1, source_target_pairs={{0,8},{8,0},{1,9},{9,1},{2,10},{10,2},{3,11},{11,3},{4,12},{12,4},... | collective-permute-start | bytes 12582920 | tf_op jit(solution)/shard_map/ppermute | solution.py:38
  212.2 53.1 %copy-start.1 = (f32[4,512,512]{2,1,0:T(8,128)}, f32[4,512,512]{2,1,0:T(8,128)S(1)}, u32[]{:S(2)}) copy-start(f32[4,512,512]{2,1,0:T(8,128)S(1)} %shard_map.84) | copy-start | bytes 12582916
  212.3 53.1 %copy-start.2 = (f32[4,512,512]{2,1,0:T(8,128)}, f32[4,512,512]{2,1,0:T(8,128)S(1)}, u32[]{:S(2)}) copy-start(f32[4,512,512]{2,1,0:T(8,128)S(1)} %collective-permute-done) | copy-start | bytes 12582916
  212.8 29.6 %copy-start.3 = (s32[4,2,16]{2,1,0:T(2,128)S(1)}, s32[4,2,16]{2,1,0:T(2,128)}, u32[]{:S(2)}) copy-start(s32[4,2,16]{2,1,0:T(2,128)} %param.11) | copy-start | bytes 1540
  212.8 29.6 %copy-start.4 = (f32[125]{0:T(128)S(1)}, f32[125]{0:T(128)}, u32[]{:S(2)}) copy-start(f32[125]{0:T(128)} %param.12) | copy-start | bytes 1504
  212.8 15.1 %collective-permute-start.1 = (f32[256,512]{1,0:T(8,128)S(1)}, f32[256,512]{1,0:T(8,128)S(1)}, u32[]{:S(2)}, u32[]{:S(2)}) collective-permute-start(f32[256,512]{1,0:T(8,128)S(1)} %get-tuple-element.15), channel_id=1, source_target_pairs={{0,16},{16,0},{32,48},{48,32},{1,17},{17,1},{33,49},{49,33},{2,18}... | collective-permute-start | bytes 1572872 | tf_op jit(solution)/shard_map/ppermute | solution.py:38
  215.3 14.0 %collective-permute-start.14 = (f32[256,512]{1,0:T(8,128)S(1)}, f32[256,512]{1,0:T(8,128)S(1)}, u32[]{:S(2)}, u32[]{:S(2)}) collective-permute-start(f32[256,512]{1,0:T(8,128)S(1)} %get-tuple-element.16), channel_id=1, source_target_pairs={{0,64},{64,0},{128,192},{192,128},{1,65},{65,1},{129,193},{193,129... | collective-permute-start | bytes 1572872 | tf_op jit(solution)/shard_map/ppermute | solution.py:38
  215.3 15.2 %collective-permute-start.9 = (f32[256,512]{1,0:T(8,128)S(1)}, f32[256,512]{1,0:T(8,128)S(1)}, u32[]{:S(2)}, u32[]{:S(2)}) collective-permute-start(f32[256,512]{1,0:T(8,128)S(1)} %get-tuple-element.17), channel_id=1, source_target_pairs={{0,192},{64,128},{128,64},{192,0},{1,193},{65,129},{129,65},{193,1... | collective-permute-start | bytes 1572872 | tf_op jit(solution)/shard_map/ppermute | solution.py:38
  216.9 53.3 %copy-start.5 = (s32[8]{0:T(128)S(1)}, s32[8]{0:T(128)}, u32[]{:S(2)}) copy-start(s32[8]{0:T(128)} %param.13) | copy-start | bytes 100
  216.9 13.6 %collective-permute-start.5 = (f32[256,512]{1,0:T(8,128)S(1)}, f32[256,512]{1,0:T(8,128)S(1)}, u32[]{:S(2)}, u32[]{:S(2)}) collective-permute-start(f32[256,512]{1,0:T(8,128)S(1)} %get-tuple-element.18), channel_id=1, source_target_pairs={{0,48},{16,32},{32,16},{48,0},{1,49},{17,33},{33,17},{49,1},{2,50}... | collective-permute-start | bytes 1572872 | tf_op jit(solution)/shard_map/ppermute | solution.py:38
  230.9 7.7 %collective-permute-start.2 = (f32[128,512]{1,0:T(8,128)S(1)}, f32[128,512]{1,0:T(8,128)S(1)}, u32[]{:S(2)}, u32[]{:S(2)}) collective-permute-start(f32[128,512]{1,0:T(8,128)S(1)} %get-tuple-element.11), channel_id=1, source_target_pairs={{0,64},{64,0},{128,192},{192,128},{1,65},{65,1},{129,193},{193,129... | collective-permute-start | bytes 786440 | tf_op jit(solution)/shard_map/ppermute | solution.py:38
  231.5 7.2 %collective-permute-start.15 = (f32[128,512]{1,0:T(8,128)S(1)}, f32[128,512]{1,0:T(8,128)S(1)}, u32[]{:S(2)}, u32[]{:S(2)}) collective-permute-start(f32[128,512]{1,0:T(8,128)S(1)} %get-tuple-element.12), channel_id=1, source_target_pairs={{0,48},{16,32},{32,16},{48,0},{1,49},{17,33},{33,17},{49,1},{2,50}... | collective-permute-start | bytes 786440 | tf_op jit(solution)/shard_map/ppermute | solution.py:38
  231.8 7.0 %collective-permute-start.10 = (f32[128,512]{1,0:T(8,128)S(1)}, f32[128,512]{1,0:T(8,128)S(1)}, u32[]{:S(2)}, u32[]{:S(2)}) collective-permute-start(f32[128,512]{1,0:T(8,128)S(1)} %get-tuple-element.13), channel_id=1, source_target_pairs={{0,16},{16,0},{32,48},{48,32},{1,17},{17,1},{33,49},{49,33},{2,18}... | collective-permute-start | bytes 786440 | tf_op jit(solution)/shard_map/ppermute | solution.py:38
  233.6 7.6 %collective-permute-start.6 = (f32[128,512]{1,0:T(8,128)S(1)}, f32[128,512]{1,0:T(8,128)S(1)}, u32[]{:S(2)}, u32[]{:S(2)}) collective-permute-start(f32[128,512]{1,0:T(8,128)S(1)} %get-tuple-element.14), channel_id=1, source_target_pairs={{0,192},{64,128},{128,64},{192,0},{1,193},{65,129},{129,65},{193,1... | collective-permute-start | bytes 786440 | tf_op jit(solution)/shard_map/ppermute | solution.py:38
  241.4 5.1 %collective-permute-start.11 = (f32[64,512]{1,0:T(8,128)S(1)}, f32[64,512]{1,0:T(8,128)S(1)}, u32[]{:S(2)}, u32[]{:S(2)}) collective-permute-start(f32[64,512]{1,0:T(8,128)S(1)} %get-tuple-element.9), channel_id=1, source_target_pairs={{0,64},{64,0},{128,192},{192,128},{1,65},{65,1},{129,193},{193,129... | collective-permute-start | bytes 393224 | tf_op jit(solution)/shard_map/ppermute | solution.py:38
  241.8 5.0 %collective-permute-start.7 = (f32[64,512]{1,0:T(8,128)S(1)}, f32[64,512]{1,0:T(8,128)S(1)}, u32[]{:S(2)}, u32[]{:S(2)}) collective-permute-start(f32[64,512]{1,0:T(8,128)S(1)} %get-tuple-element.10), channel_id=1, source_target_pairs={{0,16},{16,0},{32,48},{48,32},{1,17},{17,1},{33,49},{49,33},{2,18}... | collective-permute-start | bytes 393224 | tf_op jit(solution)/shard_map/ppermute | solution.py:38
  242.6 8.3 %collective-permute-start.16 = (f32[64,512]{1,0:T(8,128)S(1)}, f32[64,512]{1,0:T(8,128)S(1)}, u32[]{:S(2)}, u32[]{:S(2)}) collective-permute-start(f32[64,512]{1,0:T(8,128)S(1)} %get-tuple-element.8), channel_id=1, source_target_pairs={{0,192},{64,128},{128,64},{192,0},{1,193},{65,129},{129,65},{193,1... | collective-permute-start | bytes 393224 | tf_op jit(solution)/shard_map/ppermute | solution.py:38
  246.8 4.8 %collective-permute-start.12 = (f32[32,512]{1,0:T(8,128)S(1)}, f32[32,512]{1,0:T(8,128)S(1)}, u32[]{:S(2)}, u32[]{:S(2)}) collective-permute-start(f32[32,512]{1,0:T(8,128)S(1)} %get-tuple-element.23), channel_id=1, source_target_pairs={{0,48},{16,32},{32,16},{48,0},{1,49},{17,33},{33,17},{49,1},{2,50}... | collective-permute-start | bytes 196616 | tf_op jit(solution)/shard_map/ppermute | solution.py:38
  249.4 4.3 %collective-permute-start.8 = (f32[32,512]{1,0:T(8,128)S(1)}, f32[32,512]{1,0:T(8,128)S(1)}, u32[]{:S(2)}, u32[]{:S(2)}) collective-permute-start(f32[32,512]{1,0:T(8,128)S(1)} %get-tuple-element.22), channel_id=1, source_target_pairs={{0,64},{64,0},{128,192},{192,128},{1,65},{65,1},{129,193},{193,129... | collective-permute-start | bytes 196616 | tf_op jit(solution)/shard_map/ppermute | solution.py:38
  250.8 11.5 %collective-permute-start.3 = (f32[64,512]{1,0:T(8,128)S(1)}, f32[64,512]{1,0:T(8,128)S(1)}, u32[]{:S(2)}, u32[]{:S(2)}) collective-permute-start(f32[64,512]{1,0:T(8,128)S(1)} %get-tuple-element.7), channel_id=1, source_target_pairs={{0,48},{16,32},{32,16},{48,0},{1,49},{17,33},{33,17},{49,1},{2,50}... | collective-permute-start | bytes 393224 | tf_op jit(solution)/shard_map/ppermute | solution.py:38
  253.8 11.5 %collective-permute-start.13 = (f32[32,1024]{1,0:T(8,128)S(1)}, f32[32,1024]{1,0:T(8,128)S(1)}, u32[]{:S(2)}, u32[]{:S(2)}) collective-permute-start(f32[32,1024]{1,0:T(8,128)S(1)} %pad_maximum_fusion), channel_id=1, source_target_pairs={{0,4},{1,5},{2,6},{3,7},{4,0},{5,1},{6,2},{7,3},{8,12},{9,13},{10,... | collective-permute-start | bytes 393224 | tf_op jit(solution)/shard_map/ppermute | solution.py:38
  261.1 4.3 %collective-permute-start.17 = (f32[32,512]{1,0:T(8,128)S(1)}, f32[32,512]{1,0:T(8,128)S(1)}, u32[]{:S(2)}, u32[]{:S(2)}) collective-permute-start(f32[32,512]{1,0:T(8,128)S(1)} %get-tuple-element.19), channel_id=1, source_target_pairs={{0,16},{16,0},{32,48},{48,32},{1,17},{17,1},{33,49},{49,33},{2,18}... | collective-permute-start | bytes 196616 | tf_op jit(solution)/shard_map/ppermute | solution.py:38
  265.4 8.9 %collective-permute-start.18 = (f32[32,512]{1,0:T(8,128)S(1)}, f32[32,512]{1,0:T(8,128)S(1)}, u32[]{:S(2)}, u32[]{:S(2)}) collective-permute-start(f32[32,512]{1,0:T(8,128)S(1)} %get-tuple-element.6), channel_id=1, source_target_pairs={{0,2},{1,3},{2,0},{3,1},{4,6},{5,7},{6,4},{7,5},{8,10},{9,11},{10,... | collective-permute-start | bytes 196616 | tf_op jit(solution)/shard_map/ppermute | solution.py:38
  268.3 6.0 %collective-permute-start.4 = (f32[32,512]{1,0:T(8,128)S(1)}, f32[32,512]{1,0:T(8,128)S(1)}, u32[]{:S(2)}, u32[]{:S(2)}) collective-permute-start(f32[32,512]{1,0:T(8,128)S(1)} %get-tuple-element.5), channel_id=1, source_target_pairs={{0,192},{64,128},{128,64},{192,0},{1,193},{65,129},{129,65},{193,1... | collective-permute-start | bytes 196616 | tf_op jit(solution)/shard_map/ppermute | solution.py:38
  275.2 4.0 %collective-permute-start.19 = (f32[32,256]{1,0:T(8,128)S(1)}, f32[32,256]{1,0:T(8,128)S(1)}, u32[]{:S(2)}, u32[]{:S(2)}) collective-permute-start(f32[32,256]{1,0:T(8,128)S(1)} %slice.699), channel_id=1, source_target_pairs={{0,1},{1,0},{2,3},{3,2},{4,5},{5,4},{6,7},{7,6},{8,9},{9,8},{10,11... | collective-permute-start | bytes 98312 | tf_op jit(solution)/shard_map/ppermute | solution.py:38

commit v2 on v0

v2 whole, which is shorter than its diff:
```python
import jax
import jax.numpy as jnp
from jax import lax
from jax.experimental import pallas as pl
from jax.experimental.pallas import tpu as pltpu
from jax.sharding import Mesh, PartitionSpec as P

SUB = 64
A_SLAB = 32
N_Y, N_X, N_CORE, N_REP = 4, 4, 2, 8
N_RED = N_Y * N_X * N_CORE
RED = ("y", "x", "core")
STRIDE = {"x": N_CORE, "y": N_CORE * N_X}
ORDER = (("x", "y"), ("y", "x"))
MASKS = ((1, 3), (3, 1))
MIB = 1024 * 1024
AMP_SPACE = pl.ANY


def offset(core, half, pos):
    first, second = (STRIDE[axis] for axis in ORDER[core])
    off = (pos & 3) * second
    for k, mask in enumerate(MASKS[half]):
        if (pos >> (3 - k)) & 1:
            off ^= mask * first
    return off


def pairs(turn, mask):
    return [(i, i ^ (mask * STRIDE[ORDER[i % 2][turn]])) for i in range(N_RED)]


def where_am_i():
    return (lax.axis_index("y") * N_X + lax.axis_index("x")) * N_CORE + lax.axis_index("core")


def pack_kernel(perm_ref, amp_ref, out_ref, sems):
    tile = out_ref.shape[2]

    def copy(r):
        cols = pl.ds(pl.multiple_of(perm_ref[0, r] * tile, tile), tile)
        return pltpu.make_async_copy(amp_ref.at[:, cols], out_ref.at[r], sems.at[r])

    for r in range(N_RED):
        copy(r).start()
    for r in range(N_RED):
        copy(r).wait()


def pack(amplitudes, tile_perm, tile):
    rows = amplitudes.shape[0]
    return pl.pallas_call(
        pack_kernel,
        out_shape=jax.ShapeDtypeStruct((N_RED, rows, tile), amplitudes.dtype),
        in_specs=[pl.BlockSpec(memory_space=pltpu.SMEM), pl.BlockSpec(memory_space=AMP_SPACE)],
        out_specs=pl.BlockSpec(memory_space=pltpu.VMEM),
        scratch_shapes=[pltpu.SemaphoreType.DMA((N_RED,))],
        compiler_params=pltpu.CompilerParams(vmem_limit_bytes=16 * MIB),
        cost_estimate=pl.CostEstimate(
            flops=0, bytes_accessed=4 * amplitudes.size, transcendentals=0
        ),
    )(tile_perm, amplitudes)


def dot_kernel(other, amp_ref, b_ref, out_ref, lhs):
    rows = amp_ref.shape[1]
    width = b_ref.shape[1] // N_REP
    per = N_REP // 2
    core = lax.axis_index("core") ^ other
    me = where_am_i() ^ other
    rep = lax.axis_index("rep")
    for half in range(2):
        for pos in range(16):
            block = me ^ jnp.where(core == 0, offset(0, half, pos), offset(1, half, pos))
            lhs[pos * rows : (pos + 1) * rows, :] = amp_ref[block]

        def step(k, carry):
            place = half * per + k
            source = (place // 2 + (place % 2) * per) ^ rep
            b = b_ref[:, pl.ds(pl.multiple_of(source * width, width), width)]
            cols = pl.ds(pl.multiple_of(k * width, width), width)
            out_ref[half, :, cols] = jnp.dot(lhs[...], b, preferred_element_type=jnp.float32)
            return carry

        lax.fori_loop(0, per, step, 0)


def dot_rows(other, amp, b):
    n_red, rows, tile = amp.shape
    m, half = rows * 16, b.shape[1] // 2
    vmem = pl.BlockSpec(memory_space=pltpu.VMEM)
    return pl.pallas_call(
        lambda *refs: dot_kernel(other, *refs),
        out_shape=jax.ShapeDtypeStruct((2, m, half), jnp.float32),
        in_specs=[vmem, vmem],
        out_specs=vmem,
        scratch_shapes=[pltpu.VMEM((m, tile), amp.dtype)],
        compiler_params=pltpu.CompilerParams(vmem_limit_bytes=24 * MIB),
        cost_estimate=pl.CostEstimate(
            flops=4 * m * tile * half,
            bytes_accessed=2 * b.size + 2 * m * tile + 8 * m * half,
            transcendentals=0,
        ),
    )(amp, b)


def total(terms):
    out = terms[0]
    for t in terms[1:]:
        out = out + t
    return out


def energy_gap(
    occ_index, occ_energy, block_sizes, slab_irrep, virt_energy, red, rep, rows, columns
):
    n_occ = occ_energy.shape[0]
    matches = occ_index[:, :, :, None] == jnp.arange(n_occ, dtype=jnp.int32)[None, None, None, :]
    orbital_e = jnp.sum(jnp.where(matches, occ_energy[None, None, None, :], 0.0), axis=-1)
    pair_energy = (orbital_e[:, 0, :, None] + orbital_e[:, 1, None, :]).reshape(-1)
    row_energy = lax.dynamic_slice_in_dim(pair_energy, red * rows, rows, 0)
    irreps = jnp.arange(block_sizes.shape[0], dtype=jnp.int32)
    start = jnp.sum(jnp.where(irreps < slab_irrep[0], block_sizes, 0))
    e_a = lax.dynamic_slice(virt_energy, (start,), (A_SLAB,))
    e_b = lax.dynamic_slice(virt_energy, (start,), (SUB,))
    slab_energy = (e_a[:, None] + e_b[None, :]).reshape(-1)
    col_energy = lax.dynamic_slice_in_dim(slab_energy, rep * columns, columns, 0)
    return row_energy[:, None] - col_energy[None, :]


def body(
    amplitudes, integrals, tile_perm, occ_index, occ_energy, block_sizes, slab_irrep, virt_energy
):
    rows = amplitudes.shape[0]
    tile = integrals.shape[0]
    columns = integrals.shape[1] // N_REP
    red, rep = where_am_i(), lax.axis_index("rep")
    ordered = pack(amplitudes, tile_perm, tile)
    received = lax.all_to_all(ordered, RED, split_axis=0, concat_axis=0, tiled=True)
    away = dot_rows(1, received, integrals)
    arrived = lax.ppermute(away, "core", [(0, 1), (1, 0)])
    home = dot_rows(0, received, integrals)
    n = 8 * rows
    sends = lax.optimization_barrier([home[half, n:] + arrived[half, n:] for half in range(2)])
    gots = [lax.ppermute(sends[half], RED, pairs(0, MASKS[half][0])) for half in range(2)]
    keeps = [home[half, :n] + arrived[half, :n] for half in range(2)]
    denominator = energy_gap(
        occ_index, occ_energy, block_sizes, slab_irrep, virt_energy, red, rep, rows, columns
    )
    gots, keeps, denominator = lax.optimization_barrier((gots, keeps, denominator))
    n = 4 * rows
    sends = lax.optimization_barrier([keeps[half][n:] + gots[half][n:] for half in range(2)])
    keeps = [keeps[half][:n] + gots[half][:n] for half in range(2)]
    gots = [lax.ppermute(sends[half], RED, pairs(0, MASKS[half][1])) for half in range(2)]
    gots, keeps = lax.optimization_barrier((gots, keeps))
    mine = jnp.concatenate([keeps[half] + gots[half] for half in range(2)], axis=1)
    mine = total(
        [mine[:rows]]
        + [
            lax.ppermute(mine[k * rows : (k + 1) * rows], RED, pairs(1, k))
            for k in range(1, 4)
        ]
    )
    width = 2 * columns
    mine = total(
        [mine[:, :width]]
        + [
            lax.ppermute(mine[:, k * width : (k + 1) * width], "rep", [(i, i ^ k) for i in range(N_REP)])
            for k in range(1, 4)
        ]
    )
    got = lax.ppermute(mine[:, columns:], "rep", [(i, i ^ 4) for i in range(N_REP)])
    return (mine[:, :columns] + got) / denominator


def solution(mesh):
    grid = Mesh(mesh.devices.reshape(N_Y, N_X, N_CORE, N_REP), RED + ("rep",))
    placed = (P(RED, "rep"), P(RED + ("rep",), None), P("rep", None), P(), P(), P(), P(), P())
    return jax.shard_map(
        body, mesh=grid, in_specs=placed, out_specs=P(RED, "rep"), check_vma=False
    )
```

time: 237 us -> 138 us (0.58)
  waiting for transfers between devices: 134 us -> 30.2 us
  starting transfers between devices: 0.04 us -> 20.9 us
  Pallas kernels: 0 us -> 14.8 us
  between operations: 15.8 us -> 2.85 us
  matrix products: 11.1 us -> 0 us
  local copies, waits for them, and re-layouts: 11.6 us -> 4.74 us
    reduce_scatter x2 -> x0, waiting for transfers between devices: 134 us -> none  [the longest x1 95.8 us: body(): lax.psum_scatter(jnp.dot(local_amp, integrals, preferred_element_type=jnp...]
    ppermute x0 -> x12, waiting for transfers between devices: none -> 30.2 us  [the longest x2 9 us: body(): lax.ppermute(sends[half], RED, pairs(0, MASKS[half][0]))]
    ppermute x0 -> x12, starting transfers between devices: none -> 20.9 us  [the longest x1 5.65 us: body(): lax.ppermute(mine[:, columns:], 'rep', [(i, i ^ 4) for i in range(N_REP)])]
    pallas_call x0 -> x3, Pallas kernels: none -> 14.8 us  [the longest x2 12.4 us: dot_rows(): pl.pallas_call(lambda *refs: dot_kernel(other, *refs), out_shape=jax.Shap...]
    dot_general x1 -> x0, matrix products: 11.1 us -> none  [body(): jnp.dot(local_amp, integrals, preferred_element_type=jnp.float32)]
    gather x1 -> x0, local copies, waits for them, and re-layouts: 4.97 us -> none  [body(): ordered = jnp.take(pieces, tile_perm[0], axis=1)]
    reshape x1 -> x0, local copies, waits for them, and re-layouts: 4.71 us -> none  [body(): pieces = amplitudes.reshape(rows, n_red, tile)]
    add x2 -> x8, other arithmetic: 0.15 us -> 4.21 us  [the longest x1 1.92 us: body(): keeps = [home[half, :n] + arrived[half, :n] for half in range(2)]]
  transfers between devices with their start and end apart: 2 -> 12, of which waited for: 2 -> 10; matrix products, arithmetic and copies ran while one was open for 1% -> 2% of each run, Pallas kernels for 0% -> 5%
where the time goes in v2:
time: 138 us; the launch traced here: 137 us
  blocking collectives  57.5 us (42%)
  waiting for transfers between devices  30.2 us (22%)
  starting transfers between devices  20.9 us (15%)
  Pallas kernels  14.8 us (11%)
  other arithmetic  5.85 us (4%)
  local copies, waits for them, and re-layouts  4.74 us (3%)
  between operations  2.85 us (2%)
    all_to_all x1, blocking collectives, body(): lax.all_to_all(ordered, RED, split_axis=0, concat_axis=0, tiled=True)  57.5 us
    pallas_call x2, Pallas kernels, dot_rows(): pl.pallas_call(lambda *refs: dot_kernel(other, *refs), out_shape=jax.Shap...  12.4 us
    ppermute x2, waiting for transfers between devices, body(): lax.ppermute(sends[half], RED, pairs(0, MASKS[half][0]))  9 us
    ppermute x3, waiting for transfers between devices, body(): lax.ppermute(mine[k * rows:(k + 1) * rows], RED, pairs(1, k))  7.2 us
    ppermute x2, waiting for transfers between devices, body(): lax.ppermute(sends[half], RED, pairs(0, MASKS[half][1]))  7.16 us
    ppermute x1, starting transfers between devices, body(): lax.ppermute(mine[:, columns:], 'rep', [(i, i ^ 4) for i in range(N_REP)])  5.65 us
    ppermute x3, starting transfers between devices, body(): lax.ppermute(mine[:, k * width:(k + 1) * width], 'rep', [(i, i ^ k) for i...  5.37 us
    ppermute x3, waiting for transfers between devices, body(): lax.ppermute(mine[:, k * width:(k + 1) * width], 'rep', [(i, i ^ k) for i...  4.5 us
  transfers between devices with their start and end apart: 12, of which 10 were waited for; matrix products, arithmetic and copies ran while one was open for 2% of the time, Pallas kernels for 5%

profile of v2, /device:TPU:2, one launch (start us, length us, event | category | flops | bytes accessed | tf_op | source)
XLA Modules:
  0.0 136.8 jit_solution(15681340825967672674)
XLA Ops:
  0.0 2.2 %copy-done.1 = bf16[32,65536]{1,0:T(8,128)(2,1)S(1)} copy-done((bf16[32,65536]{1,0:T(8,128)(2,1)S(1)}, bf16[32,65536]{1,0:T(8,128)(2,1)}, u32[]{:S(2)}) %copy-start.1) | copy-done | bytes 4194328
  2.2 0.7 copy-done.2
  2.8 2.4 %shard_map.82 = bf16[32,32,2048]{2,1,0:T(8,128)(2,1)S(1)} custom-call(s32[1,32]{1,0:T(1,128)S(1)} %copy-done.2, bf16[32,65536]{1,0:T(8,128)(2,1)S(1)} %copy-done.1), custom_call_target="tpu_custom_call" | custom-call | bytes 8388608 | tf_op jit(solution)/shard_map/pallas_call | solution.py:52
  5.2 0.0 copy-start
  5.2 57.5 %all_to_all.5.refs_0_ = bf16[32,32,2048]{2,1,0:T(8,128)(2,1)S(1)} all-to-all(bf16[32,32,2048]{2,1,0:T(8,128)(2,1)S(1)} %shard_map.82), channel_id=1, replica_groups=mesh['y'=4,'x'=4,'core'=2,'rep'=8] {'y','x','core'}, dimensions={0} | all-to-all | bytes 8388608 | tf_op jit(solution)/shard_map/all_to_all | solution.py:139
  62.7 6.2 %shard_map.84 = f32[2,512,1024]{2,1,0:T(8,128)S(1)} custom-call(bf16[32,32,2048]{2,1,0:T(8,128)(2,1)S(1)} %all_to_all.5.refs_0_, bf16[2048,2048]{1,0:T(8,128)(2,1)S(1)} %copy-done), custom_call_target="tpu_custom_call" | custom-call | flops 4294967296 | bytes 14680064 | tf_op jit(solution)/shard_map/pallas_call | solution.py:92
  68.9 0.3 collective-permute-start
  69.9 6.2 %shard_map.83 = f32[2,512,1024]{2,1,0:T(8,128)S(1)} custom-call(bf16[32,32,2048]{2,1,0:T(8,128)(2,1)S(1)} %all_to_all.5.refs_0_, bf16[2048,2048]{1,0:T(8,128)(2,1)S(1)} %copy-done), custom_call_target="tpu_custom_call" | custom-call | flops 4294967296 | bytes 14680064 | tf_op jit(solution)/shard_map/pallas_call | solution.py:92
  76.1 0.0 copy-start.3
  76.1 0.0 copy-start.4
  76.1 0.1 collective-permute-done
  76.2 1.9 %fusion = (f32[256,1024]{1,0:T(8,128)S(1)}, f32[256,1024]{1,0:T(8,128)S(1)}, f32[256,1024]{1,0:T(8,128)S(1)}, f32[256,1024]{1,0:T(8,128)}) fusion(f32[2,512,1024]{2,1,0:T(8,128)S(1)} %collective-permute-done, f32[2,512,1024]{2,1,0:T(8,128)S(1)} %shard_map.83), kind=kLoop, calls=%fused_computation.7 | loop fusion | flops 1048576 | bytes 12582912 | tf_op jit(solution)/shard_map/add | solution.py:146
  78.1 1.5 %collective-permute-start.1 = (f32[256,1024]{1,0:T(8,128)}, f32[256,1024]{1,0:T(8,128)}, u32[]{:S(2)}, u32[]{:S(2)}) collective-permute-start(f32[256,1024]{1,0:T(8,128)} %get-tuple-element.18), channel_id=1, source_target_pairs={{0,16},{8,72},{16,0},{24,88},{32,48},{40,104},{48,32},{56,120},{64... | collective-permute-start | bytes 3145736 | tf_op jit(solution)/shard_map/ppermute | solution.py:145
  79.6 0.8 collective-permute-start.2
  80.4 0.7 fusion.13
  83.2 0.8 dynamic_slice.14
  84.0 0.8 dynamic_slice.13
  84.7 0.1 broadcast_add_fusion.1
  84.8 0.1 add.138
  84.9 0.2 select_reduce_fusion
  85.1 0.1 broadcast_add_fusion
  85.2 0.1 add.130
  85.2 0.1 dynamic_slice.15
  85.3 0.1 dynamic_slice.12
  85.4 0.1 broadcast_subtract_fusion
  85.5 7.8 %collective-permute-done.1 = f32[256,1024]{1,0:T(8,128)} collective-permute-done((f32[256,1024]{1,0:T(8,128)}, f32[256,1024]{1,0:T(8,128)}, u32[]{:S(2)}, u32[]{:S(2)}) %collective-permute-start.1) | collective-permute-done | bytes 1048608 | tf_op jit(solution)/shard_map/ppermute | solution.py:145
  93.2 1.3 collective-permute-done.2
  94.5 1.9 %slice_add_fusion.4 = (f32[128,1024]{1,0:T(8,128)S(1)}, f32[128,1024]{1,0:T(8,128)S(1)}, f32[128,1024]{1,0:T(8,128)S(1)}, f32[128,1024]{1,0:T(8,128)S(1)}) fusion(f32[256,1024]{1,0:T(8,128)} %collective-permute-done.2, f32[256,1024]{1,0:T(8,128)S(1)} %get-tuple-element.22, f32[256,1024]{1,0:T(8,128)} %collective-permute-done.1, ...), kind=kLoop, calls=%fused_computation.14 | loop fusion | flops 524288 | bytes 6291456 | tf_op jit(solution)/shard_map/add | solution.py:153
  96.4 0.9 collective-permute-start.3
  97.3 2.2 %collective-permute-start.4 = (f32[128,1024]{1,0:T(8,128)S(1)}, f32[128,1024]{1,0:T(8,128)S(1)}, u32[]{:S(2)}, u32[]{:S(2)}) collective-permute-start(f32[128,1024]{1,0:T(8,128)S(1)} %get-tuple-element.25), channel_id=1, source_target_pairs={{0,16},{8,72},{16,0},{24,88},{32,48},{40,104},{48,32},{56,120},{64... | collective-permute-start | bytes 1572872 | tf_op jit(solution)/shard_map/ppermute | solution.py:154
  99.5 6.1 %collective-permute-done.3 = f32[128,1024]{1,0:T(8,128)S(1)} collective-permute-done((f32[128,1024]{1,0:T(8,128)S(1)}, f32[128,1024]{1,0:T(8,128)S(1)}, u32[]{:S(2)}, u32[]{:S(2)}) %collective-permute-start.3) | collective-permute-done | bytes 524320 | tf_op jit(solution)/shard_map/ppermute | solution.py:154
  105.6 1.0 collective-permute-done.4
  106.7 0.1 add.144
  106.7 0.1 add.145
  106.8 0.1 fusion.9
  106.9 1.1 collective-permute-start.7
  107.9 1.7 %collective-permute-start.6 = (f32[32,2048]{1,0:T(8,128)S(1)}, f32[32,2048]{1,0:T(8,128)S(1)}, u32[]{:S(2)}, u32[]{:S(2)}) collective-permute-start(f32[32,2048]{1,0:T(8,128)S(1)} %get-tuple-element.41), channel_id=1, source_target_pairs={{0,128},{8,40},{16,144},{24,56},{32,160},{40,8},{48,176},{56,24},{... | collective-permute-start | bytes 786440 | tf_op jit(solution)/shard_map/ppermute | solution.py:160
  109.6 1.4 %collective-permute-start.5 = (f32[32,2048]{1,0:T(8,128)S(1)}, f32[32,2048]{1,0:T(8,128)S(1)}, u32[]{:S(2)}, u32[]{:S(2)}) collective-permute-start(f32[32,2048]{1,0:T(8,128)S(1)} %get-tuple-element.39), channel_id=1, source_target_pairs={{0,64},{8,24},{16,80},{24,8},{32,96},{40,56},{48,112},{56,40},{64,... | collective-permute-start | bytes 786440 | tf_op jit(solution)/shard_map/ppermute | solution.py:160
  111.0 6.3 %collective-permute-done.7 = f32[32,2048]{1,0:T(8,128)S(1)} collective-permute-done((f32[32,2048]{1,0:T(8,128)S(1)}, f32[32,2048]{1,0:T(8,128)S(1)}, u32[]{:S(2)}, u32[]{:S(2)}) %collective-permute-start.7) | collective-permute-done | bytes 262176 | tf_op jit(solution)/shard_map/ppermute | solution.py:160
  117.3 0.9 collective-permute-done.5
  118.2 0.1 fusion.8
  118.3 4.7 %collective-permute-start.10 = (f32[32,512]{1,0:T(8,128)S(1)}, f32[32,512]{1,0:T(8,128)S(1)}, u32[]{:S(2)}, u32[]{:S(2)}) collective-permute-start(f32[32,512]{1,0:T(8,128)S(1)} %get-tuple-element.43), channel_id=1, source_target_pairs={{0,3},{1,2},{2,1},{3,0},{4,7},{5,6},{6,5},{7,4},{8,11},{9,10},{10,... | collective-permute-start | bytes 196616 | tf_op jit(solution)/shard_map/ppermute | solution.py:168
  123.1 0.7 collective-permute-start.8
  123.7 2.1 %collective-permute-done.10 = f32[32,512]{1,0:T(8,128)S(1)} collective-permute-done((f32[32,512]{1,0:T(8,128)S(1)}, f32[32,512]{1,0:T(8,128)S(1)}, u32[]{:S(2)}, u32[]{:S(2)}) %collective-permute-start.10) | collective-permute-done | bytes 65568 | tf_op jit(solution)/shard_map/ppermute | solution.py:168
  125.8 2.4 %collective-permute-done.9 = f32[32,512]{1,0:T(8,128)S(1)} collective-permute-done((f32[32,512]{1,0:T(8,128)S(1)}, f32[32,512]{1,0:T(8,128)S(1)}, u32[]{:S(2)}, u32[]{:S(2)}) %collective-permute-start.9) | collective-permute-done | bytes 65568 | tf_op jit(solution)/shard_map/ppermute | solution.py:168
  128.3 5.7 %collective-permute-start.11 = (f32[32,256]{1,0:T(8,128)S(1)}, f32[32,256]{1,0:T(8,128)S(1)}, u32[]{:S(2)}, u32[]{:S(2)}) collective-permute-start(f32[32,256]{1,0:T(8,128)S(1)} %slice.133), channel_id=1, source_target_pairs={{0,4},{1,5},{2,6},{3,7},{4,0},{5,1},{6,2},{7,3},{8,12},{9,13},{10,... | collective-permute-start | bytes 98312 | tf_op jit(solution)/shard_map/ppermute | solution.py:172
  133.9 2.3 %collective-permute-done.11 = f32[32,256]{1,0:T(8,128)S(1)} collective-permute-done((f32[32,256]{1,0:T(8,128)S(1)}, f32[32,256]{1,0:T(8,128)S(1)}, u32[]{:S(2)}, u32[]{:S(2)}) %collective-permute-start.11) | collective-permute-done | bytes 32800 | tf_op jit(solution)/shard_map/ppermute | solution.py:172
  136.2 0.6 fusion.12
  (14 shorter events, 0.1 us)
Async XLA Ops:
  0.0 2.2 %copy-start.1 = (bf16[32,65536]{1,0:T(8,128)(2,1)S(1)}, bf16[32,65536]{1,0:T(8,128)(2,1)}, u32[]{:S(2)}) copy-start(bf16[32,65536]{1,0:T(8,128)(2,1)} %amp_ref.1) | copy-start | bytes 12582916
  2.2 0.7 copy-start.2
  5.2 57.5 %copy-start = (bf16[2048,2048]{1,0:T(8,128)(2,1)S(1)}, bf16[2048,2048]{1,0:T(8,128)(2,1)}, u32[]{:S(2)}) copy-start(bf16[2048,2048]{1,0:T(8,128)(2,1)} %refs_1_.3) | copy-start | bytes 25165828
  68.9 7.2 %collective-permute-start = (f32[2,512,1024]{2,1,0:T(8,128)S(1)}, f32[2,512,1024]{2,1,0:T(8,128)S(1)}, u32[]{:S(2)}, u32[]{:S(2)}) collective-permute-start(f32[2,512,1024]{2,1,0:T(8,128)S(1)} %shard_map.84), channel_id=1, source_target_pairs={{0,8},{8,0},{1,9},{9,1},{2,10},{10,2},{3,11},{11,3},{4,12},{12,4},... | collective-permute-start | bytes 12582920 | tf_op jit(solution)/shard_map/ppermute | solution.py:141
  76.1 4.3 %copy-start.5 = (s32[8]{0:T(128)S(1)}, s32[8]{0:T(128)}, u32[]{:S(2)}) copy-start(s32[8]{0:T(128)} %param.13) | copy-start | bytes 100
  76.1 8.8 %copy-start.3 = (s32[4,2,16]{2,1,0:T(2,128)S(1)}, s32[4,2,16]{2,1,0:T(2,128)}, u32[]{:S(2)}) copy-start(s32[4,2,16]{2,1,0:T(2,128)} %param.11) | copy-start | bytes 1540
  76.1 8.8 %copy-start.4 = (f32[125]{0:T(128)S(1)}, f32[125]{0:T(128)}, u32[]{:S(2)}) copy-start(f32[125]{0:T(128)} %param.12) | copy-start | bytes 1504
  78.1 15.1 %collective-permute-start.1 = (f32[256,1024]{1,0:T(8,128)}, f32[256,1024]{1,0:T(8,128)}, u32[]{:S(2)}, u32[]{:S(2)}) collective-permute-start(f32[256,1024]{1,0:T(8,128)} %get-tuple-element.18), channel_id=1, source_target_pairs={{0,16},{8,72},{16,0},{24,88},{32,48},{40,104},{48,32},{56,120},{64... | collective-permute-start | bytes 3145736 | tf_op jit(solution)/shard_map/ppermute | solution.py:145
  79.6 14.9 %collective-permute-start.2 = (f32[256,1024]{1,0:T(8,128)S(1)}, f32[256,1024]{1,0:T(8,128)}, u32[]{:S(2)}, u32[]{:S(2)}) collective-permute-start(f32[256,1024]{1,0:T(8,128)S(1)} %get-tuple-element.19), channel_id=1, source_target_pairs={{0,48},{8,200},{16,32},{24,216},{32,16},{40,232},{48,0},{56,248},{... | collective-permute-start | bytes 3145736 | tf_op jit(solution)/shard_map/ppermute | solution.py:145
  96.4 9.3 %collective-permute-start.3 = (f32[128,1024]{1,0:T(8,128)S(1)}, f32[128,1024]{1,0:T(8,128)S(1)}, u32[]{:S(2)}, u32[]{:S(2)}) collective-permute-start(f32[128,1024]{1,0:T(8,128)S(1)} %get-tuple-element.24), channel_id=1, source_target_pairs={{0,48},{8,200},{16,32},{24,216},{32,16},{40,232},{48,0},{56,248},{... | collective-permute-start | bytes 1572872 | tf_op jit(solution)/shard_map/ppermute | solution.py:154
  97.3 9.4 %collective-permute-start.4 = (f32[128,1024]{1,0:T(8,128)S(1)}, f32[128,1024]{1,0:T(8,128)S(1)}, u32[]{:S(2)}, u32[]{:S(2)}) collective-permute-start(f32[128,1024]{1,0:T(8,128)S(1)} %get-tuple-element.25), channel_id=1, source_target_pairs={{0,16},{8,72},{16,0},{24,88},{32,48},{40,104},{48,32},{56,120},{64... | collective-permute-start | bytes 1572872 | tf_op jit(solution)/shard_map/ppermute | solution.py:154
  106.9 10.5 %collective-permute-start.7 = (f32[32,2048]{1,0:T(8,128)S(1)}, f32[32,2048]{1,0:T(8,128)S(1)}, u32[]{:S(2)}, u32[]{:S(2)}) collective-permute-start(f32[32,2048]{1,0:T(8,128)S(1)} %get-tuple-element.40), channel_id=1, source_target_pairs={{0,192},{8,56},{16,208},{24,40},{32,224},{40,24},{48,240},{56,8},{... | collective-permute-start | bytes 786440 | tf_op jit(solution)/shard_map/ppermute | solution.py:160
  107.9 9.4 %collective-permute-start.6 = (f32[32,2048]{1,0:T(8,128)S(1)}, f32[32,2048]{1,0:T(8,128)S(1)}, u32[]{:S(2)}, u32[]{:S(2)}) collective-permute-start(f32[32,2048]{1,0:T(8,128)S(1)} %get-tuple-element.41), channel_id=1, source_target_pairs={{0,128},{8,40},{16,144},{24,56},{32,160},{40,8},{48,176},{56,24},{... | collective-permute-start | bytes 786440 | tf_op jit(solution)/shard_map/ppermute | solution.py:160
  109.6 8.6 %collective-permute-start.5 = (f32[32,2048]{1,0:T(8,128)S(1)}, f32[32,2048]{1,0:T(8,128)S(1)}, u32[]{:S(2)}, u32[]{:S(2)}) collective-permute-start(f32[32,2048]{1,0:T(8,128)S(1)} %get-tuple-element.39), channel_id=1, source_target_pairs={{0,64},{8,24},{16,80},{24,8},{32,96},{40,56},{48,112},{56,40},{64,... | collective-permute-start | bytes 786440 | tf_op jit(solution)/shard_map/ppermute | solution.py:160
  118.3 7.5 %collective-permute-start.10 = (f32[32,512]{1,0:T(8,128)S(1)}, f32[32,512]{1,0:T(8,128)S(1)}, u32[]{:S(2)}, u32[]{:S(2)}) collective-permute-start(f32[32,512]{1,0:T(8,128)S(1)} %get-tuple-element.43), channel_id=1, source_target_pairs={{0,3},{1,2},{2,1},{3,0},{4,7},{5,6},{6,5},{7,4},{8,11},{9,10},{10,... | collective-permute-start | bytes 196616 | tf_op jit(solution)/shard_map/ppermute | solution.py:168
  123.1 5.2 %collective-permute-start.9 = (f32[32,512]{1,0:T(8,128)S(1)}, f32[32,512]{1,0:T(8,128)S(1)}, u32[]{:S(2)}, u32[]{:S(2)}) collective-permute-start(f32[32,512]{1,0:T(8,128)S(1)} %get-tuple-element.44), channel_id=1, source_target_pairs={{0,2},{1,3},{2,0},{3,1},{4,6},{5,7},{6,4},{7,5},{8,10},{9,11},{10,... | collective-permute-start | bytes 196616 | tf_op jit(solution)/shard_map/ppermute | solution.py:168
  123.1 5.2 %collective-permute-start.8 = (f32[32,512]{1,0:T(8,128)S(1)}, f32[32,512]{1,0:T(8,128)S(1)}, u32[]{:S(2)}, u32[]{:S(2)}) collective-permute-start(f32[32,512]{1,0:T(8,128)S(1)} %get-tuple-element.42), channel_id=1, source_target_pairs={{0,1},{1,0},{2,3},{3,2},{4,5},{5,4},{6,7},{7,6},{8,9},{9,8},{10,11... | collective-permute-start | bytes 196616 | tf_op jit(solution)/shard_map/ppermute | solution.py:168
  128.3 7.9 %collective-permute-start.11 = (f32[32,256]{1,0:T(8,128)S(1)}, f32[32,256]{1,0:T(8,128)S(1)}, u32[]{:S(2)}, u32[]{:S(2)}) collective-permute-start(f32[32,256]{1,0:T(8,128)S(1)} %slice.133), channel_id=1, source_target_pairs={{0,4},{1,5},{2,6},{3,7},{4,0},{5,1},{6,2},{7,3},{8,12},{9,13},{10,... | collective-permute-start | bytes 98312 | tf_op jit(solution)/shard_map/ppermute | solution.py:172

commit v3 on v2

v3 whole, which is shorter than its diff:
```python
import functools

import jax
import jax.numpy as jnp
from jax import lax
from jax.experimental import pallas as pl
from jax.experimental.pallas import tpu as pltpu
from jax.sharding import Mesh, PartitionSpec as P

SUB = 64
A_SLAB = 32
N_Y, N_X, N_CORE, N_REP = 4, 4, 2, 8
N_RED = N_Y * N_X * N_CORE
RED = ("y", "x", "core")
STRIDE = {"x": N_CORE, "y": N_CORE * N_X}
ORDER = (("x", "y"), ("y", "x"))
MASKS = ((1, 3), (3, 1))
MIB = 1024 * 1024


def offset(core, half, pos):
    first, second = (STRIDE[axis] for axis in ORDER[core])
    off = (pos & 3) * second
    for k, mask in enumerate(MASKS[half]):
        if (pos >> (3 - k)) & 1:
            off ^= mask * first
    return off


def pairs(turn, mask):
    return [(i, i ^ (mask * STRIDE[ORDER[i % 2][turn]])) for i in range(N_RED)]


def where_am_i():
    return (lax.axis_index("y") * N_X + lax.axis_index("x")) * N_CORE + lax.axis_index("core")


def pack_kernel(perm_ref, amp_ref, out_ref):
    tile = out_ref.shape[2]
    for r in range(N_RED):
        cols = pl.ds(pl.multiple_of(perm_ref[0, r] * tile, tile), tile)
        out_ref[r] = amp_ref[:, cols]


def pack(amplitudes, tile_perm, tile):
    rows = amplitudes.shape[0]
    vmem = pl.BlockSpec(memory_space=pltpu.VMEM)
    return pl.pallas_call(
        pack_kernel,
        out_shape=jax.ShapeDtypeStruct((N_RED, rows, tile), amplitudes.dtype),
        in_specs=[pl.BlockSpec(memory_space=pltpu.SMEM), vmem],
        out_specs=vmem,
        compiler_params=pltpu.CompilerParams(vmem_limit_bytes=16 * MIB),
        cost_estimate=pl.CostEstimate(
            flops=0, bytes_accessed=4 * amplitudes.size, transcendentals=0
        ),
    )(tile_perm, amplitudes)


def dot_tiles(other, group, amp_ref, b_ref, lhs):
    rows = amp_ref.shape[1]
    width = b_ref.shape[1] // N_REP
    core = lax.axis_index("core") ^ other
    me = where_am_i() ^ other
    rep = lax.axis_index("rep")
    for half in range(2):
        for pos in range(16):
            block = me ^ jnp.where(core == 0, offset(0, half, pos), offset(1, half, pos))
            lhs[pos * rows : (pos + 1) * rows, :] = amp_ref[block]
        for k in range(2):
            source = (2 * group + half + 4 * k) ^ rep
            b = b_ref[:, pl.ds(pl.multiple_of(source * width, width), width)]
            cols = slice(k * width, (k + 1) * width)
            yield half, cols, jnp.dot(lhs[...], b, preferred_element_type=jnp.float32)


def away_kernel(group, amp_ref, b_ref, out_ref, lhs):
    for half, cols, out in dot_tiles(1, group, amp_ref, b_ref, lhs):
        out_ref[half, :, cols] = out


def home_kernel(group, amp_ref, b_ref, arrived_ref, far0, far1, near0, near1, lhs):
    n = far0.shape[0]
    for half, cols, out in dot_tiles(0, group, amp_ref, b_ref, lhs):
        out += arrived_ref[half, :, cols]
        (near0, near1)[half][:, cols] = out[:n]
        (far0, far1)[half][:, cols] = out[n:]


def in_vmem(kernel, shapes, *args, scratch=(), limit=24):
    vmem = pl.BlockSpec(memory_space=pltpu.VMEM)
    return pl.pallas_call(
        kernel,
        out_shape=[jax.ShapeDtypeStruct(shape, jnp.float32) for shape in shapes],
        in_specs=[vmem] * len(args),
        out_specs=[vmem] * len(shapes),
        scratch_shapes=scratch,
        compiler_params=pltpu.CompilerParams(vmem_limit_bytes=limit * MIB),
        cost_estimate=pl.CostEstimate(flops=0, bytes_accessed=0, transcendentals=0),
    )(*args)


def step_kernel(keep0, keep1, got0, got1, far0, far1, near0, near1):
    n = far0.shape[0]
    for keep, got, far, near in ((keep0, got0, far0, near0), (keep1, got1, far1, near1)):
        near[...] = keep[:n] + got[:n]
        far[...] = keep[n:] + got[n:]


def join_kernel(*refs):
    rows = refs[8].shape[0]
    quarter = refs[0].shape[1]
    for i in range(4):
        for k in range(4):
            part = slice(k * rows, (k + 1) * rows)
            refs[8 + k][:, i * quarter : (i + 1) * quarter] = refs[i][part] + refs[4 + i][part]


def spread_kernel(a, b, c, d, *outs):
    quarter = outs[0].shape[1]
    for k, out in enumerate(outs):
        cols = slice(k * quarter, (k + 1) * quarter)
        out[...] = (a[:, cols] + b[:, cols]) + (c[:, cols] + d[:, cols])


def energy_gap(
    occ_index, occ_energy, block_sizes, slab_irrep, virt_energy, red, rep, rows, columns
):
    n_occ = occ_energy.shape[0]
    matches = occ_index[:, :, :, None] == jnp.arange(n_occ, dtype=jnp.int32)[None, None, None, :]
    orbital_e = jnp.sum(jnp.where(matches, occ_energy[None, None, None, :], 0.0), axis=-1)
    pair_energy = (orbital_e[:, 0, :, None] + orbital_e[:, 1, None, :]).reshape(-1)
    row_energy = lax.dynamic_slice_in_dim(pair_energy, red * rows, rows, 0)
    irreps = jnp.arange(block_sizes.shape[0], dtype=jnp.int32)
    start = jnp.sum(jnp.where(irreps < slab_irrep[0], block_sizes, 0))
    e_a = lax.dynamic_slice(virt_energy, (start,), (A_SLAB,))
    e_b = lax.dynamic_slice(virt_energy, (start,), (SUB,))
    slab_energy = (e_a[:, None] + e_b[None, :]).reshape(-1)
    col_energy = lax.dynamic_slice_in_dim(slab_energy, rep * columns, columns, 0)
    return row_energy[:, None] - col_energy[None, :]


def body(
    amplitudes, integrals, tile_perm, occ_index, occ_energy, block_sizes, slab_irrep, virt_energy
):
    rows = amplitudes.shape[0]
    tile = integrals.shape[0]
    columns = integrals.shape[1] // N_REP
    red, rep = where_am_i(), lax.axis_index("rep")
    ordered = pack(amplitudes, tile_perm, tile)
    received = lax.all_to_all(ordered, RED, split_axis=0, concat_axis=0, tiled=True)
    m, quarter = 16 * rows, 2 * columns
    lhs = [pltpu.VMEM((m, tile), amplitudes.dtype)]
    arrived = []
    for group in range(2):
        (away,) = in_vmem(
            functools.partial(away_kernel, group),
            [(2, m, quarter)],
            received,
            integrals,
            scratch=lhs,
        )
        arrived.append(lax.ppermute(away, "core", [(0, 1), (1, 0)]))
    keeps, gots = [], []
    for group in range(2):
        far0, far1, *near = in_vmem(
            functools.partial(home_kernel, group),
            [(m // 2, quarter)] * 4,
            received,
            integrals,
            arrived[group],
            scratch=lhs,
        )
        keeps.append(near)
        gots.append([lax.ppermute(far, RED, pairs(0, MASKS[h][0])) for h, far in enumerate((far0, far1))])
    last, more = [], []
    for group in range(2):
        far0, far1, *near = in_vmem(step_kernel, [(m // 4, quarter)] * 4, *keeps[group], *gots[group])
        last += near
        more += [lax.ppermute(far, RED, pairs(0, MASKS[h][1])) for h, far in enumerate((far0, far1))]
    mine, *sends = in_vmem(join_kernel, [(rows, 4 * quarter)] * 4, *last, *more)
    gots = [lax.ppermute(send, RED, pairs(1, k + 1)) for k, send in enumerate(sends)]
    sends, occ_energy, virt_energy = lax.optimization_barrier((sends, occ_energy, virt_energy))
    denominator = energy_gap(
        occ_index, occ_energy, block_sizes, slab_irrep, virt_energy, red, rep, rows, columns
    )
    gots, denominator = lax.optimization_barrier((gots, denominator))
    mine, *sends = in_vmem(spread_kernel, [(rows, quarter)] * 4, mine, *gots)
    gots = [
        lax.ppermute(send, "rep", [(i, i ^ (k + 1)) for i in range(N_REP)])
        for k, send in enumerate(sends)
    ]
    mine = (mine + gots[0]) + (gots[1] + gots[2])
    got = lax.ppermute(mine[:, columns:], "rep", [(i, i ^ 4) for i in range(N_REP)])
    return (mine[:, :columns] + got) / denominator


def solution(mesh):
    grid = Mesh(mesh.devices.reshape(N_Y, N_X, N_CORE, N_REP), RED + ("rep",))
    placed = (P(RED, "rep"), P(RED + ("rep",), None), P("rep", None), P(), P(), P(), P(), P())
    return jax.shard_map(
        body, mesh=grid, in_specs=placed, out_specs=P(RED, "rep"), check_vma=False
    )
```

time: 138 us -> 129 us (0.935)
  starting transfers between devices: 20.9 us -> 25.9 us
  waiting for transfers between devices: 30.2 us -> 25.4 us
  other arithmetic: 5.85 us -> 1.68 us
  Pallas kernels: 14.8 us -> 10.7 us
    ppermute x11 -> x16, starting transfers between devices: 15.2 us -> 21.7 us  [the longest x4 6.24 us: body(): lax.ppermute(far, RED, pairs(0, MASKS[h][1]))]
    ppermute x11 -> x16, waiting for transfers between devices: 27.9 us -> 21.7 us  [the longest x3 7 us: body(): lax.ppermute(send, RED, pairs(1, k + 1))]
    add x6 -> x1, other arithmetic: 4.06 us -> 0.02 us  [body(): mine = mine + gots[0] + (gots[1] + gots[2])]
    pallas_call x2 -> x8, Pallas kernels: 12.4 us -> 9.91 us  [in_vmem(): pl.pallas_call(kernel, out_shape=[jax.ShapeDtypeStruct(shape, jnp.float32...]
    pallas_call x1, Pallas kernels: 2.38 us -> 0.81 us  [pack(): pl.pallas_call(pack_kernel, out_shape=jax.ShapeDtypeStruct((N_RED, rows,...]
    ppermute x1, starting transfers between devices: 5.65 us -> 4.24 us  [body(): lax.ppermute(mine[:, columns:], 'rep', [(i, i ^ 4) for i in range(N_REP)])]
    ppermute x1, waiting for transfers between devices: 2.27 us -> 3.67 us  [body(): lax.ppermute(mine[:, columns:], 'rep', [(i, i ^ 4) for i in range(N_REP)])]
  transfers between devices with their start and end apart: 12 -> 17, of which waited for: 10 -> 13; matrix products, arithmetic and copies ran while one was open for 2% -> 1% of each run, Pallas kernels for 5% -> 6%
where the time goes in v3:
time: 129 us
  blocking collectives  57.5 us (45%)
  starting transfers between devices  25.9 us (20%)
  waiting for transfers between devices  25.4 us (20%)
  Pallas kernels  10.7 us (8%)
  local copies, waits for them, and re-layouts  4.72 us (4%)
  between operations  2.69 us (2%)
  other arithmetic  1.68 us (1%)
    all_to_all x1, blocking collectives, body(): lax.all_to_all(ordered, RED, split_axis=0, concat_axis=0, tiled=True)  57.5 us
    pallas_call x8, Pallas kernels, in_vmem(): pl.pallas_call(kernel, out_shape=[jax.ShapeDtypeStruct(shape, jnp.float32...  9.91 us
    ppermute x3, waiting for transfers between devices, body(): lax.ppermute(send, RED, pairs(1, k + 1))  7 us
    ppermute x3, waiting for transfers between devices, body(): lax.ppermute(send, 'rep', [(i, i ^ k + 1) for i in range(N_REP)])  6.51 us
    ppermute x4, starting transfers between devices, body(): lax.ppermute(far, RED, pairs(0, MASKS[h][1]))  6.24 us
    ppermute x4, waiting for transfers between devices, body(): lax.ppermute(far, RED, pairs(0, MASKS[h][0]))  5.85 us
    ppermute x3, starting transfers between devices, body(): lax.ppermute(send, 'rep', [(i, i ^ k + 1) for i in range(N_REP)])  5.22 us
    ppermute x4, starting transfers between devices, body(): lax.ppermute(far, RED, pairs(0, MASKS[h][0]))  4.82 us
  transfers between devices with their start and end apart: 17, of which 13 were waited for; matrix products, arithmetic and copies ran while one was open for 1% of the time, Pallas kernels for 6%

profile of v3, /device:TPU:2, one launch (start us, length us, event | category | flops | bytes accessed | tf_op | source)
XLA Modules:
  0.0 128.6 jit_solution(10546106940529795291)
XLA Ops:
  0.0 2.2 %copy-done.1 = bf16[32,65536]{1,0:T(8,128)(2,1)S(1)} copy-done((bf16[32,65536]{1,0:T(8,128)(2,1)S(1)}, bf16[32,65536]{1,0:T(8,128)(2,1)}, u32[]{:S(2)}) %copy-start.1) | copy-done | bytes 4194328
  2.2 0.7 copy-done.2
  2.8 0.8 shard_map.82
  3.7 57.5 %all_to_all.5.amp_ref = bf16[32,32,2048]{2,1,0:T(8,128)(2,1)S(1)} all-to-all(bf16[32,32,2048]{2,1,0:T(8,128)(2,1)S(1)} %shard_map.82), channel_id=1, replica_groups=mesh['y'=4,'x'=4,'core'=2,'rep'=8] {'y','x','core'}, dimensions={0} | all-to-all | bytes 8388608 | tf_op jit(solution)/shard_map/all_to_all | solution.py:151
  61.2 2.4 %shard_map.86 = f32[2,512,512]{2,1,0:T(8,128)S(1)} custom-call(bf16[32,32,2048]{2,1,0:T(8,128)(2,1)S(1)} %all_to_all.5.amp_ref, bf16[2048,2048]{1,0:T(8,128)(2,1)S(1)} %copy-done), custom_call_target="tpu_custom_call" | custom-call | tf_op jit(solution)/shard_map/pallas_call | solution.py:92
  63.6 0.3 collective-permute-start.3
  63.8 2.4 %shard_map.83 = f32[2,512,512]{2,1,0:T(8,128)S(1)} custom-call(bf16[32,32,2048]{2,1,0:T(8,128)(2,1)S(1)} %all_to_all.5.amp_ref, bf16[2048,2048]{1,0:T(8,128)(2,1)S(1)} %copy-done), custom_call_target="tpu_custom_call" | custom-call | tf_op jit(solution)/shard_map/pallas_call | solution.py:92
  66.2 0.4 collective-permute-start
  66.6 1.2 collective-permute-done.3.arrived_ref
  67.8 2.4 %shard_map.87 = (f32[256,512]{1,0:T(8,128)S(1)}, f32[256,512]{1,0:T(8,128)S(1)}, f32[256,512]{1,0:T(8,128)S(1)}, f32[256,512]{1,0:T(8,128)S(1)}) custom-call(bf16[32,32,2048]{2,1,0:T(8,128)(2,1)S(1)} %all_to_all.5.amp_ref, bf16[2048,2048]{1,0:T(8,128)(2,1)S(1)} %copy-done, f32[2,512,512]{2,1,0:T(8,128)S(1)} %collective-permute-done.3.arrived_ref), custom_call_target="tpu_custom_call" | custom-call | tf_op jit(solution)/shard_map/pallas_call | solution.py:92
  70.2 1.5 %collective-permute-start.4 = (f32[256,512]{1,0:T(8,128)S(1)}, f32[256,512]{1,0:T(8,128)S(1)}, u32[]{:S(2)}, u32[]{:S(2)}) collective-permute-start(f32[256,512]{1,0:T(8,128)S(1)} %get-tuple-element.43), channel_id=1, source_target_pairs={{0,16},{8,72},{16,0},{24,88},{32,48},{40,104},{48,32},{56,120},{64... | collective-permute-start | bytes 1572872 | tf_op jit(solution)/shard_map/ppermute | solution.py:175
  71.8 0.7 collective-permute-start.5
  72.5 2.4 %shard_map.84 = (f32[256,512]{1,0:T(8,128)S(1)}, f32[256,512]{1,0:T(8,128)S(1)}, f32[256,512]{1,0:T(8,128)S(1)}, f32[256,512]{1,0:T(8,128)S(1)}) custom-call(bf16[32,32,2048]{2,1,0:T(8,128)(2,1)S(1)} %all_to_all.5.amp_ref, bf16[2048,2048]{1,0:T(8,128)(2,1)S(1)} %copy-done, f32[2,512,512]{2,1,0:T(8,128)S(1)} %collective-permute-done.arrived_ref), custom_call_target="tpu_custom_call" | custom-call | tf_op jit(solution)/shard_map/pallas_call | solution.py:92
  74.9 1.2 collective-permute-start.1
  76.1 1.4 %collective-permute-start.2 = (f32[256,512]{1,0:T(8,128)S(1)}, f32[256,512]{1,0:T(8,128)S(1)}, u32[]{:S(2)}, u32[]{:S(2)}) collective-permute-start(f32[256,512]{1,0:T(8,128)S(1)} %get-tuple-element.38), channel_id=1, source_target_pairs={{0,48},{8,200},{16,32},{24,216},{32,16},{40,232},{48,0},{56,248},{... | collective-permute-start | bytes 1572872 | tf_op jit(solution)/shard_map/ppermute | solution.py:175
  77.5 2.0 %collective-permute-done.4.got0 = f32[256,512]{1,0:T(8,128)S(1)} collective-permute-done((f32[256,512]{1,0:T(8,128)S(1)}, f32[256,512]{1,0:T(8,128)S(1)}, u32[]{:S(2)}, u32[]{:S(2)}) %collective-permute-start.4) | collective-permute-done | bytes 524320 | tf_op jit(solution)/shard_map/ppermute | solution.py:175
  79.5 1.5 %collective-permute-done.5.got1 = f32[256,512]{1,0:T(8,128)S(1)} collective-permute-done((f32[256,512]{1,0:T(8,128)S(1)}, f32[256,512]{1,0:T(8,128)S(1)}, u32[]{:S(2)}, u32[]{:S(2)}) %collective-permute-start.5) | collective-permute-done | bytes 524320 | tf_op jit(solution)/shard_map/ppermute | solution.py:175
  81.0 0.1 shard_map.88
  81.1 0.8 collective-permute-start.8
  81.9 2.3 %collective-permute-start.9 = (f32[128,512]{1,0:T(8,128)S(1)}, f32[128,512]{1,0:T(8,128)S(1)}, u32[]{:S(2)}, u32[]{:S(2)}) collective-permute-start(f32[128,512]{1,0:T(8,128)S(1)} %get-tuple-element.50), channel_id=1, source_target_pairs={{0,16},{8,72},{16,0},{24,88},{32,48},{40,104},{48,32},{56,120},{64... | collective-permute-start | bytes 786440 | tf_op jit(solution)/shard_map/ppermute | solution.py:180
  84.2 0.9 collective-permute-done.1.got0
  85.1 1.5 %collective-permute-done.2.got1 = f32[256,512]{1,0:T(8,128)S(1)} collective-permute-done((f32[256,512]{1,0:T(8,128)S(1)}, f32[256,512]{1,0:T(8,128)S(1)}, u32[]{:S(2)}, u32[]{:S(2)}) %collective-permute-start.2) | collective-permute-done | bytes 524320 | tf_op jit(solution)/shard_map/ppermute | solution.py:175
  86.6 0.1 shard_map.85
  86.7 0.8 collective-permute-start.6
  87.5 2.3 %collective-permute-start.7 = (f32[128,512]{1,0:T(8,128)S(1)}, f32[128,512]{1,0:T(8,128)S(1)}, u32[]{:S(2)}, u32[]{:S(2)}) collective-permute-start(f32[128,512]{1,0:T(8,128)S(1)} %get-tuple-element.48), channel_id=1, source_target_pairs={{0,16},{8,72},{16,0},{24,88},{32,48},{40,104},{48,32},{56,120},{64... | collective-permute-start | bytes 786440 | tf_op jit(solution)/shard_map/ppermute | solution.py:180
  90.5 0.6 fusion.1
  93.0 0.1 collective-permute-done.6.refs_4_
  93.1 1.0 collective-permute-done.7.refs_5_
  94.1 0.1 shard_map.89
  94.3 0.8 dynamic_slice.13
  95.0 0.8 dynamic_slice.14
  95.8 0.6 collective-permute-start.10
  96.4 1.8 %collective-permute-start.11 = (f32[32,2048]{1,0:T(8,128)S(1)}, f32[32,2048]{1,0:T(8,128)S(1)}, u32[]{:S(2)}, u32[]{:S(2)}) collective-permute-start(f32[32,2048]{1,0:T(8,128)S(1)} %get-tuple-element.53), channel_id=1, source_target_pairs={{0,128},{8,40},{16,144},{24,56},{32,160},{40,8},{48,176},{56,24},{... | collective-permute-start | bytes 786440 | tf_op jit(solution)/shard_map/ppermute | solution.py:182
  98.3 2.2 %collective-permute-start.12 = (f32[32,2048]{1,0:T(8,128)S(1)}, f32[32,2048]{1,0:T(8,128)S(1)}, u32[]{:S(2)}, u32[]{:S(2)}) collective-permute-start(f32[32,2048]{1,0:T(8,128)S(1)} %get-tuple-element.54), channel_id=1, source_target_pairs={{0,192},{8,56},{16,208},{24,40},{32,224},{40,24},{48,240},{56,8},{... | collective-permute-start | bytes 786440 | tf_op jit(solution)/shard_map/ppermute | solution.py:182
  100.5 0.2 select_reduce_fusion
  100.8 0.1 add.71
  101.1 0.1 dynamic_slice.15
  101.1 0.1 broadcast_subtract_fusion
  101.2 1.0 collective-permute-done.10.b
  102.2 3.3 %collective-permute-done.11.c = f32[32,2048]{1,0:T(8,128)S(1)} collective-permute-done((f32[32,2048]{1,0:T(8,128)S(1)}, f32[32,2048]{1,0:T(8,128)S(1)}, u32[]{:S(2)}, u32[]{:S(2)}) %collective-permute-start.11) | collective-permute-done | bytes 262176 | tf_op jit(solution)/shard_map/ppermute | solution.py:182
  105.5 2.7 %collective-permute-done.12.d = f32[32,2048]{1,0:T(8,128)S(1)} collective-permute-done((f32[32,2048]{1,0:T(8,128)S(1)}, f32[32,2048]{1,0:T(8,128)S(1)}, u32[]{:S(2)}, u32[]{:S(2)}) %collective-permute-start.12) | collective-permute-done | bytes 262176 | tf_op jit(solution)/shard_map/ppermute | solution.py:182
  108.3 2.0 %collective-permute-start.13 = (f32[32,512]{1,0:T(8,128)S(1)}, f32[32,512]{1,0:T(8,128)S(1)}, u32[]{:S(2)}, u32[]{:S(2)}) collective-permute-start(f32[32,512]{1,0:T(8,128)S(1)} %get-tuple-element.61), channel_id=1, source_target_pairs={{0,1},{1,0},{2,3},{3,2},{4,5},{5,4},{6,7},{7,6},{8,9},{9,8},{10,11... | collective-permute-start | bytes 196616 | tf_op jit(solution)/shard_map/ppermute | solution.py:190
  110.3 3.2 %collective-permute-start.14 = (f32[32,512]{1,0:T(8,128)S(1)}, f32[32,512]{1,0:T(8,128)S(1)}, u32[]{:S(2)}, u32[]{:S(2)}) collective-permute-start(f32[32,512]{1,0:T(8,128)S(1)} %get-tuple-element.62), channel_id=1, source_target_pairs={{0,2},{1,3},{2,0},{3,1},{4,6},{5,7},{6,4},{7,5},{8,10},{9,11},{10,... | collective-permute-start | bytes 196616 | tf_op jit(solution)/shard_map/ppermute | solution.py:190
  113.5 2.9 %collective-permute-done.14 = f32[32,512]{1,0:T(8,128)S(1)} collective-permute-done((f32[32,512]{1,0:T(8,128)S(1)}, f32[32,512]{1,0:T(8,128)S(1)}, u32[]{:S(2)}, u32[]{:S(2)}) %collective-permute-start.14) | collective-permute-done | bytes 65568 | tf_op jit(solution)/shard_map/ppermute | solution.py:190
  116.4 3.6 %collective-permute-done.15 = f32[32,512]{1,0:T(8,128)S(1)} collective-permute-done((f32[32,512]{1,0:T(8,128)S(1)}, f32[32,512]{1,0:T(8,128)S(1)}, u32[]{:S(2)}, u32[]{:S(2)}) %collective-permute-start.15) | collective-permute-done | bytes 65568 | tf_op jit(solution)/shard_map/ppermute | solution.py:190
  120.0 4.2 %collective-permute-start.16 = (f32[32,256]{1,0:T(8,128)S(1)}, f32[32,256]{1,0:T(8,128)S(1)}, u32[]{:S(2)}, u32[]{:S(2)}) collective-permute-start(f32[32,256]{1,0:T(8,128)S(1)} %slice.19), channel_id=1, source_target_pairs={{0,4},{1,5},{2,6},{3,7},{4,0},{5,1},{6,2},{7,3},{8,12},{9,13},{10,... | collective-permute-start | bytes 98312 | tf_op jit(solution)/shard_map/ppermute | solution.py:194
  124.3 3.7 %collective-permute-done.16 = f32[32,256]{1,0:T(8,128)S(1)} collective-permute-done((f32[32,256]{1,0:T(8,128)S(1)}, f32[32,256]{1,0:T(8,128)S(1)}, u32[]{:S(2)}, u32[]{:S(2)}) %collective-permute-start.16) | collective-permute-done | bytes 32800 | tf_op jit(solution)/shard_map/ppermute | solution.py:194
  128.0 0.6 fusion
  (23 shorter events, 0.4 us)
Async XLA Ops:
  0.0 2.2 %copy-start.1 = (bf16[32,65536]{1,0:T(8,128)(2,1)S(1)}, bf16[32,65536]{1,0:T(8,128)(2,1)}, u32[]{:S(2)}) copy-start(bf16[32,65536]{1,0:T(8,128)(2,1)} %amp_ref.1) | copy-start | bytes 12582916
  2.2 0.7 copy-start.2
  3.7 57.5 %copy-start = (bf16[2048,2048]{1,0:T(8,128)(2,1)S(1)}, bf16[2048,2048]{1,0:T(8,128)(2,1)}, u32[]{:S(2)}) copy-start(bf16[2048,2048]{1,0:T(8,128)(2,1)} %b_ref.7) | copy-start | bytes 25165828
  63.6 4.2 %collective-permute-start.3 = (f32[2,512,512]{2,1,0:T(8,128)S(1)}, f32[2,512,512]{2,1,0:T(8,128)S(1)}, u32[]{:S(2)}, u32[]{:S(2)}) collective-permute-start(f32[2,512,512]{2,1,0:T(8,128)S(1)} %shard_map.86), channel_id=1, source_target_pairs={{0,8},{8,0},{1,9},{9,1},{2,10},{10,2},{3,11},{11,3},{4,12},{12,4},... | collective-permute-start | bytes 6291464 | tf_op jit(solution)/shard_map/ppermute | solution.py:163
  66.2 6.3 %collective-permute-start = (f32[2,512,512]{2,1,0:T(8,128)S(1)}, f32[2,512,512]{2,1,0:T(8,128)S(1)}, u32[]{:S(2)}, u32[]{:S(2)}) collective-permute-start(f32[2,512,512]{2,1,0:T(8,128)S(1)} %shard_map.83), channel_id=1, source_target_pairs={{0,8},{8,0},{1,9},{9,1},{2,10},{10,2},{3,11},{11,3},{4,12},{12,4},... | collective-permute-start | bytes 6291464 | tf_op jit(solution)/shard_map/ppermute | solution.py:163
  70.2 9.3 %collective-permute-start.4 = (f32[256,512]{1,0:T(8,128)S(1)}, f32[256,512]{1,0:T(8,128)S(1)}, u32[]{:S(2)}, u32[]{:S(2)}) collective-permute-start(f32[256,512]{1,0:T(8,128)S(1)} %get-tuple-element.43), channel_id=1, source_target_pairs={{0,16},{8,72},{16,0},{24,88},{32,48},{40,104},{48,32},{56,120},{64... | collective-permute-start | bytes 1572872 | tf_op jit(solution)/shard_map/ppermute | solution.py:175
  71.8 9.2 %collective-permute-start.5 = (f32[256,512]{1,0:T(8,128)S(1)}, f32[256,512]{1,0:T(8,128)S(1)}, u32[]{:S(2)}, u32[]{:S(2)}) collective-permute-start(f32[256,512]{1,0:T(8,128)S(1)} %get-tuple-element.44), channel_id=1, source_target_pairs={{0,48},{8,200},{16,32},{24,216},{32,16},{40,232},{48,0},{56,248},{... | collective-permute-start | bytes 1572872 | tf_op jit(solution)/shard_map/ppermute | solution.py:175
  74.9 15.6 %copy-start.5 = (s32[8]{0:T(128)S(1)}, s32[8]{0:T(128)}, u32[]{:S(2)}) copy-start(s32[8]{0:T(128)} %param.13) | copy-start | bytes 100
  74.9 25.6 %copy-start.3 = (s32[4,2,16]{2,1,0:T(2,128)S(1)}, s32[4,2,16]{2,1,0:T(2,128)}, u32[]{:S(2)}) copy-start(s32[4,2,16]{2,1,0:T(2,128)} %param.11) | copy-start | bytes 1540
  74.9 25.6 %copy-start.4 = (f32[125]{0:T(128)S(1)}, f32[125]{0:T(128)}, u32[]{:S(2)}) copy-start(f32[125]{0:T(128)} %param.12) | copy-start | bytes 1504
  74.9 10.2 %collective-permute-start.1 = (f32[256,512]{1,0:T(8,128)S(1)}, f32[256,512]{1,0:T(8,128)S(1)}, u32[]{:S(2)}, u32[]{:S(2)}) collective-permute-start(f32[256,512]{1,0:T(8,128)S(1)} %get-tuple-element.37), channel_id=1, source_target_pairs={{0,16},{8,72},{16,0},{24,88},{32,48},{40,104},{48,32},{56,120},{64... | collective-permute-start | bytes 1572872 | tf_op jit(solution)/shard_map/ppermute | solution.py:175
  76.1 10.5 %collective-permute-start.2 = (f32[256,512]{1,0:T(8,128)S(1)}, f32[256,512]{1,0:T(8,128)S(1)}, u32[]{:S(2)}, u32[]{:S(2)}) collective-permute-start(f32[256,512]{1,0:T(8,128)S(1)} %get-tuple-element.38), channel_id=1, source_target_pairs={{0,48},{8,200},{16,32},{24,216},{32,16},{40,232},{48,0},{56,248},{... | collective-permute-start | bytes 1572872 | tf_op jit(solution)/shard_map/ppermute | solution.py:175
  81.1 11.9 %collective-permute-start.8 = (f32[128,512]{1,0:T(8,128)S(1)}, f32[128,512]{1,0:T(8,128)S(1)}, u32[]{:S(2)}, u32[]{:S(2)}) collective-permute-start(f32[128,512]{1,0:T(8,128)S(1)} %get-tuple-element.49), channel_id=1, source_target_pairs={{0,48},{8,200},{16,32},{24,216},{32,16},{40,232},{48,0},{56,248},{... | collective-permute-start | bytes 786440 | tf_op jit(solution)/shard_map/ppermute | solution.py:180
  81.9 11.2 %collective-permute-start.9 = (f32[128,512]{1,0:T(8,128)S(1)}, f32[128,512]{1,0:T(8,128)S(1)}, u32[]{:S(2)}, u32[]{:S(2)}) collective-permute-start(f32[128,512]{1,0:T(8,128)S(1)} %get-tuple-element.50), channel_id=1, source_target_pairs={{0,16},{8,72},{16,0},{24,88},{32,48},{40,104},{48,32},{56,120},{64... | collective-permute-start | bytes 786440 | tf_op jit(solution)/shard_map/ppermute | solution.py:180
  86.7 6.5 %collective-permute-start.6 = (f32[128,512]{1,0:T(8,128)S(1)}, f32[128,512]{1,0:T(8,128)S(1)}, u32[]{:S(2)}, u32[]{:S(2)}) collective-permute-start(f32[128,512]{1,0:T(8,128)S(1)} %get-tuple-element.47), channel_id=1, source_target_pairs={{0,48},{8,200},{16,32},{24,216},{32,16},{40,232},{48,0},{56,248},{... | collective-permute-start | bytes 786440 | tf_op jit(solution)/shard_map/ppermute | solution.py:180
  87.5 6.7 %collective-permute-start.7 = (f32[128,512]{1,0:T(8,128)S(1)}, f32[128,512]{1,0:T(8,128)S(1)}, u32[]{:S(2)}, u32[]{:S(2)}) collective-permute-start(f32[128,512]{1,0:T(8,128)S(1)} %get-tuple-element.48), channel_id=1, source_target_pairs={{0,16},{8,72},{16,0},{24,88},{32,48},{40,104},{48,32},{56,120},{64... | collective-permute-start | bytes 786440 | tf_op jit(solution)/shard_map/ppermute | solution.py:180
  95.8 6.4 %collective-permute-start.10 = (f32[32,2048]{1,0:T(8,128)S(1)}, f32[32,2048]{1,0:T(8,128)S(1)}, u32[]{:S(2)}, u32[]{:S(2)}) collective-permute-start(f32[32,2048]{1,0:T(8,128)S(1)} %get-tuple-element.52), channel_id=1, source_target_pairs={{0,64},{8,24},{16,80},{24,8},{32,96},{40,56},{48,112},{56,40},{64,... | collective-permute-start | bytes 786440 | tf_op jit(solution)/shard_map/ppermute | solution.py:182
  96.4 9.1 %collective-permute-start.11 = (f32[32,2048]{1,0:T(8,128)S(1)}, f32[32,2048]{1,0:T(8,128)S(1)}, u32[]{:S(2)}, u32[]{:S(2)}) collective-permute-start(f32[32,2048]{1,0:T(8,128)S(1)} %get-tuple-element.53), channel_id=1, source_target_pairs={{0,128},{8,40},{16,144},{24,56},{32,160},{40,8},{48,176},{56,24},{... | collective-permute-start | bytes 786440 | tf_op jit(solution)/shard_map/ppermute | solution.py:182
  98.3 10.0 %collective-permute-start.12 = (f32[32,2048]{1,0:T(8,128)S(1)}, f32[32,2048]{1,0:T(8,128)S(1)}, u32[]{:S(2)}, u32[]{:S(2)}) collective-permute-start(f32[32,2048]{1,0:T(8,128)S(1)} %get-tuple-element.54), channel_id=1, source_target_pairs={{0,192},{8,56},{16,208},{24,40},{32,224},{40,24},{48,240},{56,8},{... | collective-permute-start | bytes 786440 | tf_op jit(solution)/shard_map/ppermute | solution.py:182
  108.3 5.2 %collective-permute-start.13 = (f32[32,512]{1,0:T(8,128)S(1)}, f32[32,512]{1,0:T(8,128)S(1)}, u32[]{:S(2)}, u32[]{:S(2)}) collective-permute-start(f32[32,512]{1,0:T(8,128)S(1)} %get-tuple-element.61), channel_id=1, source_target_pairs={{0,1},{1,0},{2,3},{3,2},{4,5},{5,4},{6,7},{7,6},{8,9},{9,8},{10,11... | collective-permute-start | bytes 196616 | tf_op jit(solution)/shard_map/ppermute | solution.py:190
  110.3 6.2 %collective-permute-start.14 = (f32[32,512]{1,0:T(8,128)S(1)}, f32[32,512]{1,0:T(8,128)S(1)}, u32[]{:S(2)}, u32[]{:S(2)}) collective-permute-start(f32[32,512]{1,0:T(8,128)S(1)} %get-tuple-element.62), channel_id=1, source_target_pairs={{0,2},{1,3},{2,0},{3,1},{4,6},{5,7},{6,4},{7,5},{8,10},{9,11},{10,... | collective-permute-start | bytes 196616 | tf_op jit(solution)/shard_map/ppermute | solution.py:190
  113.5 6.5 %collective-permute-start.15 = (f32[32,512]{1,0:T(8,128)S(1)}, f32[32,512]{1,0:T(8,128)S(1)}, u32[]{:S(2)}, u32[]{:S(2)}) collective-permute-start(f32[32,512]{1,0:T(8,128)S(1)} %get-tuple-element.63), channel_id=1, source_target_pairs={{0,3},{1,2},{2,1},{3,0},{4,7},{5,6},{6,5},{7,4},{8,11},{9,10},{10,... | collective-permute-start | bytes 196616 | tf_op jit(solution)/shard_map/ppermute | solution.py:190
  120.0 7.9 %collective-permute-start.16 = (f32[32,256]{1,0:T(8,128)S(1)}, f32[32,256]{1,0:T(8,128)S(1)}, u32[]{:S(2)}, u32[]{:S(2)}) collective-permute-start(f32[32,256]{1,0:T(8,128)S(1)} %slice.19), channel_id=1, source_target_pairs={{0,4},{1,5},{2,6},{3,7},{4,0},{5,1},{6,2},{7,3},{8,12},{9,13},{10,... | collective-permute-start | bytes 98312 | tf_op jit(solution)/shard_map/ppermute | solution.py:194

commit v4 on v3

--- a/solution.py
+++ b/solution.py
@@ -8,7 +8,6 @@
 from jax.sharding import Mesh, PartitionSpec as P
 
 SUB = 64
-A_SLAB = 32
 N_Y, N_X, N_CORE, N_REP = 4, 4, 2, 8
 N_RED = N_Y * N_X * N_CORE
 RED = ("y", "x", "core")
@@ -35,10 +34,10 @@
     return (lax.axis_index("y") * N_X + lax.axis_index("x")) * N_CORE + lax.axis_index("core")
 
 
-def pack_kernel(perm_ref, amp_ref, out_ref):
+def pack_kernel(first_ref, amp_ref, out_ref):
     tile = out_ref.shape[2]
     for r in range(N_RED):
-        cols = pl.ds(pl.multiple_of(perm_ref[0, r] * tile, tile), tile)
+        cols = pl.ds(pl.multiple_of(first_ref[0, r], tile), tile)
         out_ref[r] = amp_ref[:, cols]
 
 
@@ -54,7 +53,7 @@
         cost_estimate=pl.CostEstimate(
             flops=0, bytes_accessed=4 * amplitudes.size, transcendentals=0
         ),
-    )(tile_perm, amplitudes)
+    )(tile_perm * tile, amplitudes)
 
 
 def dot_tiles(other, group, amp_ref, b_ref, lhs):
@@ -107,37 +106,53 @@
         far[...] = keep[n:] + got[n:]
 
 
-def join_kernel(*refs):
-    rows = refs[8].shape[0]
-    quarter = refs[0].shape[1]
-    for i in range(4):
-        for k in range(4):
-            part = slice(k * rows, (k + 1) * rows)
-            refs[8 + k][:, i * quarter : (i + 1) * quarter] = refs[i][part] + refs[4 + i][part]
-
-
-def spread_kernel(a, b, c, d, *outs):
-    quarter = outs[0].shape[1]
+def join_kernel(keep0, keep1, got0, got1, *outs):
+    rows = outs[0].shape[0]
+    quarter = keep0.shape[1]
     for k, out in enumerate(outs):
-        cols = slice(k * quarter, (k + 1) * quarter)
-        out[...] = (a[:, cols] + b[:, cols]) + (c[:, cols] + d[:, cols])
-
-
-def energy_gap(
-    occ_index, occ_energy, block_sizes, slab_irrep, virt_energy, red, rep, rows, columns
-):
-    n_occ = occ_energy.shape[0]
-    matches = occ_index[:, :, :, None] == jnp.arange(n_occ, dtype=jnp.int32)[None, None, None, :]
-    orbital_e = jnp.sum(jnp.where(matches, occ_energy[None, None, None, :], 0.0), axis=-1)
-    pair_energy = (orbital_e[:, 0, :, None] + orbital_e[:, 1, None, :]).reshape(-1)
-    row_energy = lax.dynamic_slice_in_dim(pair_energy, red * rows, rows, 0)
-    irreps = jnp.arange(block_sizes.shape[0], dtype=jnp.int32)
-    start = jnp.sum(jnp.where(irreps < slab_irrep[0], block_sizes, 0))
-    e_a = lax.dynamic_slice(virt_energy, (start,), (A_SLAB,))
-    e_b = lax.dynamic_slice(virt_energy, (start,), (SUB,))
-    slab_energy = (e_a[:, None] + e_b[None, :]).reshape(-1)
-    col_energy = lax.dynamic_slice_in_dim(slab_energy, rep * columns, columns, 0)
-    return row_energy[:, None] - col_energy[None, :]
+        part = slice(k * rows, (k + 1) * rows)
+        out[:, :quarter] = keep0[part] + got0[part]
+        out[:, quarter:] = keep1[part] + got1[part]
+
+
+def sum_kernel(a, b, c, d, left, right):
+    n = left.shape[1]
+    left[...] = (a[:, :n] + b[:, :n]) + (c[:, :n] + d[:, :n])
+    right[...] = (a[:, n:] + b[:, n:]) + (c[:, n:] + d[:, n:])
+
+
+def energy_kernel(occ_index, occ_energy, block_sizes, slab_irrep, virt_energy, out_ref):
+    rows, columns = out_ref.shape
+    tile = occ_index.shape[2]
+    red, rep = where_am_i(), lax.axis_index("rep")
+    row = lax.broadcasted_iota(jnp.int32, (rows, columns), 0)
+    column = lax.broadcasted_iota(jnp.int32, (1, columns), 1)
+    pair, first = red * rows // (tile * tile), red * rows % (tile * tile) // tile
+    left = jnp.zeros((rows, columns), jnp.float32)
+    for i in range(rows // tile):
+        left = jnp.where(row // tile == i, occ_energy[occ_index[pair, 0, first + i]], left)
+    right = jnp.zeros((rows, columns), jnp.float32)
+    for j in range(tile):
+        right = jnp.where(row % tile == j, occ_energy[occ_index[pair, 1, j]], right)
+    start = 0
+    for h in range(block_sizes.shape[0]):
+        start += jnp.where(h < slab_irrep[0], block_sizes[h], 0)
+    e_a = jnp.zeros((1, columns), jnp.float32)
+    for a in range(columns // SUB):
+        e_a = jnp.where(column // SUB == a, virt_energy[start + rep * (columns // SUB) + a], e_a)
+    e_b = jnp.zeros((1, columns), jnp.float32)
+    for b in range(SUB):
+        e_b = jnp.where(column % SUB == b, virt_energy[start + b], e_b)
+    out_ref[...] = (left + right) - (e_a + e_b)
+
+
+def energy_gap(rows, columns, *args):
+    return pl.pallas_call(
+        energy_kernel,
+        out_shape=jax.ShapeDtypeStruct((rows, columns), jnp.float32),
+        in_specs=[pl.BlockSpec(memory_space=pltpu.SMEM)] * len(args),
+        out_specs=pl.BlockSpec(memory_space=pltpu.VMEM),
+    )(*args)
 
 
 def body(
@@ -146,7 +161,6 @@
     rows = amplitudes.shape[0]
     tile = integrals.shape[0]
     columns = integrals.shape[1] // N_REP
-    red, rep = where_am_i(), lax.axis_index("rep")
     ordered = pack(amplitudes, tile_perm, tile)
     received = lax.all_to_all(ordered, RED, split_axis=0, concat_axis=0, tiled=True)
     m, quarter = 16 * rows, 2 * columns
@@ -176,23 +190,24 @@
     last, more = [], []
     for group in range(2):
         far0, far1, *near = in_vmem(step_kernel, [(m // 4, quarter)] * 4, *keeps[group], *gots[group])
-        last += near
-        more += [lax.ppermute(far, RED, pairs(0, MASKS[h][1])) for h, far in enumerate((far0, far1))]
-    mine, *sends = in_vmem(join_kernel, [(rows, 4 * quarter)] * 4, *last, *more)
-    gots = [lax.ppermute(send, RED, pairs(1, k + 1)) for k, send in enumerate(sends)]
-    sends, occ_energy, virt_energy = lax.optimization_barrier((sends, occ_energy, virt_energy))
-    denominator = energy_gap(
-        occ_index, occ_energy, block_sizes, slab_irrep, virt_energy, red, rep, rows, columns
+        last.append(near)
+        more.append([lax.ppermute(far, RED, pairs(0, MASKS[h][1])) for h, far in enumerate((far0, far1))])
+    blocks = []
+    for group in range(2):
+        mine, *sends = in_vmem(join_kernel, [(rows, 2 * quarter)] * 4, *last[group], *more[group])
+        gots = [lax.ppermute(send, RED, pairs(1, k + 1)) for k, send in enumerate(sends)]
+        blocks += in_vmem(sum_kernel, [(rows, quarter)] * 2, mine, *gots)
+    gots = [
+        lax.ppermute(blocks[k], "rep", [(i, i ^ k) for i in range(N_REP)]) for k in range(1, 4)
+    ]
+    mine, send = in_vmem(sum_kernel, [(rows, columns)] * 2, blocks[0], *gots)
+    send, occ_energy = lax.optimization_barrier((send, occ_energy))
+    got = lax.ppermute(send, "rep", [(i, i ^ 4) for i in range(N_REP)])
+    gap = energy_gap(
+        rows, columns, occ_index, occ_energy, block_sizes, slab_irrep, virt_energy
     )
-    gots, denominator = lax.optimization_barrier((gots, denominator))
-    mine, *sends = in_vmem(spread_kernel, [(rows, quarter)] * 4, mine, *gots)
-    gots = [
-        lax.ppermute(send, "rep", [(i, i ^ (k + 1)) for i in range(N_REP)])
-        for k, send in enumerate(sends)
-    ]
-    mine = (mine + gots[0]) + (gots[1] + gots[2])
-    got = lax.ppermute(mine[:, columns:], "rep", [(i, i ^ 4) for i in range(N_REP)])
-    return (mine[:, :columns] + got) / denominator
+    got, gap = lax.optimization_barrier((got, gap))
+    return (mine + got) / gap
 
 
 def solution(mesh):

time: 129 us -> 122 us (0.946)
  waiting for transfers between devices: 25.4 us -> 13.5 us
  starting transfers between devices: 25.9 us -> 32.9 us
  local copies, waits for them, and re-layouts: 4.72 us -> 2.19 us
  between operations: 2.69 us -> 0.75 us
  Pallas kernels: 10.7 us -> 12.3 us
    ppermute x3 -> x6, waiting for transfers between devices: 7 us -> 0.02 us  [body(): lax.ppermute(send, RED, pairs(1, k + 1))]
    ppermute x4, waiting for transfers between devices: 10.2 us -> 4.07 us  [the longest x3 4.07 us: body(): lax.ppermute(blocks[k], 'rep', [(i, i ^ k) for i in range(N_REP)])]
    ppermute x3 -> x6, starting transfers between devices: 4.7 us -> 9.57 us  [body(): lax.ppermute(send, RED, pairs(1, k + 1))]
    ppermute x4, starting transfers between devices: 9.46 us -> 11.6 us  [the longest x1 5.81 us: body(): got = lax.ppermute(send, 'rep', [(i, i ^ 4) for i in range(N_REP)])]
    dynamic_slice x4 -> x0, local copies, waits for them, and re-layouts: 1.7 us -> none  [the longest x1 0.78 us: energy_gap(): e_a = lax.dynamic_slice(virt_energy, (start,), (A_SLAB,))]
    pallas_call x0 -> x1, Pallas kernels: none -> 1.6 us  [energy_gap(): pl.pallas_call(energy_kernel, out_shape=jax.ShapeDtypeStruct((rows, colum...]
    unnamed x12 -> x4, local copies, waits for them, and re-layouts: 2.87 us -> 2.19 us
    pallas_call x8 -> x11, Pallas kernels: 9.91 us -> 9.93 us  [in_vmem(): pl.pallas_call(kernel, out_shape=[jax.ShapeDtypeStruct(shape, jnp.float32...]
  transfers between devices with their start and end apart: 17 -> 20, of which waited for: 13 -> 8; matrix products, arithmetic and copies ran while one was open for 1% -> 0% of each run, Pallas kernels for 6% -> 8%
where the time goes in v4:
time: 122 us; the launch traced here: 121 us
  blocking collectives  57.5 us (47%)
  starting transfers between devices  32.9 us (27%)
  waiting for transfers between devices  13.5 us (11%)
  Pallas kernels  12.3 us (10%)
  local copies, waits for them, and re-layouts  2.19 us (2%)
  other arithmetic  2.04 us (2%)
    all_to_all x1, blocking collectives, body(): lax.all_to_all(ordered, RED, split_axis=0, concat_axis=0, tiled=True)  57.5 us
    pallas_call x11, Pallas kernels, in_vmem(): pl.pallas_call(kernel, out_shape=[jax.ShapeDtypeStruct(shape, jnp.float32...  9.93 us
    ppermute x6, starting transfers between devices, body(): lax.ppermute(send, RED, pairs(1, k + 1))  9.57 us
    ppermute x4, starting transfers between devices, body(): lax.ppermute(far, RED, pairs(0, MASKS[h][1]))  6.24 us
    ppermute x4, waiting for transfers between devices, body(): lax.ppermute(far, RED, pairs(0, MASKS[h][0]))  5.87 us
    ppermute x1, starting transfers between devices, body(): got = lax.ppermute(send, 'rep', [(i, i ^ 4) for i in range(N_REP)])  5.81 us
    ppermute x3, starting transfers between devices, body(): lax.ppermute(blocks[k], 'rep', [(i, i ^ k) for i in range(N_REP)])  5.74 us
    ppermute x4, starting transfers between devices, body(): lax.ppermute(far, RED, pairs(0, MASKS[h][0]))  4.83 us
  transfers between devices with their start and end apart: 20, of which 8 were waited for; matrix products, arithmetic and copies ran while one was open for 0% of the time, Pallas kernels for 8%

profile of v4, /device:TPU:2, one launch (start us, length us, event | category | flops | bytes accessed | tf_op | source)
XLA Modules:
  0.0 121.2 jit_solution(6125848398069857808)
XLA Ops:
  0.0 0.7 broadcast_multiply_fusion.first_ref
  0.7 2.2 %copy-done.1 = bf16[32,65536]{1,0:T(8,128)(2,1)S(1)} copy-done((bf16[32,65536]{1,0:T(8,128)(2,1)S(1)}, bf16[32,65536]{1,0:T(8,128)(2,1)}, u32[]{:S(2)}) %copy-start.1) | copy-done | bytes 4194328
  2.8 0.8 shard_map.82
  3.7 0.0 copy-start
  3.7 57.5 %all_to_all.5.amp_ref = bf16[32,32,2048]{2,1,0:T(8,128)(2,1)S(1)} all-to-all(bf16[32,32,2048]{2,1,0:T(8,128)(2,1)S(1)} %shard_map.82), channel_id=1, replica_groups=mesh['y'=4,'x'=4,'core'=2,'rep'=8] {'y','x','core'}, dimensions={0} | all-to-all | bytes 8388608 | tf_op jit(solution)/shard_map/all_to_all | solution.py:165
  61.2 2.4 %shard_map.88 = f32[2,512,512]{2,1,0:T(8,128)S(1)} custom-call(bf16[32,32,2048]{2,1,0:T(8,128)(2,1)S(1)} %all_to_all.5.amp_ref, bf16[2048,2048]{1,0:T(8,128)(2,1)S(1)} %copy-done), custom_call_target="tpu_custom_call" | custom-call | tf_op jit(solution)/shard_map/pallas_call | solution.py:91
  63.6 0.3 collective-permute-start.9
  63.8 2.4 %shard_map.83 = f32[2,512,512]{2,1,0:T(8,128)S(1)} custom-call(bf16[32,32,2048]{2,1,0:T(8,128)(2,1)S(1)} %all_to_all.5.amp_ref, bf16[2048,2048]{1,0:T(8,128)(2,1)S(1)} %copy-done), custom_call_target="tpu_custom_call" | custom-call | tf_op jit(solution)/shard_map/pallas_call | solution.py:91
  66.2 0.4 collective-permute-start
  66.6 1.2 collective-permute-done.9.arrived_ref
  67.8 2.4 %shard_map.89 = (f32[256,512]{1,0:T(8,128)S(1)}, f32[256,512]{1,0:T(8,128)S(1)}, f32[256,512]{1,0:T(8,128)S(1)}, f32[256,512]{1,0:T(8,128)S(1)}) custom-call(bf16[32,32,2048]{2,1,0:T(8,128)(2,1)S(1)} %all_to_all.5.amp_ref, bf16[2048,2048]{1,0:T(8,128)(2,1)S(1)} %copy-done, f32[2,512,512]{2,1,0:T(8,128)S(1)} %collective-permute-done.9.arrived_ref), custom_call_target="tpu_custom_call" | custom-call | tf_op jit(solution)/shard_map/pallas_call | solution.py:91
  70.2 1.5 %collective-permute-start.10 = (f32[256,512]{1,0:T(8,128)S(1)}, f32[256,512]{1,0:T(8,128)S(1)}, u32[]{:S(2)}, u32[]{:S(2)}) collective-permute-start(f32[256,512]{1,0:T(8,128)S(1)} %get-tuple-element.55), channel_id=1, source_target_pairs={{0,16},{8,72},{16,0},{24,88},{32,48},{40,104},{48,32},{56,120},{64... | collective-permute-start | bytes 1572872 | tf_op jit(solution)/shard_map/ppermute | solution.py:189
  71.8 0.7 collective-permute-start.11
  72.5 0.0 collective-permute-done.arrived_ref
  72.5 2.4 %shard_map.84 = (f32[256,512]{1,0:T(8,128)S(1)}, f32[256,512]{1,0:T(8,128)S(1)}, f32[256,512]{1,0:T(8,128)S(1)}, f32[256,512]{1,0:T(8,128)S(1)}) custom-call(bf16[32,32,2048]{2,1,0:T(8,128)(2,1)S(1)} %all_to_all.5.amp_ref, bf16[2048,2048]{1,0:T(8,128)(2,1)S(1)} %copy-done, f32[2,512,512]{2,1,0:T(8,128)S(1)} %collective-permute-done.arrived_ref), custom_call_target="tpu_custom_call" | custom-call | tf_op jit(solution)/shard_map/pallas_call | solution.py:91
  74.9 1.2 collective-permute-start.1
  76.1 1.4 %collective-permute-start.2 = (f32[256,512]{1,0:T(8,128)S(1)}, f32[256,512]{1,0:T(8,128)S(1)}, u32[]{:S(2)}, u32[]{:S(2)}) collective-permute-start(f32[256,512]{1,0:T(8,128)S(1)} %get-tuple-element.42), channel_id=1, source_target_pairs={{0,48},{8,200},{16,32},{24,216},{32,16},{40,232},{48,0},{56,248},{... | collective-permute-start | bytes 1572872 | tf_op jit(solution)/shard_map/ppermute | solution.py:189
  77.5 2.0 %collective-permute-done.10.got0 = f32[256,512]{1,0:T(8,128)S(1)} collective-permute-done((f32[256,512]{1,0:T(8,128)S(1)}, f32[256,512]{1,0:T(8,128)S(1)}, u32[]{:S(2)}, u32[]{:S(2)}) %collective-permute-start.10) | collective-permute-done | bytes 524320 | tf_op jit(solution)/shard_map/ppermute | solution.py:189
  79.5 1.5 %collective-permute-done.11.got1 = f32[256,512]{1,0:T(8,128)S(1)} collective-permute-done((f32[256,512]{1,0:T(8,128)S(1)}, f32[256,512]{1,0:T(8,128)S(1)}, u32[]{:S(2)}, u32[]{:S(2)}) %collective-permute-start.11) | collective-permute-done | bytes 524320 | tf_op jit(solution)/shard_map/ppermute | solution.py:189
  81.0 0.1 shard_map.90
  81.1 0.8 collective-permute-start.12
  81.9 2.3 %collective-permute-start.13 = (f32[128,512]{1,0:T(8,128)S(1)}, f32[128,512]{1,0:T(8,128)S(1)}, u32[]{:S(2)}, u32[]{:S(2)}) collective-permute-start(f32[128,512]{1,0:T(8,128)S(1)} %get-tuple-element.60), channel_id=1, source_target_pairs={{0,16},{8,72},{16,0},{24,88},{32,48},{40,104},{48,32},{56,120},{64... | collective-permute-start | bytes 786440 | tf_op jit(solution)/shard_map/ppermute | solution.py:194
  84.2 0.9 collective-permute-done.1.got0
  85.1 1.5 %collective-permute-done.2.got1 = f32[256,512]{1,0:T(8,128)S(1)} collective-permute-done((f32[256,512]{1,0:T(8,128)S(1)}, f32[256,512]{1,0:T(8,128)S(1)}, u32[]{:S(2)}, u32[]{:S(2)}) %collective-permute-start.2) | collective-permute-done | bytes 524320 | tf_op jit(solution)/shard_map/ppermute | solution.py:189
  86.6 0.1 shard_map.85
  86.7 0.8 collective-permute-start.3
  87.5 2.3 %collective-permute-start.4 = (f32[128,512]{1,0:T(8,128)S(1)}, f32[128,512]{1,0:T(8,128)S(1)}, u32[]{:S(2)}, u32[]{:S(2)}) collective-permute-start(f32[128,512]{1,0:T(8,128)S(1)} %get-tuple-element.46), channel_id=1, source_target_pairs={{0,16},{8,72},{16,0},{24,88},{32,48},{40,104},{48,32},{56,120},{64... | collective-permute-start | bytes 786440 | tf_op jit(solution)/shard_map/ppermute | solution.py:194
  89.8 0.0 collective-permute-done.12.got0
  89.8 0.1 shard_map.91
  89.9 0.7 collective-permute-start.14
  90.6 1.7 %collective-permute-start.15 = (f32[32,1024]{1,0:T(8,128)S(1)}, f32[32,1024]{1,0:T(8,128)S(1)}, u32[]{:S(2)}, u32[]{:S(2)}) collective-permute-start(f32[32,1024]{1,0:T(8,128)S(1)} %get-tuple-element.63), channel_id=1, source_target_pairs={{0,128},{8,40},{16,144},{24,56},{32,160},{40,8},{48,176},{56,24},{... | collective-permute-start | bytes 393224 | tf_op jit(solution)/shard_map/ppermute | solution.py:198
  92.3 2.4 %collective-permute-start.16 = (f32[32,1024]{1,0:T(8,128)S(1)}, f32[32,1024]{1,0:T(8,128)S(1)}, u32[]{:S(2)}, u32[]{:S(2)}) collective-permute-start(f32[32,1024]{1,0:T(8,128)S(1)} %get-tuple-element.64), channel_id=1, source_target_pairs={{0,192},{8,56},{16,208},{24,40},{32,224},{40,24},{48,240},{56,8},{... | collective-permute-start | bytes 393224 | tf_op jit(solution)/shard_map/ppermute | solution.py:198
  94.7 2.3 %collective-permute-done.4.got1 = f32[128,512]{1,0:T(8,128)S(1)} collective-permute-done((f32[128,512]{1,0:T(8,128)S(1)}, f32[128,512]{1,0:T(8,128)S(1)}, u32[]{:S(2)}, u32[]{:S(2)}) %collective-permute-start.4) | collective-permute-done | bytes 262176 | tf_op jit(solution)/shard_map/ppermute | solution.py:194
  97.0 0.1 shard_map.86
  97.0 0.7 collective-permute-start.5
  97.7 1.5 %collective-permute-start.6 = (f32[32,1024]{1,0:T(8,128)S(1)}, f32[32,1024]{1,0:T(8,128)S(1)}, u32[]{:S(2)}, u32[]{:S(2)}) collective-permute-start(f32[32,1024]{1,0:T(8,128)S(1)} %get-tuple-element.49), channel_id=1, source_target_pairs={{0,128},{8,40},{16,144},{24,56},{32,160},{40,8},{48,176},{56,24},{... | collective-permute-start | bytes 393224 | tf_op jit(solution)/shard_map/ppermute | solution.py:198
  99.2 0.0 collective-permute-done.14.b
  99.2 2.6 %collective-permute-start.7 = (f32[32,1024]{1,0:T(8,128)S(1)}, f32[32,1024]{1,0:T(8,128)S(1)}, u32[]{:S(2)}, u32[]{:S(2)}) collective-permute-start(f32[32,1024]{1,0:T(8,128)S(1)} %get-tuple-element.50), channel_id=1, source_target_pairs={{0,192},{8,56},{16,208},{24,40},{32,224},{40,24},{48,240},{56,8},{... | collective-permute-start | bytes 393224 | tf_op jit(solution)/shard_map/ppermute | solution.py:198
  101.8 3.3 %collective-permute-start.17 = (f32[32,512]{1,0:T(8,128)S(1)}, f32[32,512]{1,0:T(8,128)S(1)}, u32[]{:S(2)}, u32[]{:S(2)}) collective-permute-start(f32[32,512]{1,0:T(8,128)S(1)} %get-tuple-element.65), channel_id=1, source_target_pairs={{0,2},{1,3},{2,0},{3,1},{4,6},{5,7},{6,4},{7,5},{8,10},{9,11},{10,... | collective-permute-start | bytes 196616 | tf_op jit(solution)/shard_map/ppermute | solution.py:201
  105.2 1.4 %collective-permute-start.18 = (f32[32,512]{1,0:T(8,128)S(1)}, f32[32,512]{1,0:T(8,128)S(1)}, u32[]{:S(2)}, u32[]{:S(2)}) collective-permute-start(f32[32,512]{1,0:T(8,128)S(1)} %get-tuple-element.66), channel_id=1, source_target_pairs={{0,3},{1,2},{2,1},{3,0},{4,7},{5,6},{6,5},{7,4},{8,11},{9,10},{10,... | collective-permute-start | bytes 196616 | tf_op jit(solution)/shard_map/ppermute | solution.py:201
  106.6 0.0 collective-permute-done.5.b
  106.6 0.0 collective-permute-done.6.c
  106.6 1.0 collective-permute-start.8
  107.6 3.8 %collective-permute-done.18.d = f32[32,512]{1,0:T(8,128)S(1)} collective-permute-done((f32[32,512]{1,0:T(8,128)S(1)}, f32[32,512]{1,0:T(8,128)S(1)}, u32[]{:S(2)}, u32[]{:S(2)}) %collective-permute-start.18) | collective-permute-done | bytes 65568 | tf_op jit(solution)/shard_map/ppermute | solution.py:201
  111.4 0.3 collective-permute-done.8.b
  111.7 5.8 %collective-permute-start.19 = (f32[32,256]{1,0:T(8,128)S(1)}, f32[32,256]{1,0:T(8,128)S(1)}, u32[]{:S(2)}, u32[]{:S(2)}) collective-permute-start(f32[32,256]{1,0:T(8,128)S(1)} %get-tuple-element.69), channel_id=1, source_target_pairs={{0,4},{1,5},{2,6},{3,7},{4,0},{5,1},{6,2},{7,3},{8,12},{9,13},{10,... | collective-permute-start | bytes 98312 | tf_op jit(solution)/shard_map/ppermute | solution.py:205
  118.2 1.6 %shard_map.94 = f32[32,256]{1,0:T(8,128)} custom-call(s32[4,2,16]{2,1,0:T(2,128)} %occ_index.1, f32[125]{0:T(128)} %occ_energy, s32[8]{0:T(128)} %block_sizes.1, s32[1]{0:T(128)S(6)} %copy.9.slab_irrep, f32[2048]{0:T(1024)} %virt_energy.1), custom_call_target="tpu_custom_call" | custom-call | tf_op jit(solution)/shard_map/pallas_call | solution.py:150
  119.8 1.4 %add_divide_fusion = f32[32,256]{1,0:T(8,128)} fusion(f32[32,256]{1,0:T(8,128)} %shard_map.94, f32[32,256]{1,0:T(8,128)S(1)} %get-tuple-element.67, f32[32,256]{1,0:T(8,128)S(1)} %collective-permute-done.19), kind=kLoop, calls=%fused_computation | loop fusion | flops 16384 | bytes 131072 | tf_op jit(solution)/shard_map/div | solution.py:210
  (12 shorter events, 0.1 us)
Async XLA Ops:
  0.7 2.2 %copy-start.1 = (bf16[32,65536]{1,0:T(8,128)(2,1)S(1)}, bf16[32,65536]{1,0:T(8,128)(2,1)}, u32[]{:S(2)}) copy-start(bf16[32,65536]{1,0:T(8,128)(2,1)} %amp_ref.1) | copy-start | bytes 12582916
  3.7 57.5 %copy-start = (bf16[2048,2048]{1,0:T(8,128)(2,1)S(1)}, bf16[2048,2048]{1,0:T(8,128)(2,1)}, u32[]{:S(2)}) copy-start(bf16[2048,2048]{1,0:T(8,128)(2,1)} %b_ref.7) | copy-start | bytes 25165828
  63.6 4.2 %collective-permute-start.9 = (f32[2,512,512]{2,1,0:T(8,128)S(1)}, f32[2,512,512]{2,1,0:T(8,128)S(1)}, u32[]{:S(2)}, u32[]{:S(2)}) collective-permute-start(f32[2,512,512]{2,1,0:T(8,128)S(1)} %shard_map.88), channel_id=1, source_target_pairs={{0,8},{8,0},{1,9},{9,1},{2,10},{10,2},{3,11},{11,3},{4,12},{12,4},... | collective-permute-start | bytes 6291464 | tf_op jit(solution)/shard_map/ppermute | solution.py:177
  66.2 6.3 %collective-permute-start = (f32[2,512,512]{2,1,0:T(8,128)S(1)}, f32[2,512,512]{2,1,0:T(8,128)S(1)}, u32[]{:S(2)}, u32[]{:S(2)}) collective-permute-start(f32[2,512,512]{2,1,0:T(8,128)S(1)} %shard_map.83), channel_id=1, source_target_pairs={{0,8},{8,0},{1,9},{9,1},{2,10},{10,2},{3,11},{11,3},{4,12},{12,4},... | collective-permute-start | bytes 6291464 | tf_op jit(solution)/shard_map/ppermute | solution.py:177
  70.2 9.3 %collective-permute-start.10 = (f32[256,512]{1,0:T(8,128)S(1)}, f32[256,512]{1,0:T(8,128)S(1)}, u32[]{:S(2)}, u32[]{:S(2)}) collective-permute-start(f32[256,512]{1,0:T(8,128)S(1)} %get-tuple-element.55), channel_id=1, source_target_pairs={{0,16},{8,72},{16,0},{24,88},{32,48},{40,104},{48,32},{56,120},{64... | collective-permute-start | bytes 1572872 | tf_op jit(solution)/shard_map/ppermute | solution.py:189
  71.8 9.2 %collective-permute-start.11 = (f32[256,512]{1,0:T(8,128)S(1)}, f32[256,512]{1,0:T(8,128)S(1)}, u32[]{:S(2)}, u32[]{:S(2)}) collective-permute-start(f32[256,512]{1,0:T(8,128)S(1)} %get-tuple-element.56), channel_id=1, source_target_pairs={{0,48},{8,200},{16,32},{24,216},{32,16},{40,232},{48,0},{56,248},{... | collective-permute-start | bytes 1572872 | tf_op jit(solution)/shard_map/ppermute | solution.py:189
  74.9 10.2 %collective-permute-start.1 = (f32[256,512]{1,0:T(8,128)S(1)}, f32[256,512]{1,0:T(8,128)S(1)}, u32[]{:S(2)}, u32[]{:S(2)}) collective-permute-start(f32[256,512]{1,0:T(8,128)S(1)} %get-tuple-element.41), channel_id=1, source_target_pairs={{0,16},{8,72},{16,0},{24,88},{32,48},{40,104},{48,32},{56,120},{64... | collective-permute-start | bytes 1572872 | tf_op jit(solution)/shard_map/ppermute | solution.py:189
  76.1 10.5 %collective-permute-start.2 = (f32[256,512]{1,0:T(8,128)S(1)}, f32[256,512]{1,0:T(8,128)S(1)}, u32[]{:S(2)}, u32[]{:S(2)}) collective-permute-start(f32[256,512]{1,0:T(8,128)S(1)} %get-tuple-element.42), channel_id=1, source_target_pairs={{0,48},{8,200},{16,32},{24,216},{32,16},{40,232},{48,0},{56,248},{... | collective-permute-start | bytes 1572872 | tf_op jit(solution)/shard_map/ppermute | solution.py:189
  81.1 8.7 %collective-permute-start.12 = (f32[128,512]{1,0:T(8,128)S(1)}, f32[128,512]{1,0:T(8,128)S(1)}, u32[]{:S(2)}, u32[]{:S(2)}) collective-permute-start(f32[128,512]{1,0:T(8,128)S(1)} %get-tuple-element.59), channel_id=1, source_target_pairs={{0,48},{8,200},{16,32},{24,216},{32,16},{40,232},{48,0},{56,248},{... | collective-permute-start | bytes 786440 | tf_op jit(solution)/shard_map/ppermute | solution.py:194
  81.9 7.9 %collective-permute-start.13 = (f32[128,512]{1,0:T(8,128)S(1)}, f32[128,512]{1,0:T(8,128)S(1)}, u32[]{:S(2)}, u32[]{:S(2)}) collective-permute-start(f32[128,512]{1,0:T(8,128)S(1)} %get-tuple-element.60), channel_id=1, source_target_pairs={{0,16},{8,72},{16,0},{24,88},{32,48},{40,104},{48,32},{56,120},{64... | collective-permute-start | bytes 786440 | tf_op jit(solution)/shard_map/ppermute | solution.py:194
  86.7 8.0 %collective-permute-start.3 = (f32[128,512]{1,0:T(8,128)S(1)}, f32[128,512]{1,0:T(8,128)S(1)}, u32[]{:S(2)}, u32[]{:S(2)}) collective-permute-start(f32[128,512]{1,0:T(8,128)S(1)} %get-tuple-element.45), channel_id=1, source_target_pairs={{0,48},{8,200},{16,32},{24,216},{32,16},{40,232},{48,0},{56,248},{... | collective-permute-start | bytes 786440 | tf_op jit(solution)/shard_map/ppermute | solution.py:194
  87.5 9.5 %collective-permute-start.4 = (f32[128,512]{1,0:T(8,128)S(1)}, f32[128,512]{1,0:T(8,128)S(1)}, u32[]{:S(2)}, u32[]{:S(2)}) collective-permute-start(f32[128,512]{1,0:T(8,128)S(1)} %get-tuple-element.46), channel_id=1, source_target_pairs={{0,16},{8,72},{16,0},{24,88},{32,48},{40,104},{48,32},{56,120},{64... | collective-permute-start | bytes 786440 | tf_op jit(solution)/shard_map/ppermute | solution.py:194
  89.9 9.3 %collective-permute-start.14 = (f32[32,1024]{1,0:T(8,128)S(1)}, f32[32,1024]{1,0:T(8,128)S(1)}, u32[]{:S(2)}, u32[]{:S(2)}) collective-permute-start(f32[32,1024]{1,0:T(8,128)S(1)} %get-tuple-element.62), channel_id=1, source_target_pairs={{0,64},{8,24},{16,80},{24,8},{32,96},{40,56},{48,112},{56,40},{64,... | collective-permute-start | bytes 393224 | tf_op jit(solution)/shard_map/ppermute | solution.py:198
  90.6 11.2 %collective-permute-start.15 = (f32[32,1024]{1,0:T(8,128)S(1)}, f32[32,1024]{1,0:T(8,128)S(1)}, u32[]{:S(2)}, u32[]{:S(2)}) collective-permute-start(f32[32,1024]{1,0:T(8,128)S(1)} %get-tuple-element.63), channel_id=1, source_target_pairs={{0,128},{8,40},{16,144},{24,56},{32,160},{40,8},{48,176},{56,24},{... | collective-permute-start | bytes 393224 | tf_op jit(solution)/shard_map/ppermute | solution.py:198
  92.3 9.5 %collective-permute-start.16 = (f32[32,1024]{1,0:T(8,128)S(1)}, f32[32,1024]{1,0:T(8,128)S(1)}, u32[]{:S(2)}, u32[]{:S(2)}) collective-permute-start(f32[32,1024]{1,0:T(8,128)S(1)} %get-tuple-element.64), channel_id=1, source_target_pairs={{0,192},{8,56},{16,208},{24,40},{32,224},{40,24},{48,240},{56,8},{... | collective-permute-start | bytes 393224 | tf_op jit(solution)/shard_map/ppermute | solution.py:198
  97.0 9.6 %collective-permute-start.5 = (f32[32,1024]{1,0:T(8,128)S(1)}, f32[32,1024]{1,0:T(8,128)S(1)}, u32[]{:S(2)}, u32[]{:S(2)}) collective-permute-start(f32[32,1024]{1,0:T(8,128)S(1)} %get-tuple-element.48), channel_id=1, source_target_pairs={{0,64},{8,24},{16,80},{24,8},{32,96},{40,56},{48,112},{56,40},{64,... | collective-permute-start | bytes 393224 | tf_op jit(solution)/shard_map/ppermute | solution.py:198
  97.7 8.9 %collective-permute-start.6 = (f32[32,1024]{1,0:T(8,128)S(1)}, f32[32,1024]{1,0:T(8,128)S(1)}, u32[]{:S(2)}, u32[]{:S(2)}) collective-permute-start(f32[32,1024]{1,0:T(8,128)S(1)} %get-tuple-element.49), channel_id=1, source_target_pairs={{0,128},{8,40},{16,144},{24,56},{32,160},{40,8},{48,176},{56,24},{... | collective-permute-start | bytes 393224 | tf_op jit(solution)/shard_map/ppermute | solution.py:198
  99.2 7.4 %collective-permute-start.7 = (f32[32,1024]{1,0:T(8,128)S(1)}, f32[32,1024]{1,0:T(8,128)S(1)}, u32[]{:S(2)}, u32[]{:S(2)}) collective-permute-start(f32[32,1024]{1,0:T(8,128)S(1)} %get-tuple-element.50), channel_id=1, source_target_pairs={{0,192},{8,56},{16,208},{24,40},{32,224},{40,24},{48,240},{56,8},{... | collective-permute-start | bytes 393224 | tf_op jit(solution)/shard_map/ppermute | solution.py:198
  101.8 5.8 %collective-permute-start.17 = (f32[32,512]{1,0:T(8,128)S(1)}, f32[32,512]{1,0:T(8,128)S(1)}, u32[]{:S(2)}, u32[]{:S(2)}) collective-permute-start(f32[32,512]{1,0:T(8,128)S(1)} %get-tuple-element.65), channel_id=1, source_target_pairs={{0,2},{1,3},{2,0},{3,1},{4,6},{5,7},{6,4},{7,5},{8,10},{9,11},{10,... | collective-permute-start | bytes 196616 | tf_op jit(solution)/shard_map/ppermute | solution.py:201
  105.2 6.2 %collective-permute-start.18 = (f32[32,512]{1,0:T(8,128)S(1)}, f32[32,512]{1,0:T(8,128)S(1)}, u32[]{:S(2)}, u32[]{:S(2)}) collective-permute-start(f32[32,512]{1,0:T(8,128)S(1)} %get-tuple-element.66), channel_id=1, source_target_pairs={{0,3},{1,2},{2,1},{3,0},{4,7},{5,6},{6,5},{7,4},{8,11},{9,10},{10,... | collective-permute-start | bytes 196616 | tf_op jit(solution)/shard_map/ppermute | solution.py:201
  106.6 5.1 %collective-permute-start.8 = (f32[32,512]{1,0:T(8,128)S(1)}, f32[32,512]{1,0:T(8,128)S(1)}, u32[]{:S(2)}, u32[]{:S(2)}) collective-permute-start(f32[32,512]{1,0:T(8,128)S(1)} %get-tuple-element.52), channel_id=1, source_target_pairs={{0,1},{1,0},{2,3},{3,2},{4,5},{5,4},{6,7},{7,6},{8,9},{9,8},{10,11... | collective-permute-start | bytes 196616 | tf_op jit(solution)/shard_map/ppermute | solution.py:201
  111.7 8.1 %collective-permute-start.19 = (f32[32,256]{1,0:T(8,128)S(1)}, f32[32,256]{1,0:T(8,128)S(1)}, u32[]{:S(2)}, u32[]{:S(2)}) collective-permute-start(f32[32,256]{1,0:T(8,128)S(1)} %get-tuple-element.69), channel_id=1, source_target_pairs={{0,4},{1,5},{2,6},{3,7},{4,0},{5,1},{6,2},{7,3},{8,12},{9,13},{10,... | collective-permute-start | bytes 98312 | tf_op jit(solution)/shard_map/ppermute | solution.py:205

commit v5 on v4

--- a/solution.py
+++ b/solution.py
@@ -78,19 +78,44 @@
         out_ref[half, :, cols] = out
 
 
+def encode(x, out_ref, cols):
+    n = x.shape[0]
+    parts = [x[i : i + 16] for i in range(0, n, 16)]
+    peak = jnp.abs(parts[0])
+    for part in parts[1:]:
+        peak = jnp.maximum(peak, jnp.abs(part))
+    exponent = jnp.floor(jnp.log2(jnp.maximum(peak, 1e-30))) + 1.0
+    scale = jnp.exp2(15.0 - exponent)
+    for i, part in enumerate(parts):
+        code = jnp.clip(jnp.round(part * scale), -32767.0, 32767.0)
+        out_ref[16 * i : 16 * (i + 1), cols] = code.astype(jnp.int32).astype(jnp.int16)
+    out_ref[n : n + 16, cols] = exponent.astype(jnp.int32).astype(jnp.int16)
+
+
+def decode(ref, first, rows):
+    n = ref.shape[0] - 16
+    exponent = ref[n : n + 16].astype(jnp.int32).astype(jnp.float32)
+    scale = jnp.exp2(exponent - 15.0)
+    parts = [
+        ref[i : i + 16].astype(jnp.int32).astype(jnp.float32) * scale
+        for i in range(first, first + rows, 16)
+    ]
+    return jnp.concatenate(parts, axis=0)
+
+
 def home_kernel(group, amp_ref, b_ref, arrived_ref, far0, far1, near0, near1, lhs):
-    n = far0.shape[0]
+    n = near0.shape[0]
     for half, cols, out in dot_tiles(0, group, amp_ref, b_ref, lhs):
         out += arrived_ref[half, :, cols]
         (near0, near1)[half][:, cols] = out[:n]
-        (far0, far1)[half][:, cols] = out[n:]
+        encode(out[n:], (far0, far1)[half], cols)
 
 
 def in_vmem(kernel, shapes, *args, scratch=(), limit=24):
     vmem = pl.BlockSpec(memory_space=pltpu.VMEM)
     return pl.pallas_call(
         kernel,
-        out_shape=[jax.ShapeDtypeStruct(shape, jnp.float32) for shape in shapes],
+        out_shape=[jax.ShapeDtypeStruct(*shape) for shape in shapes],
         in_specs=[vmem] * len(args),
         out_specs=[vmem] * len(shapes),
         scratch_shapes=scratch,
@@ -100,10 +125,10 @@
 
 
 def step_kernel(keep0, keep1, got0, got1, far0, far1, near0, near1):
-    n = far0.shape[0]
+    n = near0.shape[0]
     for keep, got, far, near in ((keep0, got0, far0, near0), (keep1, got1, far1, near1)):
-        near[...] = keep[:n] + got[:n]
-        far[...] = keep[n:] + got[n:]
+        near[...] = keep[:n] + decode(got, 0, n)
+        encode(keep[n:] + decode(got, n, n), far, slice(None))
 
 
 def join_kernel(keep0, keep1, got0, got1, *outs):
@@ -111,8 +136,8 @@
     quarter = keep0.shape[1]
     for k, out in enumerate(outs):
         part = slice(k * rows, (k + 1) * rows)
-        out[:, :quarter] = keep0[part] + got0[part]
-        out[:, quarter:] = keep1[part] + got1[part]
+        out[:, :quarter] = keep0[part] + decode(got0, k * rows, rows)
+        out[:, quarter:] = keep1[part] + decode(got1, k * rows, rows)
 
 
 def sum_kernel(a, b, c, d, left, right):
@@ -152,6 +177,7 @@
         out_shape=jax.ShapeDtypeStruct((rows, columns), jnp.float32),
         in_specs=[pl.BlockSpec(memory_space=pltpu.SMEM)] * len(args),
         out_specs=pl.BlockSpec(memory_space=pltpu.VMEM),
+        cost_estimate=pl.CostEstimate(flops=0, bytes_accessed=0, transcendentals=0),
     )(*args)
 
 
@@ -164,12 +190,16 @@
     ordered = pack(amplitudes, tile_perm, tile)
     received = lax.all_to_all(ordered, RED, split_axis=0, concat_axis=0, tiled=True)
     m, quarter = 16 * rows, 2 * columns
+
+    def stage(n):
+        return [((n + 16, quarter), jnp.int16)] * 2 + [((n, quarter), jnp.float32)] * 2
+
     lhs = [pltpu.VMEM((m, tile), amplitudes.dtype)]
     arrived = []
     for group in range(2):
         (away,) = in_vmem(
             functools.partial(away_kernel, group),
-            [(2, m, quarter)],
+            [((2, m, quarter), jnp.float32)],
             received,
             integrals,
             scratch=lhs,
@@ -179,7 +209,7 @@
     for group in range(2):
         far0, far1, *near = in_vmem(
             functools.partial(home_kernel, group),
-            [(m // 2, quarter)] * 4,
+            stage(m // 2),
             received,
             integrals,
             arrived[group],
@@ -187,26 +217,26 @@
         )
         keeps.append(near)
         gots.append([lax.ppermute(far, RED, pairs(0, MASKS[h][0])) for h, far in enumerate((far0, far1))])
+    keeps[1], occ_energy = lax.optimization_barrier((keeps[1], occ_energy))
+    gap = energy_gap(
+        rows, columns, occ_index, occ_energy, block_sizes, slab_irrep, virt_energy
+    )
+    gots[0], gap = lax.optimization_barrier((gots[0], gap))
     last, more = [], []
     for group in range(2):
-        far0, far1, *near = in_vmem(step_kernel, [(m // 4, quarter)] * 4, *keeps[group], *gots[group])
+        far0, far1, *near = in_vmem(step_kernel, stage(m // 4), *keeps[group], *gots[group])
         last.append(near)
         more.append([lax.ppermute(far, RED, pairs(0, MASKS[h][1])) for h, far in enumerate((far0, far1))])
     blocks = []
     for group in range(2):
-        mine, *sends = in_vmem(join_kernel, [(rows, 2 * quarter)] * 4, *last[group], *more[group])
+        mine, *sends = in_vmem(join_kernel, [((rows, 2 * quarter), jnp.float32)] * 4, *last[group], *more[group])
         gots = [lax.ppermute(send, RED, pairs(1, k + 1)) for k, send in enumerate(sends)]
-        blocks += in_vmem(sum_kernel, [(rows, quarter)] * 2, mine, *gots)
+        blocks += in_vmem(sum_kernel, [((rows, quarter), jnp.float32)] * 2, mine, *gots)
     gots = [
         lax.ppermute(blocks[k], "rep", [(i, i ^ k) for i in range(N_REP)]) for k in range(1, 4)
     ]
-    mine, send = in_vmem(sum_kernel, [(rows, columns)] * 2, blocks[0], *gots)
-    send, occ_energy = lax.optimization_barrier((send, occ_energy))
+    mine, send = in_vmem(sum_kernel, [((rows, columns), jnp.float32)] * 2, blocks[0], *gots)
     got = lax.ppermute(send, "rep", [(i, i ^ 4) for i in range(N_REP)])
-    gap = energy_gap(
-        rows, columns, occ_index, occ_energy, block_sizes, slab_irrep, virt_energy
-    )
-    got, gap = lax.optimization_barrier((got, gap))
     return (mine + got) / gap
 
 

time: 122 us -> 117 us (0.959)
  waiting for transfers between devices: 13.5 us -> 8.37 us
    ppermute x4, waiting for transfers between devices: 5.87 us -> 0.7 us  [body(): lax.ppermute(far, RED, pairs(0, MASKS[h][0]))]
    ppermute x1, waiting for transfers between devices: 0.01 us -> 2.1 us  [body(): got = lax.ppermute(send, 'rep', [(i, i ^ 4) for i in range(N_REP)])]
    ppermute x4, waiting for transfers between devices: 2.31 us -> 0.38 us  [body(): lax.ppermute(far, RED, pairs(0, MASKS[h][1]))]
  transfers between devices with their start and end apart: 20 -> 20, of which waited for: 8 -> 6; matrix products, arithmetic and copies ran while one was open for 0% -> 0% of each run, Pallas kernels for 8% -> 9%
where the time goes in v5:
time: 117 us; the launch traced here: 116 us
  blocking collectives  57.5 us (49%)
  starting transfers between devices  32.9 us (28%)
  Pallas kernels  13.1 us (11%)
  waiting for transfers between devices  8.37 us (7%)
  local copies, waits for them, and re-layouts  2.2 us (2%)
  other arithmetic  1.28 us (1%)
    all_to_all x1, blocking collectives, body(): lax.all_to_all(ordered, RED, split_axis=0, concat_axis=0, tiled=True)  57.5 us
    pallas_call x11, Pallas kernels, in_vmem(): pl.pallas_call(kernel, out_shape=[jax.ShapeDtypeStruct(*shape) for shape...  10.7 us
    ppermute x6, starting transfers between devices, body(): lax.ppermute(send, RED, pairs(1, k + 1))  9.56 us
    ppermute x4, starting transfers between devices, body(): lax.ppermute(far, RED, pairs(0, MASKS[h][1]))  6.23 us
    ppermute x3, starting transfers between devices, body(): lax.ppermute(blocks[k], 'rep', [(i, i ^ k) for i in range(N_REP)])  5.82 us
    ppermute x1, starting transfers between devices, body(): got = lax.ppermute(send, 'rep', [(i, i ^ 4) for i in range(N_REP)])  5.81 us
    ppermute x4, starting transfers between devices, body(): lax.ppermute(far, RED, pairs(0, MASKS[h][0]))  4.83 us
    ppermute x3, waiting for transfers between devices, body(): lax.ppermute(blocks[k], 'rep', [(i, i ^ k) for i in range(N_REP)])  3.98 us
  transfers between devices with their start and end apart: 20, of which 6 were waited for; matrix products, arithmetic and copies ran while one was open for 0% of the time, Pallas kernels for 9%

profile of v5, /device:TPU:2, one launch (start us, length us, event | category | flops | bytes accessed | tf_op | source)
XLA Modules:
  0.0 116.1 jit_solution(17270546730688091935)
XLA Ops:
  0.0 0.7 broadcast_multiply_fusion.first_ref
  0.7 2.2 %copy-done.1 = bf16[32,65536]{1,0:T(8,128)(2,1)S(1)} copy-done((bf16[32,65536]{1,0:T(8,128)(2,1)S(1)}, bf16[32,65536]{1,0:T(8,128)(2,1)}, u32[]{:S(2)}) %copy-start.1) | copy-done | bytes 4194328
  2.8 0.8 shard_map.82
  3.7 0.0 copy-start
  3.7 57.5 %all_to_all.5.amp_ref = bf16[32,32,2048]{2,1,0:T(8,128)(2,1)S(1)} all-to-all(bf16[32,32,2048]{2,1,0:T(8,128)(2,1)S(1)} %shard_map.82), channel_id=1, replica_groups=mesh['y'=4,'x'=4,'core'=2,'rep'=8] {'y','x','core'}, dimensions={0} | all-to-all | bytes 8388608 | tf_op jit(solution)/shard_map/all_to_all | solution.py:191
  61.2 2.4 %shard_map.85 = f32[2,512,512]{2,1,0:T(8,128)S(1)} custom-call(bf16[32,32,2048]{2,1,0:T(8,128)(2,1)S(1)} %all_to_all.5.amp_ref, bf16[2048,2048]{1,0:T(8,128)(2,1)S(1)} %copy-done), custom_call_target="tpu_custom_call" | custom-call | tf_op jit(solution)/shard_map/pallas_call | solution.py:116
  63.6 0.3 collective-permute-start.3
  63.8 2.4 %shard_map.83 = f32[2,512,512]{2,1,0:T(8,128)S(1)} custom-call(bf16[32,32,2048]{2,1,0:T(8,128)(2,1)S(1)} %all_to_all.5.amp_ref, bf16[2048,2048]{1,0:T(8,128)(2,1)S(1)} %copy-done), custom_call_target="tpu_custom_call" | custom-call | tf_op jit(solution)/shard_map/pallas_call | solution.py:116
  66.2 0.4 collective-permute-start
  66.6 1.2 %collective-permute-done.3.arrived_ref = f32[2,512,512]{2,1,0:T(8,128)S(1)} collective-permute-done((f32[2,512,512]{2,1,0:T(8,128)S(1)}, f32[2,512,512]{2,1,0:T(8,128)S(1)}, u32[]{:S(2)}, u32[]{:S(2)}) %collective-permute-start.3) | collective-permute-done | bytes 2097184 | tf_op jit(solution)/shard_map/ppermute | solution.py:207
  67.8 2.6 %shard_map.86 = (s16[272,512]{1,0:T(8,128)(2,1)S(1)}, s16[272,512]{1,0:T(8,128)(2,1)S(1)}, f32[256,512]{1,0:T(8,128)S(1)}, f32[256,512]{1,0:T(8,128)S(1)}) custom-call(bf16[32,32,2048]{2,1,0:T(8,128)(2,1)S(1)} %all_to_all.5.amp_ref, bf16[2048,2048]{1,0:T(8,128)(2,1)S(1)} %copy-done, f32[2,512,512]{2,1,0:T(8,128)S(1)} %collective-permute-done.3.arrived_ref), custom_call_target="tpu_custom_call" | custom-call | tf_op jit(solution)/shard_map/pallas_call | solution.py:116
  70.4 1.5 %collective-permute-start.10 = (s16[272,512]{1,0:T(8,128)(2,1)S(1)}, s16[272,512]{1,0:T(8,128)(2,1)S(1)}, u32[]{:S(2)}, u32[]{:S(2)}) collective-permute-start(s16[272,512]{1,0:T(8,128)(2,1)S(1)} %get-tuple-element.62), channel_id=1, source_target_pairs={{0,16},{8,72},{16,0},{24,88},{32,48},{40,104},{48,32},{56,120},{64... | collective-permute-start | bytes 835592 | tf_op jit(solution)/shard_map/ppermute | solution.py:219
  71.9 0.7 collective-permute-start.11
  72.6 2.6 %shard_map.84 = (s16[272,512]{1,0:T(8,128)(2,1)S(1)}, s16[272,512]{1,0:T(8,128)(2,1)S(1)}, f32[256,512]{1,0:T(8,128)S(1)}, f32[256,512]{1,0:T(8,128)S(1)}) custom-call(bf16[32,32,2048]{2,1,0:T(8,128)(2,1)S(1)} %all_to_all.5.amp_ref, bf16[2048,2048]{1,0:T(8,128)(2,1)S(1)} %copy-done, f32[2,512,512]{2,1,0:T(8,128)S(1)} %collective-permute-done.arrived_ref), custom_call_target="tpu_custom_call" | custom-call | tf_op jit(solution)/shard_map/pallas_call | solution.py:116
  75.2 1.2 %collective-permute-start.1 = (s16[272,512]{1,0:T(8,128)(2,1)S(1)}, s16[272,512]{1,0:T(8,128)(2,1)S(1)}, u32[]{:S(2)}, u32[]{:S(2)}) collective-permute-start(s16[272,512]{1,0:T(8,128)(2,1)S(1)} %get-tuple-element.43), channel_id=1, source_target_pairs={{0,16},{8,72},{16,0},{24,88},{32,48},{40,104},{48,32},{56,120},{64... | collective-permute-start | bytes 835592 | tf_op jit(solution)/shard_map/ppermute | solution.py:219
  76.4 1.4 %collective-permute-start.2 = (s16[272,512]{1,0:T(8,128)(2,1)S(1)}, s16[272,512]{1,0:T(8,128)(2,1)S(1)}, u32[]{:S(2)}, u32[]{:S(2)}) collective-permute-start(s16[272,512]{1,0:T(8,128)(2,1)S(1)} %get-tuple-element.44), channel_id=1, source_target_pairs={{0,48},{8,200},{16,32},{24,216},{32,16},{40,232},{48,0},{56,248},{... | collective-permute-start | bytes 835592 | tf_op jit(solution)/shard_map/ppermute | solution.py:219
  77.8 0.0 collective-permute-done.10.got0
  77.8 0.7 collective-permute-done.11.got1
  78.5 0.3 shard_map.91
  78.8 0.8 collective-permute-start.12
  79.6 2.3 %collective-permute-start.13 = (s16[144,512]{1,0:T(8,128)(2,1)S(1)}, s16[144,512]{1,0:T(8,128)(2,1)S(1)}, u32[]{:S(2)}, u32[]{:S(2)}) collective-permute-start(s16[144,512]{1,0:T(8,128)(2,1)S(1)} %get-tuple-element.67), channel_id=1, source_target_pairs={{0,16},{8,72},{16,0},{24,88},{32,48},{40,104},{48,32},{56,120},{64... | collective-permute-start | bytes 442376 | tf_op jit(solution)/shard_map/ppermute | solution.py:229
  82.5 1.6 %shard_map.87 = f32[32,256]{1,0:T(8,128)} custom-call(s32[4,2,16]{2,1,0:T(2,128)} %occ_index.1, f32[125]{0:T(128)} %occ_energy, s32[8]{0:T(128)} %block_sizes.1, s32[1]{0:T(128)S(6)} %copy.9.slab_irrep, f32[2048]{0:T(1024)} %virt_energy.1), custom_call_target="tpu_custom_call" | custom-call | tf_op jit(solution)/shard_map/pallas_call | solution.py:175
  84.1 0.0 collective-permute-done.1.got0
  84.2 0.3 shard_map.88
  84.4 1.6 %collective-permute-start.4 = (s16[144,512]{1,0:T(8,128)(2,1)S(1)}, s16[144,512]{1,0:T(8,128)(2,1)S(1)}, u32[]{:S(2)}, u32[]{:S(2)}) collective-permute-start(s16[144,512]{1,0:T(8,128)(2,1)S(1)} %get-tuple-element.52), channel_id=1, source_target_pairs={{0,48},{8,200},{16,32},{24,216},{32,16},{40,232},{48,0},{56,248},{... | collective-permute-start | bytes 442376 | tf_op jit(solution)/shard_map/ppermute | solution.py:229
  86.1 1.5 %collective-permute-start.5 = (s16[144,512]{1,0:T(8,128)(2,1)S(1)}, s16[144,512]{1,0:T(8,128)(2,1)S(1)}, u32[]{:S(2)}, u32[]{:S(2)}) collective-permute-start(s16[144,512]{1,0:T(8,128)(2,1)S(1)} %get-tuple-element.53), channel_id=1, source_target_pairs={{0,16},{8,72},{16,0},{24,88},{32,48},{40,104},{48,32},{56,120},{64... | collective-permute-start | bytes 442376 | tf_op jit(solution)/shard_map/ppermute | solution.py:229
  87.6 0.0 collective-permute-done.12.got0
  87.6 0.1 shard_map.92
  87.7 0.1 collective-permute-start.14
  87.8 2.3 %collective-permute-start.15 = (f32[32,1024]{1,0:T(8,128)S(1)}, f32[32,1024]{1,0:T(8,128)S(1)}, u32[]{:S(2)}, u32[]{:S(2)}) collective-permute-start(f32[32,1024]{1,0:T(8,128)S(1)} %get-tuple-element.70), channel_id=1, source_target_pairs={{0,128},{8,40},{16,144},{24,56},{32,160},{40,8},{48,176},{56,24},{... | collective-permute-start | bytes 393224 | tf_op jit(solution)/shard_map/ppermute | solution.py:233
  90.1 2.4 %collective-permute-start.16 = (f32[32,1024]{1,0:T(8,128)S(1)}, f32[32,1024]{1,0:T(8,128)S(1)}, u32[]{:S(2)}, u32[]{:S(2)}) collective-permute-start(f32[32,1024]{1,0:T(8,128)S(1)} %get-tuple-element.71), channel_id=1, source_target_pairs={{0,192},{8,56},{16,208},{24,40},{32,224},{40,24},{48,240},{56,8},{... | collective-permute-start | bytes 393224 | tf_op jit(solution)/shard_map/ppermute | solution.py:233
  92.4 0.0 collective-permute-done.4.got0
  92.4 0.4 collective-permute-done.5.got1
  92.8 0.1 shard_map.89
  92.9 0.1 collective-permute-start.6
  93.0 2.4 %collective-permute-start.7 = (f32[32,1024]{1,0:T(8,128)S(1)}, f32[32,1024]{1,0:T(8,128)S(1)}, u32[]{:S(2)}, u32[]{:S(2)}) collective-permute-start(f32[32,1024]{1,0:T(8,128)S(1)} %get-tuple-element.56), channel_id=1, source_target_pairs={{0,128},{8,40},{16,144},{24,56},{32,160},{40,8},{48,176},{56,24},{... | collective-permute-start | bytes 393224 | tf_op jit(solution)/shard_map/ppermute | solution.py:233
  95.4 0.0 collective-permute-done.14.b
  95.4 2.3 %collective-permute-start.8 = (f32[32,1024]{1,0:T(8,128)S(1)}, f32[32,1024]{1,0:T(8,128)S(1)}, u32[]{:S(2)}, u32[]{:S(2)}) collective-permute-start(f32[32,1024]{1,0:T(8,128)S(1)} %get-tuple-element.57), channel_id=1, source_target_pairs={{0,192},{8,56},{16,208},{24,40},{32,224},{40,24},{48,240},{56,8},{... | collective-permute-start | bytes 393224 | tf_op jit(solution)/shard_map/ppermute | solution.py:233
  97.7 0.0 collective-permute-done.16.d
  97.7 3.3 %collective-permute-start.17 = (f32[32,512]{1,0:T(8,128)S(1)}, f32[32,512]{1,0:T(8,128)S(1)}, u32[]{:S(2)}, u32[]{:S(2)}) collective-permute-start(f32[32,512]{1,0:T(8,128)S(1)} %get-tuple-element.72), channel_id=1, source_target_pairs={{0,2},{1,3},{2,0},{3,1},{4,6},{5,7},{6,4},{7,5},{8,10},{9,11},{10,... | collective-permute-start | bytes 196616 | tf_op jit(solution)/shard_map/ppermute | solution.py:236
  101.1 1.4 %collective-permute-start.18 = (f32[32,512]{1,0:T(8,128)S(1)}, f32[32,512]{1,0:T(8,128)S(1)}, u32[]{:S(2)}, u32[]{:S(2)}) collective-permute-start(f32[32,512]{1,0:T(8,128)S(1)} %get-tuple-element.73), channel_id=1, source_target_pairs={{0,3},{1,2},{2,1},{3,0},{4,7},{5,6},{6,5},{7,4},{8,11},{9,10},{10,... | collective-permute-start | bytes 196616 | tf_op jit(solution)/shard_map/ppermute | solution.py:236
  102.5 1.1 collective-permute-start.9
  103.6 0.0 collective-permute-done.17.c
  103.6 3.7 %collective-permute-done.18.d = f32[32,512]{1,0:T(8,128)S(1)} collective-permute-done((f32[32,512]{1,0:T(8,128)S(1)}, f32[32,512]{1,0:T(8,128)S(1)}, u32[]{:S(2)}, u32[]{:S(2)}) %collective-permute-start.18) | collective-permute-done | bytes 65568 | tf_op jit(solution)/shard_map/ppermute | solution.py:236
  107.3 0.3 collective-permute-done.9.b
  107.6 5.8 %collective-permute-start.19 = (f32[32,256]{1,0:T(8,128)S(1)}, f32[32,256]{1,0:T(8,128)S(1)}, u32[]{:S(2)}, u32[]{:S(2)}) collective-permute-start(f32[32,256]{1,0:T(8,128)S(1)} %get-tuple-element.75), channel_id=1, source_target_pairs={{0,4},{1,5},{2,6},{3,7},{4,0},{5,1},{6,2},{7,3},{8,12},{9,13},{10,... | collective-permute-start | bytes 98312 | tf_op jit(solution)/shard_map/ppermute | solution.py:239
  113.4 2.1 %collective-permute-done.19 = f32[32,256]{1,0:T(8,128)S(1)} collective-permute-done((f32[32,256]{1,0:T(8,128)S(1)}, f32[32,256]{1,0:T(8,128)S(1)}, u32[]{:S(2)}, u32[]{:S(2)}) %collective-permute-start.19) | collective-permute-done | bytes 32800 | tf_op jit(solution)/shard_map/ppermute | solution.py:239
  115.5 0.6 add_divide_fusion
  (14 shorter events, 0.1 us)
Async XLA Ops:
  0.7 2.2 %copy-start.1 = (bf16[32,65536]{1,0:T(8,128)(2,1)S(1)}, bf16[32,65536]{1,0:T(8,128)(2,1)}, u32[]{:S(2)}) copy-start(bf16[32,65536]{1,0:T(8,128)(2,1)} %amp_ref.1) | copy-start | bytes 12582916
  3.7 57.5 %copy-start = (bf16[2048,2048]{1,0:T(8,128)(2,1)S(1)}, bf16[2048,2048]{1,0:T(8,128)(2,1)}, u32[]{:S(2)}) copy-start(bf16[2048,2048]{1,0:T(8,128)(2,1)} %b_ref.7) | copy-start | bytes 25165828
  63.6 4.2 %collective-permute-start.3 = (f32[2,512,512]{2,1,0:T(8,128)S(1)}, f32[2,512,512]{2,1,0:T(8,128)S(1)}, u32[]{:S(2)}, u32[]{:S(2)}) collective-permute-start(f32[2,512,512]{2,1,0:T(8,128)S(1)} %shard_map.85), channel_id=1, source_target_pairs={{0,8},{8,0},{1,9},{9,1},{2,10},{10,2},{3,11},{11,3},{4,12},{12,4},... | collective-permute-start | bytes 6291464 | tf_op jit(solution)/shard_map/ppermute | solution.py:207
  66.2 6.4 %collective-permute-start = (f32[2,512,512]{2,1,0:T(8,128)S(1)}, f32[2,512,512]{2,1,0:T(8,128)S(1)}, u32[]{:S(2)}, u32[]{:S(2)}) collective-permute-start(f32[2,512,512]{2,1,0:T(8,128)S(1)} %shard_map.83), channel_id=1, source_target_pairs={{0,8},{8,0},{1,9},{9,1},{2,10},{10,2},{3,11},{11,3},{4,12},{12,4},... | collective-permute-start | bytes 6291464 | tf_op jit(solution)/shard_map/ppermute | solution.py:207
  70.4 7.4 %collective-permute-start.10 = (s16[272,512]{1,0:T(8,128)(2,1)S(1)}, s16[272,512]{1,0:T(8,128)(2,1)S(1)}, u32[]{:S(2)}, u32[]{:S(2)}) collective-permute-start(s16[272,512]{1,0:T(8,128)(2,1)S(1)} %get-tuple-element.62), channel_id=1, source_target_pairs={{0,16},{8,72},{16,0},{24,88},{32,48},{40,104},{48,32},{56,120},{64... | collective-permute-start | bytes 835592 | tf_op jit(solution)/shard_map/ppermute | solution.py:219
  71.9 6.5 %collective-permute-start.11 = (s16[272,512]{1,0:T(8,128)(2,1)S(1)}, s16[272,512]{1,0:T(8,128)(2,1)S(1)}, u32[]{:S(2)}, u32[]{:S(2)}) collective-permute-start(s16[272,512]{1,0:T(8,128)(2,1)S(1)} %get-tuple-element.63), channel_id=1, source_target_pairs={{0,48},{8,200},{16,32},{24,216},{32,16},{40,232},{48,0},{56,248},{... | collective-permute-start | bytes 835592 | tf_op jit(solution)/shard_map/ppermute | solution.py:219
  75.2 8.9 %collective-permute-start.1 = (s16[272,512]{1,0:T(8,128)(2,1)S(1)}, s16[272,512]{1,0:T(8,128)(2,1)S(1)}, u32[]{:S(2)}, u32[]{:S(2)}) collective-permute-start(s16[272,512]{1,0:T(8,128)(2,1)S(1)} %get-tuple-element.43), channel_id=1, source_target_pairs={{0,16},{8,72},{16,0},{24,88},{32,48},{40,104},{48,32},{56,120},{64... | collective-permute-start | bytes 835592 | tf_op jit(solution)/shard_map/ppermute | solution.py:219
  76.4 7.7 %collective-permute-start.2 = (s16[272,512]{1,0:T(8,128)(2,1)S(1)}, s16[272,512]{1,0:T(8,128)(2,1)S(1)}, u32[]{:S(2)}, u32[]{:S(2)}) collective-permute-start(s16[272,512]{1,0:T(8,128)(2,1)S(1)} %get-tuple-element.44), channel_id=1, source_target_pairs={{0,48},{8,200},{16,32},{24,216},{32,16},{40,232},{48,0},{56,248},{... | collective-permute-start | bytes 835592 | tf_op jit(solution)/shard_map/ppermute | solution.py:219
  78.8 8.8 %collective-permute-start.12 = (s16[144,512]{1,0:T(8,128)(2,1)S(1)}, s16[144,512]{1,0:T(8,128)(2,1)S(1)}, u32[]{:S(2)}, u32[]{:S(2)}) collective-permute-start(s16[144,512]{1,0:T(8,128)(2,1)S(1)} %get-tuple-element.66), channel_id=1, source_target_pairs={{0,48},{8,200},{16,32},{24,216},{32,16},{40,232},{48,0},{56,248},{... | collective-permute-start | bytes 442376 | tf_op jit(solution)/shard_map/ppermute | solution.py:229
  79.6 8.0 %collective-permute-start.13 = (s16[144,512]{1,0:T(8,128)(2,1)S(1)}, s16[144,512]{1,0:T(8,128)(2,1)S(1)}, u32[]{:S(2)}, u32[]{:S(2)}) collective-permute-start(s16[144,512]{1,0:T(8,128)(2,1)S(1)} %get-tuple-element.67), channel_id=1, source_target_pairs={{0,16},{8,72},{16,0},{24,88},{32,48},{40,104},{48,32},{56,120},{64... | collective-permute-start | bytes 442376 | tf_op jit(solution)/shard_map/ppermute | solution.py:229
  84.1 31.4 %copy-start.2 = (f32[32,256]{1,0:T(8,128)S(1)}, f32[32,256]{1,0:T(8,128)}, u32[]{:S(2)}) copy-start(f32[32,256]{1,0:T(8,128)} %shard_map.87) | copy-start | bytes 98308
  84.4 8.0 %collective-permute-start.4 = (s16[144,512]{1,0:T(8,128)(2,1)S(1)}, s16[144,512]{1,0:T(8,128)(2,1)S(1)}, u32[]{:S(2)}, u32[]{:S(2)}) collective-permute-start(s16[144,512]{1,0:T(8,128)(2,1)S(1)} %get-tuple-element.52), channel_id=1, source_target_pairs={{0,48},{8,200},{16,32},{24,216},{32,16},{40,232},{48,0},{56,248},{... | collective-permute-start | bytes 442376 | tf_op jit(solution)/shard_map/ppermute | solution.py:229
  86.1 6.7 %collective-permute-start.5 = (s16[144,512]{1,0:T(8,128)(2,1)S(1)}, s16[144,512]{1,0:T(8,128)(2,1)S(1)}, u32[]{:S(2)}, u32[]{:S(2)}) collective-permute-start(s16[144,512]{1,0:T(8,128)(2,1)S(1)} %get-tuple-element.53), channel_id=1, source_target_pairs={{0,16},{8,72},{16,0},{24,88},{32,48},{40,104},{48,32},{56,120},{64... | collective-permute-start | bytes 442376 | tf_op jit(solution)/shard_map/ppermute | solution.py:229
  87.7 7.8 %collective-permute-start.14 = (f32[32,1024]{1,0:T(8,128)S(1)}, f32[32,1024]{1,0:T(8,128)S(1)}, u32[]{:S(2)}, u32[]{:S(2)}) collective-permute-start(f32[32,1024]{1,0:T(8,128)S(1)} %get-tuple-element.69), channel_id=1, source_target_pairs={{0,64},{8,24},{16,80},{24,8},{32,96},{40,56},{48,112},{56,40},{64,... | collective-permute-start | bytes 393224 | tf_op jit(solution)/shard_map/ppermute | solution.py:233
  87.8 9.9 %collective-permute-start.15 = (f32[32,1024]{1,0:T(8,128)S(1)}, f32[32,1024]{1,0:T(8,128)S(1)}, u32[]{:S(2)}, u32[]{:S(2)}) collective-permute-start(f32[32,1024]{1,0:T(8,128)S(1)} %get-tuple-element.70), channel_id=1, source_target_pairs={{0,128},{8,40},{16,144},{24,56},{32,160},{40,8},{48,176},{56,24},{... | collective-permute-start | bytes 393224 | tf_op jit(solution)/shard_map/ppermute | solution.py:233
  90.1 7.6 %collective-permute-start.16 = (f32[32,1024]{1,0:T(8,128)S(1)}, f32[32,1024]{1,0:T(8,128)S(1)}, u32[]{:S(2)}, u32[]{:S(2)}) collective-permute-start(f32[32,1024]{1,0:T(8,128)S(1)} %get-tuple-element.71), channel_id=1, source_target_pairs={{0,192},{8,56},{16,208},{24,40},{32,224},{40,24},{48,240},{56,8},{... | collective-permute-start | bytes 393224 | tf_op jit(solution)/shard_map/ppermute | solution.py:233
  92.9 9.6 %collective-permute-start.6 = (f32[32,1024]{1,0:T(8,128)S(1)}, f32[32,1024]{1,0:T(8,128)S(1)}, u32[]{:S(2)}, u32[]{:S(2)}) collective-permute-start(f32[32,1024]{1,0:T(8,128)S(1)} %get-tuple-element.55), channel_id=1, source_target_pairs={{0,64},{8,24},{16,80},{24,8},{32,96},{40,56},{48,112},{56,40},{64,... | collective-permute-start | bytes 393224 | tf_op jit(solution)/shard_map/ppermute | solution.py:233
  93.0 9.5 %collective-permute-start.7 = (f32[32,1024]{1,0:T(8,128)S(1)}, f32[32,1024]{1,0:T(8,128)S(1)}, u32[]{:S(2)}, u32[]{:S(2)}) collective-permute-start(f32[32,1024]{1,0:T(8,128)S(1)} %get-tuple-element.56), channel_id=1, source_target_pairs={{0,128},{8,40},{16,144},{24,56},{32,160},{40,8},{48,176},{56,24},{... | collective-permute-start | bytes 393224 | tf_op jit(solution)/shard_map/ppermute | solution.py:233
  95.4 7.1 %collective-permute-start.8 = (f32[32,1024]{1,0:T(8,128)S(1)}, f32[32,1024]{1,0:T(8,128)S(1)}, u32[]{:S(2)}, u32[]{:S(2)}) collective-permute-start(f32[32,1024]{1,0:T(8,128)S(1)} %get-tuple-element.57), channel_id=1, source_target_pairs={{0,192},{8,56},{16,208},{24,40},{32,224},{40,24},{48,240},{56,8},{... | collective-permute-start | bytes 393224 | tf_op jit(solution)/shard_map/ppermute | solution.py:233
  97.7 5.9 %collective-permute-start.17 = (f32[32,512]{1,0:T(8,128)S(1)}, f32[32,512]{1,0:T(8,128)S(1)}, u32[]{:S(2)}, u32[]{:S(2)}) collective-permute-start(f32[32,512]{1,0:T(8,128)S(1)} %get-tuple-element.72), channel_id=1, source_target_pairs={{0,2},{1,3},{2,0},{3,1},{4,6},{5,7},{6,4},{7,5},{8,10},{9,11},{10,... | collective-permute-start | bytes 196616 | tf_op jit(solution)/shard_map/ppermute | solution.py:236
  101.1 6.2 %collective-permute-start.18 = (f32[32,512]{1,0:T(8,128)S(1)}, f32[32,512]{1,0:T(8,128)S(1)}, u32[]{:S(2)}, u32[]{:S(2)}) collective-permute-start(f32[32,512]{1,0:T(8,128)S(1)} %get-tuple-element.73), channel_id=1, source_target_pairs={{0,3},{1,2},{2,1},{3,0},{4,7},{5,6},{6,5},{7,4},{8,11},{9,10},{10,... | collective-permute-start | bytes 196616 | tf_op jit(solution)/shard_map/ppermute | solution.py:236
  102.5 5.1 %collective-permute-start.9 = (f32[32,512]{1,0:T(8,128)S(1)}, f32[32,512]{1,0:T(8,128)S(1)}, u32[]{:S(2)}, u32[]{:S(2)}) collective-permute-start(f32[32,512]{1,0:T(8,128)S(1)} %get-tuple-element.59), channel_id=1, source_target_pairs={{0,1},{1,0},{2,3},{3,2},{4,5},{5,4},{6,7},{7,6},{8,9},{9,8},{10,11... | collective-permute-start | bytes 196616 | tf_op jit(solution)/shard_map/ppermute | solution.py:236
  107.6 7.9 %collective-permute-start.19 = (f32[32,256]{1,0:T(8,128)S(1)}, f32[32,256]{1,0:T(8,128)S(1)}, u32[]{:S(2)}, u32[]{:S(2)}) collective-permute-start(f32[32,256]{1,0:T(8,128)S(1)} %get-tuple-element.75), channel_id=1, source_target_pairs={{0,4},{1,5},{2,6},{3,7},{4,0},{5,1},{6,2},{7,3},{8,12},{9,13},{10,... | collective-permute-start | bytes 98312 | tf_op jit(solution)/shard_map/ppermute | solution.py:239

commit v6 on v5

--- a/solution.py
+++ b/solution.py
@@ -17,15 +17,6 @@
 MIB = 1024 * 1024
 
 
-def offset(core, half, pos):
-    first, second = (STRIDE[axis] for axis in ORDER[core])
-    off = (pos & 3) * second
-    for k, mask in enumerate(MASKS[half]):
-        if (pos >> (3 - k)) & 1:
-            off ^= mask * first
-    return off
-
-
 def pairs(turn, mask):
     return [(i, i ^ (mask * STRIDE[ORDER[i % 2][turn]])) for i in range(N_RED)]
 
@@ -34,48 +25,98 @@
     return (lax.axis_index("y") * N_X + lax.axis_index("x")) * N_CORE + lax.axis_index("core")
 
 
-def pack_kernel(first_ref, amp_ref, out_ref):
-    tile = out_ref.shape[2]
-    for r in range(N_RED):
-        cols = pl.ds(pl.multiple_of(first_ref[0, r], tile), tile)
-        out_ref[r] = amp_ref[:, cols]
+def pack_kernel(first_ref, amp_ref, *out_refs):
+    part, tile = out_refs[0].shape[1:]
+    for stream in range(2):
+        core = lax.axis_index("core") ^ stream
+        home = where_am_i() ^ stream
+        for far in range(2):
+            for sub in range(2):
+                if stream:
+                    out_ref = out_refs[4 + far].at[pl.ds(8 * sub, 8)]
+                else:
+                    out_ref = out_refs[2 * far + sub]
+                for i in range(8):
+                    bits = (far, i >> 2, (i >> 1) & 1, i & 1)
+                    one = bits[0] * MASKS[sub][0] ^ bits[1] * MASKS[sub][1]
+                    two = bits[2] * MASKS[sub][0] ^ bits[3] * MASKS[sub][1]
+                    offs = [
+                        one * STRIDE[axes[0]] ^ two * STRIDE[axes[1]] for axes in ORDER
+                    ]
+                    target = home ^ jnp.where(core == 0, offs[0], offs[1])
+                    cols = pl.ds(pl.multiple_of(first_ref[0, target], tile), tile)
+                    out_ref[i] = amp_ref[part * sub : part * (sub + 1), cols]
 
 
 def pack(amplitudes, tile_perm, tile):
     rows = amplitudes.shape[0]
     vmem = pl.BlockSpec(memory_space=pltpu.VMEM)
+    shape = jax.ShapeDtypeStruct((8, rows // 2, tile), amplitudes.dtype)
+    both = jax.ShapeDtypeStruct((16, rows // 2, tile), amplitudes.dtype)
     return pl.pallas_call(
         pack_kernel,
-        out_shape=jax.ShapeDtypeStruct((N_RED, rows, tile), amplitudes.dtype),
+        out_shape=[shape] * 4 + [both] * 2,
         in_specs=[pl.BlockSpec(memory_space=pltpu.SMEM), vmem],
-        out_specs=vmem,
-        compiler_params=pltpu.CompilerParams(vmem_limit_bytes=16 * MIB),
+        out_specs=[vmem] * 6,
+        compiler_params=pltpu.CompilerParams(vmem_limit_bytes=24 * MIB),
         cost_estimate=pl.CostEstimate(
             flops=0, bytes_accessed=4 * amplitudes.size, transcendentals=0
         ),
     )(tile_perm * tile, amplitudes)
 
 
-def dot_tiles(other, group, amp_ref, b_ref, lhs):
-    rows = amp_ref.shape[1]
+FORWARD = (
+    ((0, 4, 8), (1, 4, 8)),
+    ((0, 2, 4), (1, 2, 4), (2, 2, 4), (2, 6, 8)),
+    ((0, 1, 2), (1, 1, 2), (2, 1, 2), (2, 5, 6), (3, 1, 2), (3, 3, 4), (3, 5, 6), (3, 7, 8)),
+)
+FINAL = (
+    ((0, 0), (1, 0), (2, 0), (2, 4))
+    + tuple((3, 2 * i) for i in range(4))
+    + tuple((4, i) for i in range(8))
+)
+
+
+def of_sub(ref, sub):
+    return ref.at[pl.ds(8 * sub, 8)] if ref.shape[0] == 16 else ref
+
+
+def forward_kernel(plan, sub, *refs):
+    *held, out_ref = refs
+    at = 0
+    for array, first, last in plan:
+        out_ref[at : at + last - first] = of_sub(held[array], sub)[first:last]
+        at += last - first
+
+
+def block_at(stream, half, sub, pos):
+    one = (pos >> 3) * MASKS[half][0] ^ ((pos >> 2) & 1) * MASKS[half][1]
+    two = pos & 3
+    if stream:
+        one, two = two, one
+    for f in range(16):
+        bits = (f & 1, (f >> 1) & 1, (f >> 2) & 1, f >> 3)
+        here = bits[0] * MASKS[sub][0] ^ bits[1] * MASKS[sub][1]
+        there = bits[2] * MASKS[sub][0] ^ bits[3] * MASKS[sub][1]
+        if (here, there) == (one, two):
+            return FINAL[f]
+
+
+def dot_tiles(stream, group, held, b_ref, lhs):
+    part = held[0].shape[1]
     width = b_ref.shape[1] // N_REP
-    core = lax.axis_index("core") ^ other
-    me = where_am_i() ^ other
     rep = lax.axis_index("rep")
     for half in range(2):
         for pos in range(16):
-            block = me ^ jnp.where(core == 0, offset(0, half, pos), offset(1, half, pos))
-            lhs[pos * rows : (pos + 1) * rows, :] = amp_ref[block]
+            for sub in range(2):
+                array, index = block_at(stream, half, sub, pos)
+                row = (2 * pos + sub) * part
+                lhs[row : row + part, :] = of_sub(held[5 * sub + array], sub)[index]
         for k in range(2):
             source = (2 * group + half + 4 * k) ^ rep
             b = b_ref[:, pl.ds(pl.multiple_of(source * width, width), width)]
             cols = slice(k * width, (k + 1) * width)
             yield half, cols, jnp.dot(lhs[...], b, preferred_element_type=jnp.float32)
-
-
-def away_kernel(group, amp_ref, b_ref, out_ref, lhs):
-    for half, cols, out in dot_tiles(1, group, amp_ref, b_ref, lhs):
-        out_ref[half, :, cols] = out
 
 
 def encode(x, out_ref, cols):
@@ -92,7 +133,7 @@
     out_ref[n : n + 16, cols] = exponent.astype(jnp.int32).astype(jnp.int16)
 
 
-def decode(ref, first, rows):
+def decode(ref, first, rows, cols=slice(None)):
     n = ref.shape[0] - 16
     exponent = ref[n : n + 16].astype(jnp.int32).astype(jnp.float32)
     scale = jnp.exp2(exponent - 15.0)
@@ -103,12 +144,24 @@
     return jnp.concatenate(parts, axis=0)
 
 
-def home_kernel(group, amp_ref, b_ref, arrived_ref, far0, far1, near0, near1, lhs):
+def away_kernel(group, *refs):
+    *held, b_ref, out_ref, lhs = refs
+    for half, cols, out in dot_tiles(1, group, held, b_ref, lhs):
+        encode(out, out_ref.at[half], cols)
+
+
+def home_kernel(group, *refs):
+    *held, b_ref, out_ref, lhs = refs
+    for half, cols, out in dot_tiles(0, group, held, b_ref, lhs):
+        out_ref[half, :, cols] = out
+
+
+def merge_kernel(home, arrived, far0, far1, near0, near1):
     n = near0.shape[0]
-    for half, cols, out in dot_tiles(0, group, amp_ref, b_ref, lhs):
-        out += arrived_ref[half, :, cols]
-        (near0, near1)[half][:, cols] = out[:n]
-        encode(out[n:], (far0, far1)[half], cols)
+    for half, (far, near) in enumerate(((far0, near0), (far1, near1))):
+        other = arrived.at[half]
+        near[...] = home[half, :n] + decode(other, 0, n)
+        encode(home[half, n:] + decode(other, n, n), far, slice(None))
 
 
 def in_vmem(kernel, shapes, *args, scratch=(), limit=24):
@@ -187,34 +240,58 @@
     rows = amplitudes.shape[0]
     tile = integrals.shape[0]
     columns = integrals.shape[1] // N_REP
-    ordered = pack(amplitudes, tile_perm, tile)
-    received = lax.all_to_all(ordered, RED, split_axis=0, concat_axis=0, tiled=True)
     m, quarter = 16 * rows, 2 * columns
 
     def stage(n):
         return [((n + 16, quarter), jnp.int16)] * 2 + [((n, quarter), jnp.float32)] * 2
 
     lhs = [pltpu.VMEM((m, tile), amplitudes.dtype)]
+    block = ((8, rows // 2, tile), amplitudes.dtype)
+    swap = [(0, 1), (1, 0)]
+    packed = pack(amplitudes, tile_perm, tile)
+    packed = list(packed[:4]) + [lax.ppermute(t, "core", swap) for t in (packed[5], packed[4])]
+    held = [[[packed[0]], [packed[1]]], [[packed[5]], [packed[5]]]]
+    sends = [packed[2:4], [None, None]]
+    for step in range(4):
+        turn = step // 2
+        for stream in range(2):
+            for sub in range(2):
+                if step or stream:
+                    plan = FORWARD[step - 1] if step else ((0, 0, 8),)
+                    held_now = held[stream][sub] if step else [packed[4]]
+                    (sends[stream][sub],) = in_vmem(
+                        functools.partial(forward_kernel, plan, sub), [block], *held_now
+                    )
+                got = lax.ppermute(sends[stream][sub], RED, pairs(turn, MASKS[sub][step % 2]))
+                held[stream][sub].append(got)
+    home = [
+        in_vmem(
+            functools.partial(home_kernel, group),
+            [((2, m, quarter), jnp.float32)],
+            *held[0][0],
+            *held[0][1],
+            integrals,
+            scratch=lhs,
+        )[0]
+        for group in range(2)
+    ]
+    held[1][0][4], held[1][1][4], home = lax.optimization_barrier(
+        (held[1][0][4], held[1][1][4], home)
+    )
     arrived = []
     for group in range(2):
         (away,) = in_vmem(
             functools.partial(away_kernel, group),
-            [((2, m, quarter), jnp.float32)],
-            received,
+            [((2, m + 16, quarter), jnp.int16)],
+            *held[1][0],
+            *held[1][1],
             integrals,
             scratch=lhs,
         )
-        arrived.append(lax.ppermute(away, "core", [(0, 1), (1, 0)]))
+        arrived.append(lax.ppermute(away, "core", swap))
     keeps, gots = [], []
     for group in range(2):
-        far0, far1, *near = in_vmem(
-            functools.partial(home_kernel, group),
-            stage(m // 2),
-            received,
-            integrals,
-            arrived[group],
-            scratch=lhs,
-        )
+        far0, far1, *near = in_vmem(merge_kernel, stage(m // 2), home[group], arrived[group])
         keeps.append(near)
         gots.append([lax.ppermute(far, RED, pairs(0, MASKS[h][0])) for h, far in enumerate((far0, far1))])
     keeps[1], occ_energy = lax.optimization_barrier((keeps[1], occ_energy))

time: 117 us -> 111 us (0.949)
  blocking collectives: 57.5 us -> 0 us
  starting transfers between devices: 32.9 us -> 59.1 us
  waiting for transfers between devices: 8.37 us -> 32.1 us
  Pallas kernels: 13.1 us -> 15.1 us
    all_to_all x1 -> x0, blocking collectives: 57.5 us -> none  [body(): lax.all_to_all(ordered, RED, split_axis=0, concat_axis=0, tiled=True)]
    ppermute x2 -> x20, starting transfers between devices: 0.69 us -> 28.1 us  [the longest x16 26.9 us: body(): lax.ppermute(sends[stream][sub], RED, pairs(turn, MASKS[sub][step % 2]))]
    ppermute x2 -> x20, waiting for transfers between devices: 1.2 us -> 22.6 us  [the longest x16 22.6 us: body(): lax.ppermute(sends[stream][sub], RED, pairs(turn, MASKS[sub][step % 2]))]
    ppermute x4, waiting for transfers between devices: 0.7 us -> 3.09 us  [body(): lax.ppermute(far, RED, pairs(0, MASKS[h][0]))]
    pallas_call x11 -> x27, Pallas kernels: 10.7 us -> 12.6 us  [in_vmem(): pl.pallas_call(kernel, out_shape=[jax.ShapeDtypeStruct(*shape) for shape...]
    ppermute x4, starting transfers between devices: 6.23 us -> 4.82 us  [body(): lax.ppermute(far, RED, pairs(0, MASKS[h][1]))]
  transfers between devices with their start and end apart: 20 -> 38, of which waited for: 6 -> 14; matrix products, arithmetic and copies ran while one was open for 0% -> 0% of each run, Pallas kernels for 9% -> 10%
where the time goes in v6:
time: 111 us
  starting transfers between devices  59.1 us (53%)
  waiting for transfers between devices  32.1 us (29%)
  Pallas kernels  15.1 us (14%)
  local copies, waits for them, and re-layouts  2.2 us (2%)
  other arithmetic  1.28 us (1%)
    ppermute x16, starting transfers between devices, body(): lax.ppermute(sends[stream][sub], RED, pairs(turn, MASKS[sub][step % 2]))  26.9 us
    ppermute x16, waiting for transfers between devices, body(): lax.ppermute(sends[stream][sub], RED, pairs(turn, MASKS[sub][step % 2]))  22.6 us
    pallas_call x27, Pallas kernels, in_vmem(): pl.pallas_call(kernel, out_shape=[jax.ShapeDtypeStruct(*shape) for shape...  12.6 us
    ppermute x6, starting transfers between devices, body(): lax.ppermute(send, RED, pairs(1, k + 1))  9.56 us
    ppermute x3, starting transfers between devices, body(): lax.ppermute(blocks[k], 'rep', [(i, i ^ k) for i in range(N_REP)])  5.97 us
    ppermute x1, starting transfers between devices, body(): got = lax.ppermute(send, 'rep', [(i, i ^ 4) for i in range(N_REP)])  5.78 us
    ppermute x4, starting transfers between devices, body(): lax.ppermute(far, RED, pairs(0, MASKS[h][0]))  4.83 us
    ppermute x4, starting transfers between devices, body(): lax.ppermute(far, RED, pairs(0, MASKS[h][1]))  4.82 us
  transfers between devices with their start and end apart: 38, of which 14 were waited for; matrix products, arithmetic and copies ran while one was open for 0% of the time, Pallas kernels for 10%

profile of v6, /device:TPU:2, one launch (start us, length us, event | category | flops | bytes accessed | tf_op | source)
XLA Modules:
  0.0 110.6 jit_solution(474440355573309797)
XLA Ops:
  0.0 0.7 broadcast_multiply_fusion.first_ref
  0.7 2.2 %copy-done = bf16[32,65536]{1,0:T(8,128)(2,1)S(1)} copy-done((bf16[32,65536]{1,0:T(8,128)(2,1)S(1)}, bf16[32,65536]{1,0:T(8,128)(2,1)}, u32[]{:S(2)}) %copy-start) | copy-done | bytes 4194328
  2.8 0.8 shard_map.82
  4.3 1.5 %collective-permute-start.14 = (bf16[8,16,2048]{2,1,0:T(8,128)(2,1)S(1)}, bf16[8,16,2048]{2,1,0:T(8,128)(2,1)S(1)}, u32[]{:S(2)}, u32[]{:S(2)}) collective-permute-start(bf16[8,16,2048]{2,1,0:T(8,128)(2,1)S(1)} %get-tuple-element.56), channel_id=1, source_target_pairs={{0,48},{8,200},{16,32},{24,216},{32,16},{40,232},{48,0},{56,248},{... | collective-permute-start | bytes 1572872 | tf_op jit(solution)/shard_map/ppermute | solution.py:265
  5.8 1.8 %collective-permute-start.10 = (bf16[8,16,2048]{2,1,0:T(8,128)(2,1)S(1)}, bf16[8,16,2048]{2,1,0:T(8,128)(2,1)S(1)}, u32[]{:S(2)}, u32[]{:S(2)}) collective-permute-start(bf16[8,16,2048]{2,1,0:T(8,128)(2,1)S(1)} %get-tuple-element.54), channel_id=1, source_target_pairs={{0,16},{8,72},{16,0},{24,88},{32,48},{40,104},{48,32},{56,120},{64... | collective-permute-start | bytes 1572872 | tf_op jit(solution)/shard_map/ppermute | solution.py:265
  7.6 1.7 %collective-permute-start.6 = (bf16[8,16,2048]{2,1,0:T(8,128)(2,1)S(1)}, bf16[8,16,2048]{2,1,0:T(8,128)(2,1)S(1)}, u32[]{:S(2)}, u32[]{:S(2)}) collective-permute-start(bf16[8,16,2048]{2,1,0:T(8,128)(2,1)S(1)} %shard_map.87), channel_id=1, source_target_pairs={{0,48},{8,200},{16,32},{24,216},{32,16},{40,232},{48,0},{56,248},{... | collective-permute-start | bytes 1572872 | tf_op jit(solution)/shard_map/ppermute | solution.py:265
  9.4 0.7 collective-permute-start.2
  10.0 3.4 %collective-permute-done.14.refs_1_.refs_6_ = bf16[8,16,2048]{2,1,0:T(8,128)(2,1)S(1)} collective-permute-done((bf16[8,16,2048]{2,1,0:T(8,128)(2,1)S(1)}, bf16[8,16,2048]{2,1,0:T(8,128)(2,1)S(1)}, u32[]{:S(2)}, u32[]{:S(2)}) %collective-permute-start.14) | collective-permute-done | bytes 524320 | tf_op jit(solution)/shard_map/ppermute | solution.py:265
  13.5 3.6 %collective-permute-start.15 = (bf16[8,16,2048]{2,1,0:T(8,128)(2,1)S(1)}, bf16[8,16,2048]{2,1,0:T(8,128)(2,1)S(1)}, u32[]{:S(2)}, u32[]{:S(2)}) collective-permute-start(bf16[8,16,2048]{2,1,0:T(8,128)(2,1)S(1)} %shard_map.94), channel_id=1, source_target_pairs={{0,16},{8,72},{16,0},{24,88},{32,48},{40,104},{48,32},{56,120},{64... | collective-permute-start | bytes 1572872 | tf_op jit(solution)/shard_map/ppermute | solution.py:265
  17.6 1.5 %collective-permute-done.6.refs_1_.refs_6_ = bf16[8,16,2048]{2,1,0:T(8,128)(2,1)S(1)} collective-permute-done((bf16[8,16,2048]{2,1,0:T(8,128)(2,1)S(1)}, bf16[8,16,2048]{2,1,0:T(8,128)(2,1)S(1)}, u32[]{:S(2)}, u32[]{:S(2)}) %collective-permute-start.6) | collective-permute-done | bytes 524320 | tf_op jit(solution)/shard_map/ppermute | solution.py:265
  19.1 3.6 %collective-permute-start.7 = (bf16[8,16,2048]{2,1,0:T(8,128)(2,1)S(1)}, bf16[8,16,2048]{2,1,0:T(8,128)(2,1)S(1)}, u32[]{:S(2)}, u32[]{:S(2)}) collective-permute-start(bf16[8,16,2048]{2,1,0:T(8,128)(2,1)S(1)} %shard_map.88), channel_id=1, source_target_pairs={{0,16},{8,72},{16,0},{24,88},{32,48},{40,104},{48,32},{56,120},{64... | collective-permute-start | bytes 1572872 | tf_op jit(solution)/shard_map/ppermute | solution.py:265
  23.2 3.0 %collective-permute-done.15.refs_2_.refs_7_ = bf16[8,16,2048]{2,1,0:T(8,128)(2,1)S(1)} collective-permute-done((bf16[8,16,2048]{2,1,0:T(8,128)(2,1)S(1)}, bf16[8,16,2048]{2,1,0:T(8,128)(2,1)S(1)}, u32[]{:S(2)}, u32[]{:S(2)}) %collective-permute-start.15) | collective-permute-done | bytes 524320 | tf_op jit(solution)/shard_map/ppermute | solution.py:265
  26.2 3.1 %collective-permute-start.16 = (bf16[8,16,2048]{2,1,0:T(8,128)(2,1)S(1)}, bf16[8,16,2048]{2,1,0:T(8,128)(2,1)S(1)}, u32[]{:S(2)}, u32[]{:S(2)}) collective-permute-start(bf16[8,16,2048]{2,1,0:T(8,128)(2,1)S(1)} %shard_map.95), channel_id=1, source_target_pairs={{0,192},{8,56},{16,208},{24,40},{32,224},{40,24},{48,240},{56,8},{... | collective-permute-start | bytes 1572872 | tf_op jit(solution)/shard_map/ppermute | solution.py:265
  29.6 3.1 %collective-permute-done.7.refs_2_.refs_7_ = bf16[8,16,2048]{2,1,0:T(8,128)(2,1)S(1)} collective-permute-done((bf16[8,16,2048]{2,1,0:T(8,128)(2,1)S(1)}, bf16[8,16,2048]{2,1,0:T(8,128)(2,1)S(1)}, u32[]{:S(2)}, u32[]{:S(2)}) %collective-permute-start.7) | collective-permute-done | bytes 524320 | tf_op jit(solution)/shard_map/ppermute | solution.py:265
  32.8 5.8 %collective-permute-start.8 = (bf16[8,16,2048]{2,1,0:T(8,128)(2,1)S(1)}, bf16[8,16,2048]{2,1,0:T(8,128)(2,1)S(1)}, u32[]{:S(2)}, u32[]{:S(2)}) collective-permute-start(bf16[8,16,2048]{2,1,0:T(8,128)(2,1)S(1)} %shard_map.89), channel_id=1, source_target_pairs={{0,192},{8,56},{16,208},{24,40},{32,224},{40,24},{48,240},{56,8},{... | collective-permute-start | bytes 1572872 | tf_op jit(solution)/shard_map/ppermute | solution.py:265
  38.8 2.1 %collective-permute-start.17 = (bf16[8,16,2048]{2,1,0:T(8,128)(2,1)S(1)}, bf16[8,16,2048]{2,1,0:T(8,128)(2,1)S(1)}, u32[]{:S(2)}, u32[]{:S(2)}) collective-permute-start(bf16[8,16,2048]{2,1,0:T(8,128)(2,1)S(1)} %shard_map.96), channel_id=1, source_target_pairs={{0,64},{8,24},{16,80},{24,8},{32,96},{40,56},{48,112},{56,40},{64,... | collective-permute-start | bytes 1572872 | tf_op jit(solution)/shard_map/ppermute | solution.py:265
  41.1 4.7 %collective-permute-done.8.refs_3_.refs_8_ = bf16[8,16,2048]{2,1,0:T(8,128)(2,1)S(1)} collective-permute-done((bf16[8,16,2048]{2,1,0:T(8,128)(2,1)S(1)}, bf16[8,16,2048]{2,1,0:T(8,128)(2,1)S(1)}, u32[]{:S(2)}, u32[]{:S(2)}) %collective-permute-start.8) | collective-permute-done | bytes 524320 | tf_op jit(solution)/shard_map/ppermute | solution.py:265
  45.9 2.0 %collective-permute-done.4.refs_3_ = bf16[8,16,2048]{2,1,0:T(8,128)(2,1)S(1)} collective-permute-done((bf16[8,16,2048]{2,1,0:T(8,128)(2,1)S(1)}, bf16[8,16,2048]{2,1,0:T(8,128)(2,1)S(1)}, u32[]{:S(2)}, u32[]{:S(2)}) %collective-permute-start.4) | collective-permute-done | bytes 524320 | tf_op jit(solution)/shard_map/ppermute | solution.py:265
  48.0 1.5 %collective-permute-start.5 = (bf16[8,16,2048]{2,1,0:T(8,128)(2,1)S(1)}, bf16[8,16,2048]{2,1,0:T(8,128)(2,1)S(1)}, u32[]{:S(2)}, u32[]{:S(2)}) collective-permute-start(bf16[8,16,2048]{2,1,0:T(8,128)(2,1)S(1)} %shard_map.86), channel_id=1, source_target_pairs={{0,192},{8,56},{16,208},{24,40},{32,224},{40,24},{48,240},{56,8},{... | collective-permute-start | bytes 1572872 | tf_op jit(solution)/shard_map/ppermute | solution.py:265
  49.5 4.1 %collective-permute-done.17.refs_9_ = bf16[8,16,2048]{2,1,0:T(8,128)(2,1)S(1)} collective-permute-done((bf16[8,16,2048]{2,1,0:T(8,128)(2,1)S(1)}, bf16[8,16,2048]{2,1,0:T(8,128)(2,1)S(1)}, u32[]{:S(2)}, u32[]{:S(2)}) %collective-permute-start.17) | collective-permute-done | bytes 524320 | tf_op jit(solution)/shard_map/ppermute | solution.py:265
  53.6 2.4 %shard_map.98.home = f32[2,512,512]{2,1,0:T(8,128)S(1)} custom-call(bf16[8,16,2048]{2,1,0:T(8,128)(2,1)S(1)} %get-tuple-element.53.refs_0_, bf16[8,16,2048]{2,1,0:T(8,128)(2,1)S(1)} %collective-permute-done.10.refs_1_, bf16[8,16,2048]{2,1,0:T(8,128)(2,1)S(1)} %collective-permute-done.11.refs_2_, bf16[8,16,2048]{2,1,0:T(8,128)(2,1)S(1)} %collective-permute-done.12.refs_3_, ...), custom_call_target="tpu_custom_call" | custom-call | tf_op jit(solution)/shard_map/pallas_call | solution.py:169
  56.0 2.4 %shard_map.97.home = f32[2,512,512]{2,1,0:T(8,128)S(1)} custom-call(bf16[8,16,2048]{2,1,0:T(8,128)(2,1)S(1)} %get-tuple-element.53.refs_0_, bf16[8,16,2048]{2,1,0:T(8,128)(2,1)S(1)} %collective-permute-done.10.refs_1_, bf16[8,16,2048]{2,1,0:T(8,128)(2,1)S(1)} %collective-permute-done.11.refs_2_, bf16[8,16,2048]{2,1,0:T(8,128)(2,1)S(1)} %collective-permute-done.12.refs_3_, ...), custom_call_target="tpu_custom_call" | custom-call | tf_op jit(solution)/shard_map/pallas_call | solution.py:169
  58.3 0.8 collective-permute-done.9.refs_9_
  59.2 2.7 %shard_map.101 = s16[2,528,512]{2,1,0:T(8,128)(2,1)S(1)} custom-call(bf16[16,16,2048]{2,1,0:T(8,128)(2,1)S(1)} %collective-permute-done.refs_0_.refs_5_, bf16[8,16,2048]{2,1,0:T(8,128)(2,1)S(1)} %collective-permute-done.2.refs_1_, bf16[8,16,2048]{2,1,0:T(8,128)(2,1)S(1)} %collective-permute-done.3.refs_2_, ...), custom_call_target="tpu_custom_call" | custom-call | tf_op jit(solution)/shard_map/pallas_call | solution.py:169
  62.0 2.7 %shard_map.99 = s16[2,528,512]{2,1,0:T(8,128)(2,1)S(1)} custom-call(bf16[16,16,2048]{2,1,0:T(8,128)(2,1)S(1)} %collective-permute-done.refs_0_.refs_5_, bf16[8,16,2048]{2,1,0:T(8,128)(2,1)S(1)} %collective-permute-done.2.refs_1_, bf16[8,16,2048]{2,1,0:T(8,128)(2,1)S(1)} %collective-permute-done.3.refs_2_, ...), custom_call_target="tpu_custom_call" | custom-call | tf_op jit(solution)/shard_map/pallas_call | solution.py:169
  65.3 0.6 shard_map.102
  65.8 2.0 %collective-permute-start.28 = (s16[272,512]{1,0:T(8,128)(2,1)S(1)}, s16[272,512]{1,0:T(8,128)(2,1)S(1)}, u32[]{:S(2)}, u32[]{:S(2)}) collective-permute-start(s16[272,512]{1,0:T(8,128)(2,1)S(1)} %get-tuple-element.82), channel_id=1, source_target_pairs={{0,16},{8,72},{16,0},{24,88},{32,48},{40,104},{48,32},{56,120},{64... | collective-permute-start | bytes 835592 | tf_op jit(solution)/shard_map/ppermute | solution.py:296
  67.8 0.6 shard_map.100
  68.4 1.7 %collective-permute-start.19 = (s16[272,512]{1,0:T(8,128)(2,1)S(1)}, s16[272,512]{1,0:T(8,128)(2,1)S(1)}, u32[]{:S(2)}, u32[]{:S(2)}) collective-permute-start(s16[272,512]{1,0:T(8,128)(2,1)S(1)} %get-tuple-element.62), channel_id=1, source_target_pairs={{0,16},{8,72},{16,0},{24,88},{32,48},{40,104},{48,32},{56,120},{64... | collective-permute-start | bytes 835592 | tf_op jit(solution)/shard_map/ppermute | solution.py:296
  70.1 1.1 %collective-permute-start.20 = (s16[272,512]{1,0:T(8,128)(2,1)S(1)}, s16[272,512]{1,0:T(8,128)(2,1)S(1)}, u32[]{:S(2)}, u32[]{:S(2)}) collective-permute-start(s16[272,512]{1,0:T(8,128)(2,1)S(1)} %get-tuple-element.63), channel_id=1, source_target_pairs={{0,48},{8,200},{16,32},{24,216},{32,16},{40,232},{48,0},{56,248},{... | collective-permute-start | bytes 835592 | tf_op jit(solution)/shard_map/ppermute | solution.py:296
  71.3 1.2 %collective-permute-done.28.got0 = s16[272,512]{1,0:T(8,128)(2,1)S(1)} collective-permute-done((s16[272,512]{1,0:T(8,128)(2,1)S(1)}, s16[272,512]{1,0:T(8,128)(2,1)S(1)}, u32[]{:S(2)}, u32[]{:S(2)}) %collective-permute-start.28) | collective-permute-done | bytes 278560 | tf_op jit(solution)/shard_map/ppermute | solution.py:296
  72.5 1.9 %collective-permute-done.29.got1 = s16[272,512]{1,0:T(8,128)(2,1)S(1)} collective-permute-done((s16[272,512]{1,0:T(8,128)(2,1)S(1)}, s16[272,512]{1,0:T(8,128)(2,1)S(1)}, u32[]{:S(2)}, u32[]{:S(2)}) %collective-permute-start.29) | collective-permute-done | bytes 278560 | tf_op jit(solution)/shard_map/ppermute | solution.py:296
  74.7 1.7 %collective-permute-start.31 = (s16[144,512]{1,0:T(8,128)(2,1)S(1)}, s16[144,512]{1,0:T(8,128)(2,1)S(1)}, u32[]{:S(2)}, u32[]{:S(2)}) collective-permute-start(s16[144,512]{1,0:T(8,128)(2,1)S(1)} %get-tuple-element.87), channel_id=1, source_target_pairs={{0,16},{8,72},{16,0},{24,88},{32,48},{40,104},{48,32},{56,120},{64... | collective-permute-start | bytes 442376 | tf_op jit(solution)/shard_map/ppermute | solution.py:306
  77.1 1.6 %shard_map.103 = f32[32,256]{1,0:T(8,128)} custom-call(s32[4,2,16]{2,1,0:T(2,128)} %occ_index.1, f32[125]{0:T(128)} %occ_energy, s32[8]{0:T(128)} %block_sizes.1, s32[1]{0:T(128)S(6)} %copy.9.slab_irrep, f32[2048]{0:T(1024)} %virt_energy.1), custom_call_target="tpu_custom_call" | custom-call | tf_op jit(solution)/shard_map/pallas_call | solution.py:228
  79.0 2.4 %collective-permute-start.22 = (s16[144,512]{1,0:T(8,128)(2,1)S(1)}, s16[144,512]{1,0:T(8,128)(2,1)S(1)}, u32[]{:S(2)}, u32[]{:S(2)}) collective-permute-start(s16[144,512]{1,0:T(8,128)(2,1)S(1)} %get-tuple-element.72), channel_id=1, source_target_pairs={{0,48},{8,200},{16,32},{24,216},{32,16},{40,232},{48,0},{56,248},{... | collective-permute-start | bytes 442376 | tf_op jit(solution)/shard_map/ppermute | solution.py:306
  81.4 0.7 collective-permute-start.23
  82.2 2.5 %collective-permute-start.33 = (f32[32,1024]{1,0:T(8,128)S(1)}, f32[32,1024]{1,0:T(8,128)S(1)}, u32[]{:S(2)}, u32[]{:S(2)}) collective-permute-start(f32[32,1024]{1,0:T(8,128)S(1)} %get-tuple-element.90), channel_id=1, source_target_pairs={{0,128},{8,40},{16,144},{24,56},{32,160},{40,8},{48,176},{56,24},{... | collective-permute-start | bytes 393224 | tf_op jit(solution)/shard_map/ppermute | solution.py:310
  84.7 2.2 %collective-permute-start.34 = (f32[32,1024]{1,0:T(8,128)S(1)}, f32[32,1024]{1,0:T(8,128)S(1)}, u32[]{:S(2)}, u32[]{:S(2)}) collective-permute-start(f32[32,1024]{1,0:T(8,128)S(1)} %get-tuple-element.91), channel_id=1, source_target_pairs={{0,192},{8,56},{16,208},{24,40},{32,224},{40,24},{48,240},{56,8},{... | collective-permute-start | bytes 393224 | tf_op jit(solution)/shard_map/ppermute | solution.py:310
  87.3 0.9 collective-permute-start.24
  88.2 1.8 %collective-permute-start.25 = (f32[32,1024]{1,0:T(8,128)S(1)}, f32[32,1024]{1,0:T(8,128)S(1)}, u32[]{:S(2)}, u32[]{:S(2)}) collective-permute-start(f32[32,1024]{1,0:T(8,128)S(1)} %get-tuple-element.76), channel_id=1, source_target_pairs={{0,128},{8,40},{16,144},{24,56},{32,160},{40,8},{48,176},{56,24},{... | collective-permute-start | bytes 393224 | tf_op jit(solution)/shard_map/ppermute | solution.py:310
  89.9 2.1 %collective-permute-start.26 = (f32[32,1024]{1,0:T(8,128)S(1)}, f32[32,1024]{1,0:T(8,128)S(1)}, u32[]{:S(2)}, u32[]{:S(2)}) collective-permute-start(f32[32,1024]{1,0:T(8,128)S(1)} %get-tuple-element.77), channel_id=1, source_target_pairs={{0,192},{8,56},{16,208},{24,40},{32,224},{40,24},{48,240},{56,8},{... | collective-permute-start | bytes 393224 | tf_op jit(solution)/shard_map/ppermute | solution.py:310
  92.1 3.3 %collective-permute-start.35 = (f32[32,512]{1,0:T(8,128)S(1)}, f32[32,512]{1,0:T(8,128)S(1)}, u32[]{:S(2)}, u32[]{:S(2)}) collective-permute-start(f32[32,512]{1,0:T(8,128)S(1)} %get-tuple-element.92), channel_id=1, source_target_pairs={{0,2},{1,3},{2,0},{3,1},{4,6},{5,7},{6,4},{7,5},{8,10},{9,11},{10,... | collective-permute-start | bytes 196616 | tf_op jit(solution)/shard_map/ppermute | solution.py:313
  95.5 1.4 %collective-permute-start.36 = (f32[32,512]{1,0:T(8,128)S(1)}, f32[32,512]{1,0:T(8,128)S(1)}, u32[]{:S(2)}, u32[]{:S(2)}) collective-permute-start(f32[32,512]{1,0:T(8,128)S(1)} %get-tuple-element.93), channel_id=1, source_target_pairs={{0,3},{1,2},{2,1},{3,0},{4,7},{5,6},{6,5},{7,4},{8,11},{9,10},{10,... | collective-permute-start | bytes 196616 | tf_op jit(solution)/shard_map/ppermute | solution.py:313
  96.9 1.2 %collective-permute-start.27 = (f32[32,512]{1,0:T(8,128)S(1)}, f32[32,512]{1,0:T(8,128)S(1)}, u32[]{:S(2)}, u32[]{:S(2)}) collective-permute-start(f32[32,512]{1,0:T(8,128)S(1)} %get-tuple-element.79), channel_id=1, source_target_pairs={{0,1},{1,0},{2,3},{3,2},{4,5},{5,4},{6,7},{7,6},{8,9},{9,8},{10,11... | collective-permute-start | bytes 196616 | tf_op jit(solution)/shard_map/ppermute | solution.py:313
  98.1 3.5 %collective-permute-done.36.d = f32[32,512]{1,0:T(8,128)S(1)} collective-permute-done((f32[32,512]{1,0:T(8,128)S(1)}, f32[32,512]{1,0:T(8,128)S(1)}, u32[]{:S(2)}, u32[]{:S(2)}) %collective-permute-start.36) | collective-permute-done | bytes 65568 | tf_op jit(solution)/shard_map/ppermute | solution.py:313
  102.0 5.8 %collective-permute-start.37 = (f32[32,256]{1,0:T(8,128)S(1)}, f32[32,256]{1,0:T(8,128)S(1)}, u32[]{:S(2)}, u32[]{:S(2)}) collective-permute-start(f32[32,256]{1,0:T(8,128)S(1)} %get-tuple-element.95), channel_id=1, source_target_pairs={{0,4},{1,5},{2,6},{3,7},{4,0},{5,1},{6,2},{7,3},{8,12},{9,13},{10,... | collective-permute-start | bytes 98312 | tf_op jit(solution)/shard_map/ppermute | solution.py:316
  107.8 2.2 %collective-permute-done.37 = f32[32,256]{1,0:T(8,128)S(1)} collective-permute-done((f32[32,256]{1,0:T(8,128)S(1)}, f32[32,256]{1,0:T(8,128)S(1)}, u32[]{:S(2)}, u32[]{:S(2)}) %collective-permute-start.37) | collective-permute-done | bytes 32800 | tf_op jit(solution)/shard_map/ppermute | solution.py:316
  110.0 0.6 add_divide_fusion
  (68 shorter events, 5.0 us)
Async XLA Ops:
  0.7 2.2 %copy-start = (bf16[32,65536]{1,0:T(8,128)(2,1)S(1)}, bf16[32,65536]{1,0:T(8,128)(2,1)}, u32[]{:S(2)}) copy-start(bf16[32,65536]{1,0:T(8,128)(2,1)} %amp_ref.1) | copy-start | bytes 12582916
  3.7 3.9 %collective-permute-start.1 = (bf16[16,16,2048]{2,1,0:T(8,128)(2,1)S(1)}, bf16[16,16,2048]{2,1,0:T(8,128)(2,1)S(1)}, u32[]{:S(2)}, u32[]{:S(2)}) collective-permute-start(bf16[16,16,2048]{2,1,0:T(8,128)(2,1)S(1)} %get-tuple-element.52), channel_id=1, source_target_pairs={{0,8},{8,0},{1,9},{9,1},{2,10},{10,2},{3,11},{11,3},{4,12},{12,4},... | collective-permute-start | bytes 3145736 | tf_op jit(solution)/shard_map/ppermute | solution.py:252
  3.8 13.8 %collective-permute-start = (bf16[16,16,2048]{2,1,0:T(8,128)(2,1)S(1)}, bf16[16,16,2048]{2,1,0:T(8,128)(2,1)S(1)}, u32[]{:S(2)}, u32[]{:S(2)}) collective-permute-start(bf16[16,16,2048]{2,1,0:T(8,128)(2,1)S(1)} %get-tuple-element.51), channel_id=1, source_target_pairs={{0,8},{8,0},{1,9},{9,1},{2,10},{10,2},{3,11},{11,3},{4,12},{12,4},... | collective-permute-start | bytes 3145736 | tf_op jit(solution)/shard_map/ppermute | solution.py:252
  4.3 9.2 %collective-permute-start.14 = (bf16[8,16,2048]{2,1,0:T(8,128)(2,1)S(1)}, bf16[8,16,2048]{2,1,0:T(8,128)(2,1)S(1)}, u32[]{:S(2)}, u32[]{:S(2)}) collective-permute-start(bf16[8,16,2048]{2,1,0:T(8,128)(2,1)S(1)} %get-tuple-element.56), channel_id=1, source_target_pairs={{0,48},{8,200},{16,32},{24,216},{32,16},{40,232},{48,0},{56,248},{... | collective-permute-start | bytes 1572872 | tf_op jit(solution)/shard_map/ppermute | solution.py:265
  5.8 11.3 %collective-permute-start.10 = (bf16[8,16,2048]{2,1,0:T(8,128)(2,1)S(1)}, bf16[8,16,2048]{2,1,0:T(8,128)(2,1)S(1)}, u32[]{:S(2)}, u32[]{:S(2)}) collective-permute-start(bf16[8,16,2048]{2,1,0:T(8,128)(2,1)S(1)} %get-tuple-element.54), channel_id=1, source_target_pairs={{0,16},{8,72},{16,0},{24,88},{32,48},{40,104},{48,32},{56,120},{64... | collective-permute-start | bytes 1572872 | tf_op jit(solution)/shard_map/ppermute | solution.py:265
  7.6 11.5 %collective-permute-start.6 = (bf16[8,16,2048]{2,1,0:T(8,128)(2,1)S(1)}, bf16[8,16,2048]{2,1,0:T(8,128)(2,1)S(1)}, u32[]{:S(2)}, u32[]{:S(2)}) collective-permute-start(bf16[8,16,2048]{2,1,0:T(8,128)(2,1)S(1)} %shard_map.87), channel_id=1, source_target_pairs={{0,48},{8,200},{16,32},{24,216},{32,16},{40,232},{48,0},{56,248},{... | collective-permute-start | bytes 1572872 | tf_op jit(solution)/shard_map/ppermute | solution.py:265
  9.4 13.3 %collective-permute-start.2 = (bf16[8,16,2048]{2,1,0:T(8,128)(2,1)S(1)}, bf16[8,16,2048]{2,1,0:T(8,128)(2,1)S(1)}, u32[]{:S(2)}, u32[]{:S(2)}) collective-permute-start(bf16[8,16,2048]{2,1,0:T(8,128)(2,1)S(1)} %shard_map.83), channel_id=1, source_target_pairs={{0,16},{8,72},{16,0},{24,88},{32,48},{40,104},{48,32},{56,120},{64... | collective-permute-start | bytes 1572872 | tf_op jit(solution)/shard_map/ppermute | solution.py:265
  13.5 12.7 %collective-permute-start.15 = (bf16[8,16,2048]{2,1,0:T(8,128)(2,1)S(1)}, bf16[8,16,2048]{2,1,0:T(8,128)(2,1)S(1)}, u32[]{:S(2)}, u32[]{:S(2)}) collective-permute-start(bf16[8,16,2048]{2,1,0:T(8,128)(2,1)S(1)} %shard_map.94), channel_id=1, source_target_pairs={{0,16},{8,72},{16,0},{24,88},{32,48},{40,104},{48,32},{56,120},{64... | collective-permute-start | bytes 1572872 | tf_op jit(solution)/shard_map/ppermute | solution.py:265
  17.1 12.2 %collective-permute-start.11 = (bf16[8,16,2048]{2,1,0:T(8,128)(2,1)S(1)}, bf16[8,16,2048]{2,1,0:T(8,128)(2,1)S(1)}, u32[]{:S(2)}, u32[]{:S(2)}) collective-permute-start(bf16[8,16,2048]{2,1,0:T(8,128)(2,1)S(1)} %shard_map.91), channel_id=1, source_target_pairs={{0,48},{8,200},{16,32},{24,216},{32,16},{40,232},{48,0},{56,248},{... | collective-permute-start | bytes 1572872 | tf_op jit(solution)/shard_map/ppermute | solution.py:265
  19.1 13.6 %collective-permute-start.7 = (bf16[8,16,2048]{2,1,0:T(8,128)(2,1)S(1)}, bf16[8,16,2048]{2,1,0:T(8,128)(2,1)S(1)}, u32[]{:S(2)}, u32[]{:S(2)}) collective-permute-start(bf16[8,16,2048]{2,1,0:T(8,128)(2,1)S(1)} %shard_map.88), channel_id=1, source_target_pairs={{0,16},{8,72},{16,0},{24,88},{32,48},{40,104},{48,32},{56,120},{64... | collective-permute-start | bytes 1572872 | tf_op jit(solution)/shard_map/ppermute | solution.py:265
  22.7 15.9 %collective-permute-start.3 = (bf16[8,16,2048]{2,1,0:T(8,128)(2,1)S(1)}, bf16[8,16,2048]{2,1,0:T(8,128)(2,1)S(1)}, u32[]{:S(2)}, u32[]{:S(2)}) collective-permute-start(bf16[8,16,2048]{2,1,0:T(8,128)(2,1)S(1)} %shard_map.84), channel_id=1, source_target_pairs={{0,48},{8,200},{16,32},{24,216},{32,16},{40,232},{48,0},{56,248},{... | collective-permute-start | bytes 1572872 | tf_op jit(solution)/shard_map/ppermute | solution.py:265
  26.2 12.5 %collective-permute-start.16 = (bf16[8,16,2048]{2,1,0:T(8,128)(2,1)S(1)}, bf16[8,16,2048]{2,1,0:T(8,128)(2,1)S(1)}, u32[]{:S(2)}, u32[]{:S(2)}) collective-permute-start(bf16[8,16,2048]{2,1,0:T(8,128)(2,1)S(1)} %shard_map.95), channel_id=1, source_target_pairs={{0,192},{8,56},{16,208},{24,40},{32,224},{40,24},{48,240},{56,8},{... | collective-permute-start | bytes 1572872 | tf_op jit(solution)/shard_map/ppermute | solution.py:265
  29.4 11.5 %collective-permute-start.12 = (bf16[8,16,2048]{2,1,0:T(8,128)(2,1)S(1)}, bf16[8,16,2048]{2,1,0:T(8,128)(2,1)S(1)}, u32[]{:S(2)}, u32[]{:S(2)}) collective-permute-start(bf16[8,16,2048]{2,1,0:T(8,128)(2,1)S(1)} %shard_map.92), channel_id=1, source_target_pairs={{0,64},{8,24},{16,80},{24,8},{32,96},{40,56},{48,112},{56,40},{64,... | collective-permute-start | bytes 1572872 | tf_op jit(solution)/shard_map/ppermute | solution.py:265
  32.7 20.8 %slice-start = ((s8[8388608]{0:T(1024)(128)(4,1)}), s8[4194304]{0:T(1024)(128)(4,1)S(1)}, s32[]{:S(2)}) async-start(s8[8388608]{0:T(1024)(128)(4,1)} %bitcast), calls=%async_computation | async-start | bytes 8388608
  32.8 13.0 %collective-permute-start.8 = (bf16[8,16,2048]{2,1,0:T(8,128)(2,1)S(1)}, bf16[8,16,2048]{2,1,0:T(8,128)(2,1)S(1)}, u32[]{:S(2)}, u32[]{:S(2)}) collective-permute-start(bf16[8,16,2048]{2,1,0:T(8,128)(2,1)S(1)} %shard_map.89), channel_id=1, source_target_pairs={{0,192},{8,56},{16,208},{24,40},{32,224},{40,24},{48,240},{56,8},{... | collective-permute-start | bytes 1572872 | tf_op jit(solution)/shard_map/ppermute | solution.py:265
  38.7 9.3 %collective-permute-start.4 = (bf16[8,16,2048]{2,1,0:T(8,128)(2,1)S(1)}, bf16[8,16,2048]{2,1,0:T(8,128)(2,1)S(1)}, u32[]{:S(2)}, u32[]{:S(2)}) collective-permute-start(bf16[8,16,2048]{2,1,0:T(8,128)(2,1)S(1)} %shard_map.85), channel_id=1, source_target_pairs={{0,64},{8,24},{16,80},{24,8},{32,96},{40,56},{48,112},{56,40},{64,... | collective-permute-start | bytes 1572872 | tf_op jit(solution)/shard_map/ppermute | solution.py:265
  38.8 14.7 %slice-start.1 = ((s8[8388608]{0:T(1024)(128)(4,1)}), s8[4194304]{0:T(1024)(128)(4,1)S(1)}, s32[]{:S(2)}) async-start(s8[8388608]{0:T(1024)(128)(4,1)} %bitcast), calls=%async_computation.1 | async-start | bytes 8388608
  38.8 14.7 %collective-permute-start.17 = (bf16[8,16,2048]{2,1,0:T(8,128)(2,1)S(1)}, bf16[8,16,2048]{2,1,0:T(8,128)(2,1)S(1)}, u32[]{:S(2)}, u32[]{:S(2)}) collective-permute-start(bf16[8,16,2048]{2,1,0:T(8,128)(2,1)S(1)} %shard_map.96), channel_id=1, source_target_pairs={{0,64},{8,24},{16,80},{24,8},{32,96},{40,56},{48,112},{56,40},{64,... | collective-permute-start | bytes 1572872 | tf_op jit(solution)/shard_map/ppermute | solution.py:265
  41.0 12.6 %collective-permute-start.13 = (bf16[8,16,2048]{2,1,0:T(8,128)(2,1)S(1)}, bf16[8,16,2048]{2,1,0:T(8,128)(2,1)S(1)}, u32[]{:S(2)}, u32[]{:S(2)}) collective-permute-start(bf16[8,16,2048]{2,1,0:T(8,128)(2,1)S(1)} %shard_map.93), channel_id=1, source_target_pairs={{0,192},{8,56},{16,208},{24,40},{32,224},{40,24},{48,240},{56,8},{... | collective-permute-start | bytes 1572872 | tf_op jit(solution)/shard_map/ppermute | solution.py:265
  45.8 13.3 %collective-permute-start.9 = (bf16[8,16,2048]{2,1,0:T(8,128)(2,1)S(1)}, bf16[8,16,2048]{2,1,0:T(8,128)(2,1)S(1)}, u32[]{:S(2)}, u32[]{:S(2)}) collective-permute-start(bf16[8,16,2048]{2,1,0:T(8,128)(2,1)S(1)} %shard_map.90), channel_id=1, source_target_pairs={{0,64},{8,24},{16,80},{24,8},{32,96},{40,56},{48,112},{56,40},{64,... | collective-permute-start | bytes 1572872 | tf_op jit(solution)/shard_map/ppermute | solution.py:265
  48.0 11.2 %collective-permute-start.5 = (bf16[8,16,2048]{2,1,0:T(8,128)(2,1)S(1)}, bf16[8,16,2048]{2,1,0:T(8,128)(2,1)S(1)}, u32[]{:S(2)}, u32[]{:S(2)}) collective-permute-start(bf16[8,16,2048]{2,1,0:T(8,128)(2,1)S(1)} %shard_map.86), channel_id=1, source_target_pairs={{0,192},{8,56},{16,208},{24,40},{32,224},{40,24},{48,240},{56,8},{... | collective-permute-start | bytes 1572872 | tf_op jit(solution)/shard_map/ppermute | solution.py:265
  61.9 3.4 %collective-permute-start.21 = (s16[2,528,512]{2,1,0:T(8,128)(2,1)S(1)}, s16[2,528,512]{2,1,0:T(8,128)(2,1)S(1)}, u32[]{:S(2)}, u32[]{:S(2)}) collective-permute-start(s16[2,528,512]{2,1,0:T(8,128)(2,1)S(1)} %shard_map.101), channel_id=1, source_target_pairs={{0,8},{8,0},{1,9},{9,1},{2,10},{10,2},{3,11},{11,3},{4,12},{12,4},... | collective-permute-start | bytes 3244040 | tf_op jit(solution)/shard_map/ppermute | solution.py:291
  64.7 3.1 %collective-permute-start.18 = (s16[2,528,512]{2,1,0:T(8,128)(2,1)S(1)}, s16[2,528,512]{2,1,0:T(8,128)(2,1)S(1)}, u32[]{:S(2)}, u32[]{:S(2)}) collective-permute-start(s16[2,528,512]{2,1,0:T(8,128)(2,1)S(1)} %shard_map.99), channel_id=1, source_target_pairs={{0,8},{8,0},{1,9},{9,1},{2,10},{10,2},{3,11},{11,3},{4,12},{12,4},... | collective-permute-start | bytes 3244040 | tf_op jit(solution)/shard_map/ppermute | solution.py:291
  65.8 6.6 %collective-permute-start.28 = (s16[272,512]{1,0:T(8,128)(2,1)S(1)}, s16[272,512]{1,0:T(8,128)(2,1)S(1)}, u32[]{:S(2)}, u32[]{:S(2)}) collective-permute-start(s16[272,512]{1,0:T(8,128)(2,1)S(1)} %get-tuple-element.82), channel_id=1, source_target_pairs={{0,16},{8,72},{16,0},{24,88},{32,48},{40,104},{48,32},{56,120},{64... | collective-permute-start | bytes 835592 | tf_op jit(solution)/shard_map/ppermute | solution.py:296
  67.8 6.5 %collective-permute-start.29 = (s16[272,512]{1,0:T(8,128)(2,1)S(1)}, s16[272,512]{1,0:T(8,128)(2,1)S(1)}, u32[]{:S(2)}, u32[]{:S(2)}) collective-permute-start(s16[272,512]{1,0:T(8,128)(2,1)S(1)} %get-tuple-element.83), channel_id=1, source_target_pairs={{0,48},{8,200},{16,32},{24,216},{32,16},{40,232},{48,0},{56,248},{... | collective-permute-start | bytes 835592 | tf_op jit(solution)/shard_map/ppermute | solution.py:296
  68.4 10.3 %collective-permute-start.19 = (s16[272,512]{1,0:T(8,128)(2,1)S(1)}, s16[272,512]{1,0:T(8,128)(2,1)S(1)}, u32[]{:S(2)}, u32[]{:S(2)}) collective-permute-start(s16[272,512]{1,0:T(8,128)(2,1)S(1)} %get-tuple-element.62), channel_id=1, source_target_pairs={{0,16},{8,72},{16,0},{24,88},{32,48},{40,104},{48,32},{56,120},{64... | collective-permute-start | bytes 835592 | tf_op jit(solution)/shard_map/ppermute | solution.py:296
  70.1 8.5 %collective-permute-start.20 = (s16[272,512]{1,0:T(8,128)(2,1)S(1)}, s16[272,512]{1,0:T(8,128)(2,1)S(1)}, u32[]{:S(2)}, u32[]{:S(2)}) collective-permute-start(s16[272,512]{1,0:T(8,128)(2,1)S(1)} %get-tuple-element.63), channel_id=1, source_target_pairs={{0,48},{8,200},{16,32},{24,216},{32,16},{40,232},{48,0},{56,248},{... | collective-permute-start | bytes 835592 | tf_op jit(solution)/shard_map/ppermute | solution.py:296
  74.6 7.4 %collective-permute-start.30 = (s16[144,512]{1,0:T(8,128)(2,1)S(1)}, s16[144,512]{1,0:T(8,128)(2,1)S(1)}, u32[]{:S(2)}, u32[]{:S(2)}) collective-permute-start(s16[144,512]{1,0:T(8,128)(2,1)S(1)} %get-tuple-element.86), channel_id=1, source_target_pairs={{0,48},{8,200},{16,32},{24,216},{32,16},{40,232},{48,0},{56,248},{... | collective-permute-start | bytes 442376 | tf_op jit(solution)/shard_map/ppermute | solution.py:306
  74.7 7.3 %collective-permute-start.31 = (s16[144,512]{1,0:T(8,128)(2,1)S(1)}, s16[144,512]{1,0:T(8,128)(2,1)S(1)}, u32[]{:S(2)}, u32[]{:S(2)}) collective-permute-start(s16[144,512]{1,0:T(8,128)(2,1)S(1)} %get-tuple-element.87), channel_id=1, source_target_pairs={{0,16},{8,72},{16,0},{24,88},{32,48},{40,104},{48,32},{56,120},{64... | collective-permute-start | bytes 442376 | tf_op jit(solution)/shard_map/ppermute | solution.py:306
  78.7 31.3 %copy-start.1 = (f32[32,256]{1,0:T(8,128)S(1)}, f32[32,256]{1,0:T(8,128)}, u32[]{:S(2)}) copy-start(f32[32,256]{1,0:T(8,128)} %shard_map.103) | copy-start | bytes 98308
  79.0 8.0 %collective-permute-start.22 = (s16[144,512]{1,0:T(8,128)(2,1)S(1)}, s16[144,512]{1,0:T(8,128)(2,1)S(1)}, u32[]{:S(2)}, u32[]{:S(2)}) collective-permute-start(s16[144,512]{1,0:T(8,128)(2,1)S(1)} %get-tuple-element.72), channel_id=1, source_target_pairs={{0,48},{8,200},{16,32},{24,216},{32,16},{40,232},{48,0},{56,248},{... | collective-permute-start | bytes 442376 | tf_op jit(solution)/shard_map/ppermute | solution.py:306
  81.4 5.8 %collective-permute-start.23 = (s16[144,512]{1,0:T(8,128)(2,1)S(1)}, s16[144,512]{1,0:T(8,128)(2,1)S(1)}, u32[]{:S(2)}, u32[]{:S(2)}) collective-permute-start(s16[144,512]{1,0:T(8,128)(2,1)S(1)} %get-tuple-element.73), channel_id=1, source_target_pairs={{0,16},{8,72},{16,0},{24,88},{32,48},{40,104},{48,32},{56,120},{64... | collective-permute-start | bytes 442376 | tf_op jit(solution)/shard_map/ppermute | solution.py:306
  82.1 7.8 %collective-permute-start.32 = (f32[32,1024]{1,0:T(8,128)S(1)}, f32[32,1024]{1,0:T(8,128)S(1)}, u32[]{:S(2)}, u32[]{:S(2)}) collective-permute-start(f32[32,1024]{1,0:T(8,128)S(1)} %get-tuple-element.89), channel_id=1, source_target_pairs={{0,64},{8,24},{16,80},{24,8},{32,96},{40,56},{48,112},{56,40},{64,... | collective-permute-start | bytes 393224 | tf_op jit(solution)/shard_map/ppermute | solution.py:310
  82.2 9.8 %collective-permute-start.33 = (f32[32,1024]{1,0:T(8,128)S(1)}, f32[32,1024]{1,0:T(8,128)S(1)}, u32[]{:S(2)}, u32[]{:S(2)}) collective-permute-start(f32[32,1024]{1,0:T(8,128)S(1)} %get-tuple-element.90), channel_id=1, source_target_pairs={{0,128},{8,40},{16,144},{24,56},{32,160},{40,8},{48,176},{56,24},{... | collective-permute-start | bytes 393224 | tf_op jit(solution)/shard_map/ppermute | solution.py:310
  84.7 7.3 %collective-permute-start.34 = (f32[32,1024]{1,0:T(8,128)S(1)}, f32[32,1024]{1,0:T(8,128)S(1)}, u32[]{:S(2)}, u32[]{:S(2)}) collective-permute-start(f32[32,1024]{1,0:T(8,128)S(1)} %get-tuple-element.91), channel_id=1, source_target_pairs={{0,192},{8,56},{16,208},{24,40},{32,224},{40,24},{48,240},{56,8},{... | collective-permute-start | bytes 393224 | tf_op jit(solution)/shard_map/ppermute | solution.py:310
  87.3 9.6 %collective-permute-start.24 = (f32[32,1024]{1,0:T(8,128)S(1)}, f32[32,1024]{1,0:T(8,128)S(1)}, u32[]{:S(2)}, u32[]{:S(2)}) collective-permute-start(f32[32,1024]{1,0:T(8,128)S(1)} %get-tuple-element.75), channel_id=1, source_target_pairs={{0,64},{8,24},{16,80},{24,8},{32,96},{40,56},{48,112},{56,40},{64,... | collective-permute-start | bytes 393224 | tf_op jit(solution)/shard_map/ppermute | solution.py:310
  88.2 8.7 %collective-permute-start.25 = (f32[32,1024]{1,0:T(8,128)S(1)}, f32[32,1024]{1,0:T(8,128)S(1)}, u32[]{:S(2)}, u32[]{:S(2)}) collective-permute-start(f32[32,1024]{1,0:T(8,128)S(1)} %get-tuple-element.76), channel_id=1, source_target_pairs={{0,128},{8,40},{16,144},{24,56},{32,160},{40,8},{48,176},{56,24},{... | collective-permute-start | bytes 393224 | tf_op jit(solution)/shard_map/ppermute | solution.py:310
  89.9 7.0 %collective-permute-start.26 = (f32[32,1024]{1,0:T(8,128)S(1)}, f32[32,1024]{1,0:T(8,128)S(1)}, u32[]{:S(2)}, u32[]{:S(2)}) collective-permute-start(f32[32,1024]{1,0:T(8,128)S(1)} %get-tuple-element.77), channel_id=1, source_target_pairs={{0,192},{8,56},{16,208},{24,40},{32,224},{40,24},{48,240},{56,8},{... | collective-permute-start | bytes 393224 | tf_op jit(solution)/shard_map/ppermute | solution.py:310
  92.1 6.0 %collective-permute-start.35 = (f32[32,512]{1,0:T(8,128)S(1)}, f32[32,512]{1,0:T(8,128)S(1)}, u32[]{:S(2)}, u32[]{:S(2)}) collective-permute-start(f32[32,512]{1,0:T(8,128)S(1)} %get-tuple-element.92), channel_id=1, source_target_pairs={{0,2},{1,3},{2,0},{3,1},{4,6},{5,7},{6,4},{7,5},{8,10},{9,11},{10,... | collective-permute-start | bytes 196616 | tf_op jit(solution)/shard_map/ppermute | solution.py:313
  95.5 6.2 %collective-permute-start.36 = (f32[32,512]{1,0:T(8,128)S(1)}, f32[32,512]{1,0:T(8,128)S(1)}, u32[]{:S(2)}, u32[]{:S(2)}) collective-permute-start(f32[32,512]{1,0:T(8,128)S(1)} %get-tuple-element.93), channel_id=1, source_target_pairs={{0,3},{1,2},{2,1},{3,0},{4,7},{5,6},{6,5},{7,4},{8,11},{9,10},{10,... | collective-permute-start | bytes 196616 | tf_op jit(solution)/shard_map/ppermute | solution.py:313
  96.9 5.1 %collective-permute-start.27 = (f32[32,512]{1,0:T(8,128)S(1)}, f32[32,512]{1,0:T(8,128)S(1)}, u32[]{:S(2)}, u32[]{:S(2)}) collective-permute-start(f32[32,512]{1,0:T(8,128)S(1)} %get-tuple-element.79), channel_id=1, source_target_pairs={{0,1},{1,0},{2,3},{3,2},{4,5},{5,4},{6,7},{7,6},{8,9},{9,8},{10,11... | collective-permute-start | bytes 196616 | tf_op jit(solution)/shard_map/ppermute | solution.py:313
  102.0 8.0 %collective-permute-start.37 = (f32[32,256]{1,0:T(8,128)S(1)}, f32[32,256]{1,0:T(8,128)S(1)}, u32[]{:S(2)}, u32[]{:S(2)}) collective-permute-start(f32[32,256]{1,0:T(8,128)S(1)} %get-tuple-element.95), channel_id=1, source_target_pairs={{0,4},{1,5},{2,6},{3,7},{4,0},{5,1},{6,2},{7,3},{8,12},{9,13},{10,... | collective-permute-start | bytes 98312 | tf_op jit(solution)/shard_map/ppermute | solution.py:316

commit v7 on v6

--- a/solution.py
+++ b/solution.py
@@ -156,12 +156,16 @@
         out_ref[half, :, cols] = out
 
 
-def merge_kernel(home, arrived, far0, far1, near0, near1):
-    n = near0.shape[0]
-    for half, (far, near) in enumerate(((far0, near0), (far1, near1))):
-        other = arrived.at[half]
-        near[...] = home[half, :n] + decode(other, 0, n)
-        encode(home[half, n:] + decode(other, n, n), far, slice(None))
+def far_kernel(home, arrived, far0, far1):
+    n = home.shape[1] // 2
+    for half, far in enumerate((far0, far1)):
+        encode(home[half, n:] + decode(arrived.at[half], n, n), far, slice(None))
+
+
+def near_kernel(home, arrived, after, near0, near1):
+    n = home.shape[1] // 2
+    for half, near in enumerate((near0, near1)):
+        near[...] = home[half, :n] + decode(arrived.at[half], 0, n)
 
 
 def in_vmem(kernel, shapes, *args, scratch=(), limit=24):
@@ -177,11 +181,10 @@
     )(*args)
 
 
-def step_kernel(keep0, keep1, got0, got1, far0, far1, near0, near1):
-    n = near0.shape[0]
-    for keep, got, far, near in ((keep0, got0, far0, near0), (keep1, got1, far1, near1)):
-        near[...] = keep[:n] + decode(got, 0, n)
-        encode(keep[n:] + decode(got, n, n), far, slice(None))
+def step_kernel(keep, got, far, near):
+    n = near.shape[0]
+    near[...] = keep[:n] + decode(got, 0, n)
+    encode(keep[n:] + decode(got, n, n), far, slice(None))
 
 
 def join_kernel(keep0, keep1, got0, got1, *outs):
@@ -230,6 +233,7 @@
         out_shape=jax.ShapeDtypeStruct((rows, columns), jnp.float32),
         in_specs=[pl.BlockSpec(memory_space=pltpu.SMEM)] * len(args),
         out_specs=pl.BlockSpec(memory_space=pltpu.VMEM),
+        compiler_params=pltpu.CompilerParams(vmem_limit_bytes=8 * MIB),
         cost_estimate=pl.CostEstimate(flops=0, bytes_accessed=0, transcendentals=0),
     )(*args)
 
@@ -291,19 +295,19 @@
         arrived.append(lax.ppermute(away, "core", swap))
     keeps, gots = [], []
     for group in range(2):
-        far0, far1, *near = in_vmem(merge_kernel, stage(m // 2), home[group], arrived[group])
-        keeps.append(near)
-        gots.append([lax.ppermute(far, RED, pairs(0, MASKS[h][0])) for h, far in enumerate((far0, far1))])
-    keeps[1], occ_energy = lax.optimization_barrier((keeps[1], occ_energy))
-    gap = energy_gap(
-        rows, columns, occ_index, occ_energy, block_sizes, slab_irrep, virt_energy
-    )
-    gots[0], gap = lax.optimization_barrier((gots[0], gap))
+        fars = in_vmem(far_kernel, stage(m // 2)[:2], home[group], arrived[group])
+        gots.append([lax.ppermute(far, RED, pairs(0, MASKS[h][0])) for h, far in enumerate(fars)])
+        keeps.append(in_vmem(near_kernel, stage(m // 2)[2:], home[group], arrived[group], fars[1]))
     last, more = [], []
     for group in range(2):
-        far0, far1, *near = in_vmem(step_kernel, stage(m // 4), *keeps[group], *gots[group])
-        last.append(near)
-        more.append([lax.ppermute(far, RED, pairs(0, MASKS[h][1])) for h, far in enumerate((far0, far1))])
+        last.append([])
+        more.append([])
+        for half in range(2):
+            far, near = in_vmem(
+                step_kernel, stage(m // 4)[1:3], keeps[group][half], gots[group][half]
+            )
+            last[group].append(near)
+            more[group].append(lax.ppermute(far, RED, pairs(0, MASKS[half][1])))
     blocks = []
     for group in range(2):
         mine, *sends = in_vmem(join_kernel, [((rows, 2 * quarter), jnp.float32)] * 4, *last[group], *more[group])
@@ -314,6 +318,9 @@
     ]
     mine, send = in_vmem(sum_kernel, [((rows, columns), jnp.float32)] * 2, blocks[0], *gots)
     got = lax.ppermute(send, "rep", [(i, i ^ 4) for i in range(N_REP)])
+    gap = energy_gap(
+        rows, columns, occ_index, occ_energy, block_sizes, slab_irrep, virt_energy
+    )
     return (mine + got) / gap
 
 

time: 111 us -> 111 us (level)
  starting transfers between devices: 59.1 us -> 60.4 us
    ppermute x4, waiting for transfers between devices: 0.27 us -> 2.79 us  [body(): more[group].append(lax.ppermute(far, RED, pairs(0, MASKS[half][1])))]
    ppermute x4, waiting for transfers between devices: 3.09 us -> 0.84 us  [body(): lax.ppermute(far, RED, pairs(0, MASKS[h][0]))]
    ppermute x1, waiting for transfers between devices: 2.19 us -> 0.56 us  [body(): got = lax.ppermute(send, 'rep', [(i, i ^ 4) for i in range(N_REP)])]
    ppermute x4, starting transfers between devices: 4.82 us -> 6.3 us  [body(): more[group].append(lax.ppermute(far, RED, pairs(0, MASKS[half][1])))]
    pallas_call x27 -> x31, Pallas kernels: 12.6 us -> 12.5 us  [in_vmem(): pl.pallas_call(kernel, out_shape=[jax.ShapeDtypeStruct(*shape) for shape...]
    unnamed x8 -> x14, local copies, waits for them, and re-layouts: 2.2 us -> 2.22 us
  transfers between devices with their start and end apart: 38 -> 38, of which waited for: 14 -> 15; matrix products, arithmetic and copies ran while one was open for 0% -> 0% of each run, Pallas kernels for 10% -> 10%
where the time goes in v7:
time: 111 us; the launch traced here: 110 us
  starting transfers between devices  60.4 us (54%)
  waiting for transfers between devices  31.3 us (28%)
  Pallas kernels  14.2 us (13%)
  local copies, waits for them, and re-layouts  2.22 us (2%)
  other arithmetic  1.28 us (1%)
    ppermute x16, starting transfers between devices, body(): lax.ppermute(sends[stream][sub], RED, pairs(turn, MASKS[sub][step % 2]))  26.9 us
    ppermute x16, waiting for transfers between devices, body(): lax.ppermute(sends[stream][sub], RED, pairs(turn, MASKS[sub][step % 2]))  22.6 us
    pallas_call x31, Pallas kernels, in_vmem(): pl.pallas_call(kernel, out_shape=[jax.ShapeDtypeStruct(*shape) for shape...  12.5 us
    ppermute x6, starting transfers between devices, body(): lax.ppermute(send, RED, pairs(1, k + 1))  9.56 us
    ppermute x4, starting transfers between devices, body(): more[group].append(lax.ppermute(far, RED, pairs(0, MASKS[half][1])))  6.3 us
    ppermute x1, starting transfers between devices, body(): got = lax.ppermute(send, 'rep', [(i, i ^ 4) for i in range(N_REP)])  5.79 us
    ppermute x3, starting transfers between devices, body(): lax.ppermute(blocks[k], 'rep', [(i, i ^ k) for i in range(N_REP)])  5.34 us
    ppermute x4, starting transfers between devices, body(): lax.ppermute(far, RED, pairs(0, MASKS[h][0]))  5.28 us
  transfers between devices with their start and end apart: 38, of which 15 were waited for; matrix products, arithmetic and copies ran while one was open for 0% of the time, Pallas kernels for 10%

profile of v7, /device:TPU:2, one launch (start us, length us, event | category | flops | bytes accessed | tf_op | source)
XLA Modules:
  0.0 110.4 jit_solution(1796522059429949181)
XLA Ops:
  0.0 0.7 broadcast_multiply_fusion.first_ref
  0.7 2.2 %copy-done = bf16[32,65536]{1,0:T(8,128)(2,1)S(1)} copy-done((bf16[32,65536]{1,0:T(8,128)(2,1)S(1)}, bf16[32,65536]{1,0:T(8,128)(2,1)}, u32[]{:S(2)}) %copy-start) | copy-done | bytes 4194328
  2.8 0.8 shard_map.82
  4.3 1.5 %collective-permute-start.14 = (bf16[8,16,2048]{2,1,0:T(8,128)(2,1)S(1)}, bf16[8,16,2048]{2,1,0:T(8,128)(2,1)S(1)}, u32[]{:S(2)}, u32[]{:S(2)}) collective-permute-start(bf16[8,16,2048]{2,1,0:T(8,128)(2,1)S(1)} %get-tuple-element.50), channel_id=1, source_target_pairs={{0,48},{8,200},{16,32},{24,216},{32,16},{40,232},{48,0},{56,248},{... | collective-permute-start | bytes 1572872 | tf_op jit(solution)/shard_map/ppermute | solution.py:269
  5.8 1.8 %collective-permute-start.10 = (bf16[8,16,2048]{2,1,0:T(8,128)(2,1)S(1)}, bf16[8,16,2048]{2,1,0:T(8,128)(2,1)S(1)}, u32[]{:S(2)}, u32[]{:S(2)}) collective-permute-start(bf16[8,16,2048]{2,1,0:T(8,128)(2,1)S(1)} %get-tuple-element.48), channel_id=1, source_target_pairs={{0,16},{8,72},{16,0},{24,88},{32,48},{40,104},{48,32},{56,120},{64... | collective-permute-start | bytes 1572872 | tf_op jit(solution)/shard_map/ppermute | solution.py:269
  7.6 1.7 %collective-permute-start.6 = (bf16[8,16,2048]{2,1,0:T(8,128)(2,1)S(1)}, bf16[8,16,2048]{2,1,0:T(8,128)(2,1)S(1)}, u32[]{:S(2)}, u32[]{:S(2)}) collective-permute-start(bf16[8,16,2048]{2,1,0:T(8,128)(2,1)S(1)} %shard_map.87), channel_id=1, source_target_pairs={{0,48},{8,200},{16,32},{24,216},{32,16},{40,232},{48,0},{56,248},{... | collective-permute-start | bytes 1572872 | tf_op jit(solution)/shard_map/ppermute | solution.py:269
  9.4 0.7 collective-permute-start.2
  10.0 3.4 %collective-permute-done.14.refs_1_.refs_6_ = bf16[8,16,2048]{2,1,0:T(8,128)(2,1)S(1)} collective-permute-done((bf16[8,16,2048]{2,1,0:T(8,128)(2,1)S(1)}, bf16[8,16,2048]{2,1,0:T(8,128)(2,1)S(1)}, u32[]{:S(2)}, u32[]{:S(2)}) %collective-permute-start.14) | collective-permute-done | bytes 524320 | tf_op jit(solution)/shard_map/ppermute | solution.py:269
  13.5 3.6 %collective-permute-start.15 = (bf16[8,16,2048]{2,1,0:T(8,128)(2,1)S(1)}, bf16[8,16,2048]{2,1,0:T(8,128)(2,1)S(1)}, u32[]{:S(2)}, u32[]{:S(2)}) collective-permute-start(bf16[8,16,2048]{2,1,0:T(8,128)(2,1)S(1)} %shard_map.94), channel_id=1, source_target_pairs={{0,16},{8,72},{16,0},{24,88},{32,48},{40,104},{48,32},{56,120},{64... | collective-permute-start | bytes 1572872 | tf_op jit(solution)/shard_map/ppermute | solution.py:269
  17.1 0.5 collective-permute-start.11
  17.6 1.5 %collective-permute-done.6.refs_1_.refs_6_ = bf16[8,16,2048]{2,1,0:T(8,128)(2,1)S(1)} collective-permute-done((bf16[8,16,2048]{2,1,0:T(8,128)(2,1)S(1)}, bf16[8,16,2048]{2,1,0:T(8,128)(2,1)S(1)}, u32[]{:S(2)}, u32[]{:S(2)}) %collective-permute-start.6) | collective-permute-done | bytes 524320 | tf_op jit(solution)/shard_map/ppermute | solution.py:269
  19.1 3.6 %collective-permute-start.7 = (bf16[8,16,2048]{2,1,0:T(8,128)(2,1)S(1)}, bf16[8,16,2048]{2,1,0:T(8,128)(2,1)S(1)}, u32[]{:S(2)}, u32[]{:S(2)}) collective-permute-start(bf16[8,16,2048]{2,1,0:T(8,128)(2,1)S(1)} %shard_map.88), channel_id=1, source_target_pairs={{0,16},{8,72},{16,0},{24,88},{32,48},{40,104},{48,32},{56,120},{64... | collective-permute-start | bytes 1572872 | tf_op jit(solution)/shard_map/ppermute | solution.py:269
  22.7 0.5 collective-permute-start.3
  23.2 3.0 %collective-permute-done.15.refs_2_.refs_7_ = bf16[8,16,2048]{2,1,0:T(8,128)(2,1)S(1)} collective-permute-done((bf16[8,16,2048]{2,1,0:T(8,128)(2,1)S(1)}, bf16[8,16,2048]{2,1,0:T(8,128)(2,1)S(1)}, u32[]{:S(2)}, u32[]{:S(2)}) %collective-permute-start.15) | collective-permute-done | bytes 524320 | tf_op jit(solution)/shard_map/ppermute | solution.py:269
  26.2 3.1 %collective-permute-start.16 = (bf16[8,16,2048]{2,1,0:T(8,128)(2,1)S(1)}, bf16[8,16,2048]{2,1,0:T(8,128)(2,1)S(1)}, u32[]{:S(2)}, u32[]{:S(2)}) collective-permute-start(bf16[8,16,2048]{2,1,0:T(8,128)(2,1)S(1)} %shard_map.95), channel_id=1, source_target_pairs={{0,192},{8,56},{16,208},{24,40},{32,224},{40,24},{48,240},{56,8},{... | collective-permute-start | bytes 1572872 | tf_op jit(solution)/shard_map/ppermute | solution.py:269
  29.6 3.1 %collective-permute-done.7.refs_2_.refs_7_ = bf16[8,16,2048]{2,1,0:T(8,128)(2,1)S(1)} collective-permute-done((bf16[8,16,2048]{2,1,0:T(8,128)(2,1)S(1)}, bf16[8,16,2048]{2,1,0:T(8,128)(2,1)S(1)}, u32[]{:S(2)}, u32[]{:S(2)}) %collective-permute-start.7) | collective-permute-done | bytes 524320 | tf_op jit(solution)/shard_map/ppermute | solution.py:269
  32.8 5.8 %collective-permute-start.8 = (bf16[8,16,2048]{2,1,0:T(8,128)(2,1)S(1)}, bf16[8,16,2048]{2,1,0:T(8,128)(2,1)S(1)}, u32[]{:S(2)}, u32[]{:S(2)}) collective-permute-start(bf16[8,16,2048]{2,1,0:T(8,128)(2,1)S(1)} %shard_map.89), channel_id=1, source_target_pairs={{0,192},{8,56},{16,208},{24,40},{32,224},{40,24},{48,240},{56,8},{... | collective-permute-start | bytes 1572872 | tf_op jit(solution)/shard_map/ppermute | solution.py:269
  38.8 2.1 %collective-permute-start.17 = (bf16[8,16,2048]{2,1,0:T(8,128)(2,1)S(1)}, bf16[8,16,2048]{2,1,0:T(8,128)(2,1)S(1)}, u32[]{:S(2)}, u32[]{:S(2)}) collective-permute-start(bf16[8,16,2048]{2,1,0:T(8,128)(2,1)S(1)} %shard_map.96), channel_id=1, source_target_pairs={{0,64},{8,24},{16,80},{24,8},{32,96},{40,56},{48,112},{56,40},{64,... | collective-permute-start | bytes 1572872 | tf_op jit(solution)/shard_map/ppermute | solution.py:269
  41.1 4.7 %collective-permute-done.8.refs_3_.refs_8_ = bf16[8,16,2048]{2,1,0:T(8,128)(2,1)S(1)} collective-permute-done((bf16[8,16,2048]{2,1,0:T(8,128)(2,1)S(1)}, bf16[8,16,2048]{2,1,0:T(8,128)(2,1)S(1)}, u32[]{:S(2)}, u32[]{:S(2)}) %collective-permute-start.8) | collective-permute-done | bytes 524320 | tf_op jit(solution)/shard_map/ppermute | solution.py:269
  45.9 2.0 %collective-permute-done.4.refs_3_ = bf16[8,16,2048]{2,1,0:T(8,128)(2,1)S(1)} collective-permute-done((bf16[8,16,2048]{2,1,0:T(8,128)(2,1)S(1)}, bf16[8,16,2048]{2,1,0:T(8,128)(2,1)S(1)}, u32[]{:S(2)}, u32[]{:S(2)}) %collective-permute-start.4) | collective-permute-done | bytes 524320 | tf_op jit(solution)/shard_map/ppermute | solution.py:269
  48.0 1.5 %collective-permute-start.5 = (bf16[8,16,2048]{2,1,0:T(8,128)(2,1)S(1)}, bf16[8,16,2048]{2,1,0:T(8,128)(2,1)S(1)}, u32[]{:S(2)}, u32[]{:S(2)}) collective-permute-start(bf16[8,16,2048]{2,1,0:T(8,128)(2,1)S(1)} %shard_map.86), channel_id=1, source_target_pairs={{0,192},{8,56},{16,208},{24,40},{32,224},{40,24},{48,240},{56,8},{... | collective-permute-start | bytes 1572872 | tf_op jit(solution)/shard_map/ppermute | solution.py:269
  49.5 4.1 %collective-permute-done.17.refs_9_ = bf16[8,16,2048]{2,1,0:T(8,128)(2,1)S(1)} collective-permute-done((bf16[8,16,2048]{2,1,0:T(8,128)(2,1)S(1)}, bf16[8,16,2048]{2,1,0:T(8,128)(2,1)S(1)}, u32[]{:S(2)}, u32[]{:S(2)}) %collective-permute-start.17) | collective-permute-done | bytes 524320 | tf_op jit(solution)/shard_map/ppermute | solution.py:269
  53.6 2.4 %shard_map.98.home = f32[2,512,512]{2,1,0:T(8,128)S(1)} custom-call(bf16[8,16,2048]{2,1,0:T(8,128)(2,1)S(1)} %get-tuple-element.47.refs_0_, bf16[8,16,2048]{2,1,0:T(8,128)(2,1)S(1)} %collective-permute-done.10.refs_1_, bf16[8,16,2048]{2,1,0:T(8,128)(2,1)S(1)} %collective-permute-done.11.refs_2_, bf16[8,16,2048]{2,1,0:T(8,128)(2,1)S(1)} %collective-permute-done.12.refs_3_, ...), custom_call_target="tpu_custom_call" | custom-call | tf_op jit(solution)/shard_map/pallas_call | solution.py:173
  56.0 2.4 %shard_map.97.home = f32[2,512,512]{2,1,0:T(8,128)S(1)} custom-call(bf16[8,16,2048]{2,1,0:T(8,128)(2,1)S(1)} %get-tuple-element.47.refs_0_, bf16[8,16,2048]{2,1,0:T(8,128)(2,1)S(1)} %collective-permute-done.10.refs_1_, bf16[8,16,2048]{2,1,0:T(8,128)(2,1)S(1)} %collective-permute-done.11.refs_2_, bf16[8,16,2048]{2,1,0:T(8,128)(2,1)S(1)} %collective-permute-done.12.refs_3_, ...), custom_call_target="tpu_custom_call" | custom-call | tf_op jit(solution)/shard_map/pallas_call | solution.py:173
  58.3 0.8 collective-permute-done.9.refs_9_
  59.2 2.7 %shard_map.106 = s16[2,528,512]{2,1,0:T(8,128)(2,1)S(1)} custom-call(bf16[16,16,2048]{2,1,0:T(8,128)(2,1)S(1)} %collective-permute-done.refs_0_.refs_5_, bf16[8,16,2048]{2,1,0:T(8,128)(2,1)S(1)} %collective-permute-done.2.refs_1_, bf16[8,16,2048]{2,1,0:T(8,128)(2,1)S(1)} %collective-permute-done.3.refs_2_, ...), custom_call_target="tpu_custom_call" | custom-call | tf_op jit(solution)/shard_map/pallas_call | solution.py:173
  62.0 2.7 %shard_map.99 = s16[2,528,512]{2,1,0:T(8,128)(2,1)S(1)} custom-call(bf16[16,16,2048]{2,1,0:T(8,128)(2,1)S(1)} %collective-permute-done.refs_0_.refs_5_, bf16[8,16,2048]{2,1,0:T(8,128)(2,1)S(1)} %collective-permute-done.2.refs_1_, bf16[8,16,2048]{2,1,0:T(8,128)(2,1)S(1)} %collective-permute-done.3.refs_2_, ...), custom_call_target="tpu_custom_call" | custom-call | tf_op jit(solution)/shard_map/pallas_call | solution.py:173
  64.7 0.6 collective-permute-start.18
  65.7 2.0 %collective-permute-start.28 = (s16[272,512]{1,0:T(8,128)(2,1)S(1)}, s16[272,512]{1,0:T(8,128)(2,1)S(1)}, u32[]{:S(2)}, u32[]{:S(2)}) collective-permute-start(s16[272,512]{1,0:T(8,128)(2,1)S(1)} %get-tuple-element.71), channel_id=1, source_target_pairs={{0,16},{8,72},{16,0},{24,88},{32,48},{40,104},{48,32},{56,120},{64... | collective-permute-start | bytes 835592 | tf_op jit(solution)/shard_map/ppermute | solution.py:299
  68.1 2.6 %collective-permute-start.20 = (s16[272,512]{1,0:T(8,128)(2,1)S(1)}, s16[272,512]{1,0:T(8,128)(2,1)S(1)}, u32[]{:S(2)}, u32[]{:S(2)}) collective-permute-start(s16[272,512]{1,0:T(8,128)(2,1)S(1)} %get-tuple-element.54.after), channel_id=1, source_target_pairs={{0,48},{8,200},{16,32},{24,216},{32,16},{40,232},{48,0},{56,248},{... | collective-permute-start | bytes 835592 | tf_op jit(solution)/shard_map/ppermute | solution.py:299
  70.7 0.6 collective-permute-start.19
  71.4 0.8 collective-permute-done.29.got
  72.4 3.2 %collective-permute-start.31 = (s16[144,512]{1,0:T(8,128)(2,1)S(1)}, s16[144,512]{1,0:T(8,128)(2,1)S(1)}, u32[]{:S(2)}, u32[]{:S(2)}) collective-permute-start(s16[144,512]{1,0:T(8,128)(2,1)S(1)} %get-tuple-element.76), channel_id=1, source_target_pairs={{0,16},{8,72},{16,0},{24,88},{32,48},{40,104},{48,32},{56,120},{64... | collective-permute-start | bytes 442376 | tf_op jit(solution)/shard_map/ppermute | solution.py:310
  76.2 2.6 %collective-permute-start.22 = (s16[144,512]{1,0:T(8,128)(2,1)S(1)}, s16[144,512]{1,0:T(8,128)(2,1)S(1)}, u32[]{:S(2)}, u32[]{:S(2)}) collective-permute-start(s16[144,512]{1,0:T(8,128)(2,1)S(1)} %get-tuple-element.61), channel_id=1, source_target_pairs={{0,16},{8,72},{16,0},{24,88},{32,48},{40,104},{48,32},{56,120},{64... | collective-permute-start | bytes 442376 | tf_op jit(solution)/shard_map/ppermute | solution.py:310
  79.4 1.6 %collective-permute-done.30.got0 = s16[144,512]{1,0:T(8,128)(2,1)S(1)} collective-permute-done((s16[144,512]{1,0:T(8,128)(2,1)S(1)}, s16[144,512]{1,0:T(8,128)(2,1)S(1)}, u32[]{:S(2)}, u32[]{:S(2)}) %collective-permute-start.30) | collective-permute-done | bytes 147488 | tf_op jit(solution)/shard_map/ppermute | solution.py:310
  81.2 2.5 %collective-permute-start.33 = (f32[32,1024]{1,0:T(8,128)S(1)}, f32[32,1024]{1,0:T(8,128)S(1)}, u32[]{:S(2)}, u32[]{:S(2)}) collective-permute-start(f32[32,1024]{1,0:T(8,128)S(1)} %get-tuple-element.79), channel_id=1, source_target_pairs={{0,128},{8,40},{16,144},{24,56},{32,160},{40,8},{48,176},{56,24},{... | collective-permute-start | bytes 393224 | tf_op jit(solution)/shard_map/ppermute | solution.py:314
  83.7 2.2 %collective-permute-start.34 = (f32[32,1024]{1,0:T(8,128)S(1)}, f32[32,1024]{1,0:T(8,128)S(1)}, u32[]{:S(2)}, u32[]{:S(2)}) collective-permute-start(f32[32,1024]{1,0:T(8,128)S(1)} %get-tuple-element.80), channel_id=1, source_target_pairs={{0,192},{8,56},{16,208},{24,40},{32,224},{40,24},{48,240},{56,8},{... | collective-permute-start | bytes 393224 | tf_op jit(solution)/shard_map/ppermute | solution.py:314
  85.8 1.2 %collective-permute-done.21.got0 = s16[144,512]{1,0:T(8,128)(2,1)S(1)} collective-permute-done((s16[144,512]{1,0:T(8,128)(2,1)S(1)}, s16[144,512]{1,0:T(8,128)(2,1)S(1)}, u32[]{:S(2)}, u32[]{:S(2)}) %collective-permute-start.21) | collective-permute-done | bytes 147488 | tf_op jit(solution)/shard_map/ppermute | solution.py:310
  87.3 1.3 %collective-permute-start.24 = (f32[32,1024]{1,0:T(8,128)S(1)}, f32[32,1024]{1,0:T(8,128)S(1)}, u32[]{:S(2)}, u32[]{:S(2)}) collective-permute-start(f32[32,1024]{1,0:T(8,128)S(1)} %get-tuple-element.64), channel_id=1, source_target_pairs={{0,128},{8,40},{16,144},{24,56},{32,160},{40,8},{48,176},{56,24},{... | collective-permute-start | bytes 393224 | tf_op jit(solution)/shard_map/ppermute | solution.py:314
  88.6 3.4 %collective-permute-start.25 = (f32[32,1024]{1,0:T(8,128)S(1)}, f32[32,1024]{1,0:T(8,128)S(1)}, u32[]{:S(2)}, u32[]{:S(2)}) collective-permute-start(f32[32,1024]{1,0:T(8,128)S(1)} %get-tuple-element.65), channel_id=1, source_target_pairs={{0,192},{8,56},{16,208},{24,40},{32,224},{40,24},{48,240},{56,8},{... | collective-permute-start | bytes 393224 | tf_op jit(solution)/shard_map/ppermute | solution.py:314
  92.0 3.3 %collective-permute-start.35 = (f32[32,512]{1,0:T(8,128)S(1)}, f32[32,512]{1,0:T(8,128)S(1)}, u32[]{:S(2)}, u32[]{:S(2)}) collective-permute-start(f32[32,512]{1,0:T(8,128)S(1)} %get-tuple-element.81), channel_id=1, source_target_pairs={{0,2},{1,3},{2,0},{3,1},{4,6},{5,7},{6,4},{7,5},{8,10},{9,11},{10,... | collective-permute-start | bytes 196616 | tf_op jit(solution)/shard_map/ppermute | solution.py:317
  95.3 1.4 %collective-permute-start.36 = (f32[32,512]{1,0:T(8,128)S(1)}, f32[32,512]{1,0:T(8,128)S(1)}, u32[]{:S(2)}, u32[]{:S(2)}) collective-permute-start(f32[32,512]{1,0:T(8,128)S(1)} %get-tuple-element.82), channel_id=1, source_target_pairs={{0,3},{1,2},{2,1},{3,0},{4,7},{5,6},{6,5},{7,4},{8,11},{9,10},{10,... | collective-permute-start | bytes 196616 | tf_op jit(solution)/shard_map/ppermute | solution.py:317
  96.8 0.6 collective-permute-start.26
  97.6 4.0 %collective-permute-done.36.d = f32[32,512]{1,0:T(8,128)S(1)} collective-permute-done((f32[32,512]{1,0:T(8,128)S(1)}, f32[32,512]{1,0:T(8,128)S(1)}, u32[]{:S(2)}, u32[]{:S(2)}) %collective-permute-start.36) | collective-permute-done | bytes 65568 | tf_op jit(solution)/shard_map/ppermute | solution.py:317
  101.9 5.8 %collective-permute-start.37 = (f32[32,256]{1,0:T(8,128)S(1)}, f32[32,256]{1,0:T(8,128)S(1)}, u32[]{:S(2)}, u32[]{:S(2)}) collective-permute-start(f32[32,256]{1,0:T(8,128)S(1)} %get-tuple-element.84), channel_id=1, source_target_pairs={{0,4},{1,5},{2,6},{3,7},{4,0},{5,1},{6,2},{7,3},{8,12},{9,13},{10,... | collective-permute-start | bytes 98312 | tf_op jit(solution)/shard_map/ppermute | solution.py:320
  108.4 0.9 shard_map.114
  109.2 0.6 collective-permute-done.37
  109.8 0.6 add_divide_fusion
  (78 shorter events, 5.0 us)
Async XLA Ops:
  0.7 2.2 %copy-start = (bf16[32,65536]{1,0:T(8,128)(2,1)S(1)}, bf16[32,65536]{1,0:T(8,128)(2,1)}, u32[]{:S(2)}) copy-start(bf16[32,65536]{1,0:T(8,128)(2,1)} %amp_ref.1) | copy-start | bytes 12582916
  3.7 3.9 %collective-permute-start.1 = (bf16[16,16,2048]{2,1,0:T(8,128)(2,1)S(1)}, bf16[16,16,2048]{2,1,0:T(8,128)(2,1)S(1)}, u32[]{:S(2)}, u32[]{:S(2)}) collective-permute-start(bf16[16,16,2048]{2,1,0:T(8,128)(2,1)S(1)} %get-tuple-element.46), channel_id=1, source_target_pairs={{0,8},{8,0},{1,9},{9,1},{2,10},{10,2},{3,11},{11,3},{4,12},{12,4},... | collective-permute-start | bytes 3145736 | tf_op jit(solution)/shard_map/ppermute | solution.py:256
  3.8 13.8 %collective-permute-start = (bf16[16,16,2048]{2,1,0:T(8,128)(2,1)S(1)}, bf16[16,16,2048]{2,1,0:T(8,128)(2,1)S(1)}, u32[]{:S(2)}, u32[]{:S(2)}) collective-permute-start(bf16[16,16,2048]{2,1,0:T(8,128)(2,1)S(1)} %get-tuple-element.45), channel_id=1, source_target_pairs={{0,8},{8,0},{1,9},{9,1},{2,10},{10,2},{3,11},{11,3},{4,12},{12,4},... | collective-permute-start | bytes 3145736 | tf_op jit(solution)/shard_map/ppermute | solution.py:256
  4.3 9.2 %collective-permute-start.14 = (bf16[8,16,2048]{2,1,0:T(8,128)(2,1)S(1)}, bf16[8,16,2048]{2,1,0:T(8,128)(2,1)S(1)}, u32[]{:S(2)}, u32[]{:S(2)}) collective-permute-start(bf16[8,16,2048]{2,1,0:T(8,128)(2,1)S(1)} %get-tuple-element.50), channel_id=1, source_target_pairs={{0,48},{8,200},{16,32},{24,216},{32,16},{40,232},{48,0},{56,248},{... | collective-permute-start | bytes 1572872 | tf_op jit(solution)/shard_map/ppermute | solution.py:269
  5.8 11.3 %collective-permute-start.10 = (bf16[8,16,2048]{2,1,0:T(8,128)(2,1)S(1)}, bf16[8,16,2048]{2,1,0:T(8,128)(2,1)S(1)}, u32[]{:S(2)}, u32[]{:S(2)}) collective-permute-start(bf16[8,16,2048]{2,1,0:T(8,128)(2,1)S(1)} %get-tuple-element.48), channel_id=1, source_target_pairs={{0,16},{8,72},{16,0},{24,88},{32,48},{40,104},{48,32},{56,120},{64... | collective-permute-start | bytes 1572872 | tf_op jit(solution)/shard_map/ppermute | solution.py:269
  7.6 11.5 %collective-permute-start.6 = (bf16[8,16,2048]{2,1,0:T(8,128)(2,1)S(1)}, bf16[8,16,2048]{2,1,0:T(8,128)(2,1)S(1)}, u32[]{:S(2)}, u32[]{:S(2)}) collective-permute-start(bf16[8,16,2048]{2,1,0:T(8,128)(2,1)S(1)} %shard_map.87), channel_id=1, source_target_pairs={{0,48},{8,200},{16,32},{24,216},{32,16},{40,232},{48,0},{56,248},{... | collective-permute-start | bytes 1572872 | tf_op jit(solution)/shard_map/ppermute | solution.py:269
  9.4 13.3 %collective-permute-start.2 = (bf16[8,16,2048]{2,1,0:T(8,128)(2,1)S(1)}, bf16[8,16,2048]{2,1,0:T(8,128)(2,1)S(1)}, u32[]{:S(2)}, u32[]{:S(2)}) collective-permute-start(bf16[8,16,2048]{2,1,0:T(8,128)(2,1)S(1)} %shard_map.83), channel_id=1, source_target_pairs={{0,16},{8,72},{16,0},{24,88},{32,48},{40,104},{48,32},{56,120},{64... | collective-permute-start | bytes 1572872 | tf_op jit(solution)/shard_map/ppermute | solution.py:269
  13.5 12.7 %collective-permute-start.15 = (bf16[8,16,2048]{2,1,0:T(8,128)(2,1)S(1)}, bf16[8,16,2048]{2,1,0:T(8,128)(2,1)S(1)}, u32[]{:S(2)}, u32[]{:S(2)}) collective-permute-start(bf16[8,16,2048]{2,1,0:T(8,128)(2,1)S(1)} %shard_map.94), channel_id=1, source_target_pairs={{0,16},{8,72},{16,0},{24,88},{32,48},{40,104},{48,32},{56,120},{64... | collective-permute-start | bytes 1572872 | tf_op jit(solution)/shard_map/ppermute | solution.py:269
  17.1 12.2 %collective-permute-start.11 = (bf16[8,16,2048]{2,1,0:T(8,128)(2,1)S(1)}, bf16[8,16,2048]{2,1,0:T(8,128)(2,1)S(1)}, u32[]{:S(2)}, u32[]{:S(2)}) collective-permute-start(bf16[8,16,2048]{2,1,0:T(8,128)(2,1)S(1)} %shard_map.91), channel_id=1, source_target_pairs={{0,48},{8,200},{16,32},{24,216},{32,16},{40,232},{48,0},{56,248},{... | collective-permute-start | bytes 1572872 | tf_op jit(solution)/shard_map/ppermute | solution.py:269
  19.1 13.6 %collective-permute-start.7 = (bf16[8,16,2048]{2,1,0:T(8,128)(2,1)S(1)}, bf16[8,16,2048]{2,1,0:T(8,128)(2,1)S(1)}, u32[]{:S(2)}, u32[]{:S(2)}) collective-permute-start(bf16[8,16,2048]{2,1,0:T(8,128)(2,1)S(1)} %shard_map.88), channel_id=1, source_target_pairs={{0,16},{8,72},{16,0},{24,88},{32,48},{40,104},{48,32},{56,120},{64... | collective-permute-start | bytes 1572872 | tf_op jit(solution)/shard_map/ppermute | solution.py:269
  22.7 15.9 %collective-permute-start.3 = (bf16[8,16,2048]{2,1,0:T(8,128)(2,1)S(1)}, bf16[8,16,2048]{2,1,0:T(8,128)(2,1)S(1)}, u32[]{:S(2)}, u32[]{:S(2)}) collective-permute-start(bf16[8,16,2048]{2,1,0:T(8,128)(2,1)S(1)} %shard_map.84), channel_id=1, source_target_pairs={{0,48},{8,200},{16,32},{24,216},{32,16},{40,232},{48,0},{56,248},{... | collective-permute-start | bytes 1572872 | tf_op jit(solution)/shard_map/ppermute | solution.py:269
  26.2 12.5 %collective-permute-start.16 = (bf16[8,16,2048]{2,1,0:T(8,128)(2,1)S(1)}, bf16[8,16,2048]{2,1,0:T(8,128)(2,1)S(1)}, u32[]{:S(2)}, u32[]{:S(2)}) collective-permute-start(bf16[8,16,2048]{2,1,0:T(8,128)(2,1)S(1)} %shard_map.95), channel_id=1, source_target_pairs={{0,192},{8,56},{16,208},{24,40},{32,224},{40,24},{48,240},{56,8},{... | collective-permute-start | bytes 1572872 | tf_op jit(solution)/shard_map/ppermute | solution.py:269
  29.4 11.5 %collective-permute-start.12 = (bf16[8,16,2048]{2,1,0:T(8,128)(2,1)S(1)}, bf16[8,16,2048]{2,1,0:T(8,128)(2,1)S(1)}, u32[]{:S(2)}, u32[]{:S(2)}) collective-permute-start(bf16[8,16,2048]{2,1,0:T(8,128)(2,1)S(1)} %shard_map.92), channel_id=1, source_target_pairs={{0,64},{8,24},{16,80},{24,8},{32,96},{40,56},{48,112},{56,40},{64,... | collective-permute-start | bytes 1572872 | tf_op jit(solution)/shard_map/ppermute | solution.py:269
  32.7 20.8 %slice-start = ((s8[8388608]{0:T(1024)(128)(4,1)}), s8[4194304]{0:T(1024)(128)(4,1)S(1)}, s32[]{:S(2)}) async-start(s8[8388608]{0:T(1024)(128)(4,1)} %bitcast), calls=%async_computation | async-start | bytes 8388608
  32.8 13.0 %collective-permute-start.8 = (bf16[8,16,2048]{2,1,0:T(8,128)(2,1)S(1)}, bf16[8,16,2048]{2,1,0:T(8,128)(2,1)S(1)}, u32[]{:S(2)}, u32[]{:S(2)}) collective-permute-start(bf16[8,16,2048]{2,1,0:T(8,128)(2,1)S(1)} %shard_map.89), channel_id=1, source_target_pairs={{0,192},{8,56},{16,208},{24,40},{32,224},{40,24},{48,240},{56,8},{... | collective-permute-start | bytes 1572872 | tf_op jit(solution)/shard_map/ppermute | solution.py:269
  38.7 9.3 %collective-permute-start.4 = (bf16[8,16,2048]{2,1,0:T(8,128)(2,1)S(1)}, bf16[8,16,2048]{2,1,0:T(8,128)(2,1)S(1)}, u32[]{:S(2)}, u32[]{:S(2)}) collective-permute-start(bf16[8,16,2048]{2,1,0:T(8,128)(2,1)S(1)} %shard_map.85), channel_id=1, source_target_pairs={{0,64},{8,24},{16,80},{24,8},{32,96},{40,56},{48,112},{56,40},{64,... | collective-permute-start | bytes 1572872 | tf_op jit(solution)/shard_map/ppermute | solution.py:269
  38.8 14.7 %slice-start.1 = ((s8[8388608]{0:T(1024)(128)(4,1)}), s8[4194304]{0:T(1024)(128)(4,1)S(1)}, s32[]{:S(2)}) async-start(s8[8388608]{0:T(1024)(128)(4,1)} %bitcast), calls=%async_computation.1 | async-start | bytes 8388608
  38.8 14.7 %collective-permute-start.17 = (bf16[8,16,2048]{2,1,0:T(8,128)(2,1)S(1)}, bf16[8,16,2048]{2,1,0:T(8,128)(2,1)S(1)}, u32[]{:S(2)}, u32[]{:S(2)}) collective-permute-start(bf16[8,16,2048]{2,1,0:T(8,128)(2,1)S(1)} %shard_map.96), channel_id=1, source_target_pairs={{0,64},{8,24},{16,80},{24,8},{32,96},{40,56},{48,112},{56,40},{64,... | collective-permute-start | bytes 1572872 | tf_op jit(solution)/shard_map/ppermute | solution.py:269
  41.0 12.6 %collective-permute-start.13 = (bf16[8,16,2048]{2,1,0:T(8,128)(2,1)S(1)}, bf16[8,16,2048]{2,1,0:T(8,128)(2,1)S(1)}, u32[]{:S(2)}, u32[]{:S(2)}) collective-permute-start(bf16[8,16,2048]{2,1,0:T(8,128)(2,1)S(1)} %shard_map.93), channel_id=1, source_target_pairs={{0,192},{8,56},{16,208},{24,40},{32,224},{40,24},{48,240},{56,8},{... | collective-permute-start | bytes 1572872 | tf_op jit(solution)/shard_map/ppermute | solution.py:269
  45.8 13.3 %collective-permute-start.9 = (bf16[8,16,2048]{2,1,0:T(8,128)(2,1)S(1)}, bf16[8,16,2048]{2,1,0:T(8,128)(2,1)S(1)}, u32[]{:S(2)}, u32[]{:S(2)}) collective-permute-start(bf16[8,16,2048]{2,1,0:T(8,128)(2,1)S(1)} %shard_map.90), channel_id=1, source_target_pairs={{0,64},{8,24},{16,80},{24,8},{32,96},{40,56},{48,112},{56,40},{64,... | collective-permute-start | bytes 1572872 | tf_op jit(solution)/shard_map/ppermute | solution.py:269
  48.0 11.2 %collective-permute-start.5 = (bf16[8,16,2048]{2,1,0:T(8,128)(2,1)S(1)}, bf16[8,16,2048]{2,1,0:T(8,128)(2,1)S(1)}, u32[]{:S(2)}, u32[]{:S(2)}) collective-permute-start(bf16[8,16,2048]{2,1,0:T(8,128)(2,1)S(1)} %shard_map.86), channel_id=1, source_target_pairs={{0,192},{8,56},{16,208},{24,40},{32,224},{40,24},{48,240},{56,8},{... | collective-permute-start | bytes 1572872 | tf_op jit(solution)/shard_map/ppermute | solution.py:269
  61.9 3.4 %collective-permute-start.27 = (s16[2,528,512]{2,1,0:T(8,128)(2,1)S(1)}, s16[2,528,512]{2,1,0:T(8,128)(2,1)S(1)}, u32[]{:S(2)}, u32[]{:S(2)}) collective-permute-start(s16[2,528,512]{2,1,0:T(8,128)(2,1)S(1)} %shard_map.106), channel_id=1, source_target_pairs={{0,8},{8,0},{1,9},{9,1},{2,10},{10,2},{3,11},{11,3},{4,12},{12,4},... | collective-permute-start | bytes 3244040 | tf_op jit(solution)/shard_map/ppermute | solution.py:295
  64.7 3.0 %collective-permute-start.18 = (s16[2,528,512]{2,1,0:T(8,128)(2,1)S(1)}, s16[2,528,512]{2,1,0:T(8,128)(2,1)S(1)}, u32[]{:S(2)}, u32[]{:S(2)}) collective-permute-start(s16[2,528,512]{2,1,0:T(8,128)(2,1)S(1)} %shard_map.99), channel_id=1, source_target_pairs={{0,8},{8,0},{1,9},{9,1},{2,10},{10,2},{3,11},{11,3},{4,12},{12,4},... | collective-permute-start | bytes 3244040 | tf_op jit(solution)/shard_map/ppermute | solution.py:295
  65.6 6.6 %collective-permute-start.29 = (s16[272,512]{1,0:T(8,128)(2,1)S(1)}, s16[272,512]{1,0:T(8,128)(2,1)S(1)}, u32[]{:S(2)}, u32[]{:S(2)}) collective-permute-start(s16[272,512]{1,0:T(8,128)(2,1)S(1)} %get-tuple-element.69.after), channel_id=1, source_target_pairs={{0,48},{8,200},{16,32},{24,216},{32,16},{40,232},{48,0},{56,248},{... | collective-permute-start | bytes 835592 | tf_op jit(solution)/shard_map/ppermute | solution.py:299
  65.7 9.9 %collective-permute-start.28 = (s16[272,512]{1,0:T(8,128)(2,1)S(1)}, s16[272,512]{1,0:T(8,128)(2,1)S(1)}, u32[]{:S(2)}, u32[]{:S(2)}) collective-permute-start(s16[272,512]{1,0:T(8,128)(2,1)S(1)} %get-tuple-element.71), channel_id=1, source_target_pairs={{0,16},{8,72},{16,0},{24,88},{32,48},{40,104},{48,32},{56,120},{64... | collective-permute-start | bytes 835592 | tf_op jit(solution)/shard_map/ppermute | solution.py:299
  68.1 7.9 %collective-permute-start.20 = (s16[272,512]{1,0:T(8,128)(2,1)S(1)}, s16[272,512]{1,0:T(8,128)(2,1)S(1)}, u32[]{:S(2)}, u32[]{:S(2)}) collective-permute-start(s16[272,512]{1,0:T(8,128)(2,1)S(1)} %get-tuple-element.54.after), channel_id=1, source_target_pairs={{0,48},{8,200},{16,32},{24,216},{32,16},{40,232},{48,0},{56,248},{... | collective-permute-start | bytes 835592 | tf_op jit(solution)/shard_map/ppermute | solution.py:299
  70.7 8.1 %collective-permute-start.19 = (s16[272,512]{1,0:T(8,128)(2,1)S(1)}, s16[272,512]{1,0:T(8,128)(2,1)S(1)}, u32[]{:S(2)}, u32[]{:S(2)}) collective-permute-start(s16[272,512]{1,0:T(8,128)(2,1)S(1)} %get-tuple-element.56), channel_id=1, source_target_pairs={{0,16},{8,72},{16,0},{24,88},{32,48},{40,104},{48,32},{56,120},{64... | collective-permute-start | bytes 835592 | tf_op jit(solution)/shard_map/ppermute | solution.py:299
  72.4 7.0 %collective-permute-start.31 = (s16[144,512]{1,0:T(8,128)(2,1)S(1)}, s16[144,512]{1,0:T(8,128)(2,1)S(1)}, u32[]{:S(2)}, u32[]{:S(2)}) collective-permute-start(s16[144,512]{1,0:T(8,128)(2,1)S(1)} %get-tuple-element.76), channel_id=1, source_target_pairs={{0,16},{8,72},{16,0},{24,88},{32,48},{40,104},{48,32},{56,120},{64... | collective-permute-start | bytes 442376 | tf_op jit(solution)/shard_map/ppermute | solution.py:310
  75.7 5.2 %collective-permute-start.30 = (s16[144,512]{1,0:T(8,128)(2,1)S(1)}, s16[144,512]{1,0:T(8,128)(2,1)S(1)}, u32[]{:S(2)}, u32[]{:S(2)}) collective-permute-start(s16[144,512]{1,0:T(8,128)(2,1)S(1)} %get-tuple-element.75), channel_id=1, source_target_pairs={{0,48},{8,200},{16,32},{24,216},{32,16},{40,232},{48,0},{56,248},{... | collective-permute-start | bytes 442376 | tf_op jit(solution)/shard_map/ppermute | solution.py:310
  76.0 32.3 %copy-start.1 = (f32[2048]{0:T(1024)S(1)}, f32[2048]{0:T(1024)}, u32[]{:S(2)}) copy-start(f32[2048]{0:T(1024)} %virt_energy.1) | copy-start | bytes 24580
  76.0 32.3 %copy-start.2 = (s32[4,2,16]{2,1,0:T(2,128)S(1)}, s32[4,2,16]{2,1,0:T(2,128)}, u32[]{:S(2)}) copy-start(s32[4,2,16]{2,1,0:T(2,128)} %occ_index.1) | copy-start | bytes 1540
  76.0 32.3 %copy-start.3 = (f32[125]{0:T(128)S(1)}, f32[125]{0:T(128)}, u32[]{:S(2)}) copy-start(f32[125]{0:T(128)} %occ_energy.1) | copy-start | bytes 1504
  76.0 32.3 %copy-start.4 = (s32[8]{0:T(128)S(1)}, s32[8]{0:T(128)}, u32[]{:S(2)}) copy-start(s32[8]{0:T(128)} %block_sizes.1) | copy-start | bytes 100
  76.2 9.6 %collective-permute-start.22 = (s16[144,512]{1,0:T(8,128)(2,1)S(1)}, s16[144,512]{1,0:T(8,128)(2,1)S(1)}, u32[]{:S(2)}, u32[]{:S(2)}) collective-permute-start(s16[144,512]{1,0:T(8,128)(2,1)S(1)} %get-tuple-element.61), channel_id=1, source_target_pairs={{0,16},{8,72},{16,0},{24,88},{32,48},{40,104},{48,32},{56,120},{64... | collective-permute-start | bytes 442376 | tf_op jit(solution)/shard_map/ppermute | solution.py:310
  79.0 8.1 %collective-permute-start.21 = (s16[144,512]{1,0:T(8,128)(2,1)S(1)}, s16[144,512]{1,0:T(8,128)(2,1)S(1)}, u32[]{:S(2)}, u32[]{:S(2)}) collective-permute-start(s16[144,512]{1,0:T(8,128)(2,1)S(1)} %get-tuple-element.60), channel_id=1, source_target_pairs={{0,48},{8,200},{16,32},{24,216},{32,16},{40,232},{48,0},{56,248},{... | collective-permute-start | bytes 442376 | tf_op jit(solution)/shard_map/ppermute | solution.py:310
  81.1 7.5 %collective-permute-start.32 = (f32[32,1024]{1,0:T(8,128)S(1)}, f32[32,1024]{1,0:T(8,128)S(1)}, u32[]{:S(2)}, u32[]{:S(2)}) collective-permute-start(f32[32,1024]{1,0:T(8,128)S(1)} %get-tuple-element.78), channel_id=1, source_target_pairs={{0,64},{8,24},{16,80},{24,8},{32,96},{40,56},{48,112},{56,40},{64,... | collective-permute-start | bytes 393224 | tf_op jit(solution)/shard_map/ppermute | solution.py:314
  81.2 10.8 %collective-permute-start.33 = (f32[32,1024]{1,0:T(8,128)S(1)}, f32[32,1024]{1,0:T(8,128)S(1)}, u32[]{:S(2)}, u32[]{:S(2)}) collective-permute-start(f32[32,1024]{1,0:T(8,128)S(1)} %get-tuple-element.79), channel_id=1, source_target_pairs={{0,128},{8,40},{16,144},{24,56},{32,160},{40,8},{48,176},{56,24},{... | collective-permute-start | bytes 393224 | tf_op jit(solution)/shard_map/ppermute | solution.py:314
  83.7 8.3 %collective-permute-start.34 = (f32[32,1024]{1,0:T(8,128)S(1)}, f32[32,1024]{1,0:T(8,128)S(1)}, u32[]{:S(2)}, u32[]{:S(2)}) collective-permute-start(f32[32,1024]{1,0:T(8,128)S(1)} %get-tuple-element.80), channel_id=1, source_target_pairs={{0,192},{8,56},{16,208},{24,40},{32,224},{40,24},{48,240},{56,8},{... | collective-permute-start | bytes 393224 | tf_op jit(solution)/shard_map/ppermute | solution.py:314
  87.2 9.6 %collective-permute-start.23 = (f32[32,1024]{1,0:T(8,128)S(1)}, f32[32,1024]{1,0:T(8,128)S(1)}, u32[]{:S(2)}, u32[]{:S(2)}) collective-permute-start(f32[32,1024]{1,0:T(8,128)S(1)} %get-tuple-element.63), channel_id=1, source_target_pairs={{0,64},{8,24},{16,80},{24,8},{32,96},{40,56},{48,112},{56,40},{64,... | collective-permute-start | bytes 393224 | tf_op jit(solution)/shard_map/ppermute | solution.py:314
  87.3 9.5 %collective-permute-start.24 = (f32[32,1024]{1,0:T(8,128)S(1)}, f32[32,1024]{1,0:T(8,128)S(1)}, u32[]{:S(2)}, u32[]{:S(2)}) collective-permute-start(f32[32,1024]{1,0:T(8,128)S(1)} %get-tuple-element.64), channel_id=1, source_target_pairs={{0,128},{8,40},{16,144},{24,56},{32,160},{40,8},{48,176},{56,24},{... | collective-permute-start | bytes 393224 | tf_op jit(solution)/shard_map/ppermute | solution.py:314
  88.6 8.2 %collective-permute-start.25 = (f32[32,1024]{1,0:T(8,128)S(1)}, f32[32,1024]{1,0:T(8,128)S(1)}, u32[]{:S(2)}, u32[]{:S(2)}) collective-permute-start(f32[32,1024]{1,0:T(8,128)S(1)} %get-tuple-element.65), channel_id=1, source_target_pairs={{0,192},{8,56},{16,208},{24,40},{32,224},{40,24},{48,240},{56,8},{... | collective-permute-start | bytes 393224 | tf_op jit(solution)/shard_map/ppermute | solution.py:314
  92.0 5.6 %collective-permute-start.35 = (f32[32,512]{1,0:T(8,128)S(1)}, f32[32,512]{1,0:T(8,128)S(1)}, u32[]{:S(2)}, u32[]{:S(2)}) collective-permute-start(f32[32,512]{1,0:T(8,128)S(1)} %get-tuple-element.81), channel_id=1, source_target_pairs={{0,2},{1,3},{2,0},{3,1},{4,6},{5,7},{6,4},{7,5},{8,10},{9,11},{10,... | collective-permute-start | bytes 196616 | tf_op jit(solution)/shard_map/ppermute | solution.py:317
  95.3 6.2 %collective-permute-start.36 = (f32[32,512]{1,0:T(8,128)S(1)}, f32[32,512]{1,0:T(8,128)S(1)}, u32[]{:S(2)}, u32[]{:S(2)}) collective-permute-start(f32[32,512]{1,0:T(8,128)S(1)} %get-tuple-element.82), channel_id=1, source_target_pairs={{0,3},{1,2},{2,1},{3,0},{4,7},{5,6},{6,5},{7,4},{8,11},{9,10},{10,... | collective-permute-start | bytes 196616 | tf_op jit(solution)/shard_map/ppermute | solution.py:317
  96.8 5.1 %collective-permute-start.26 = (f32[32,512]{1,0:T(8,128)S(1)}, f32[32,512]{1,0:T(8,128)S(1)}, u32[]{:S(2)}, u32[]{:S(2)}) collective-permute-start(f32[32,512]{1,0:T(8,128)S(1)} %get-tuple-element.67), channel_id=1, source_target_pairs={{0,1},{1,0},{2,3},{3,2},{4,5},{5,4},{6,7},{7,6},{8,9},{9,8},{10,11... | collective-permute-start | bytes 196616 | tf_op jit(solution)/shard_map/ppermute | solution.py:317
  101.9 7.9 %collective-permute-start.37 = (f32[32,256]{1,0:T(8,128)S(1)}, f32[32,256]{1,0:T(8,128)S(1)}, u32[]{:S(2)}, u32[]{:S(2)}) collective-permute-start(f32[32,256]{1,0:T(8,128)S(1)} %get-tuple-element.84), channel_id=1, source_target_pairs={{0,4},{1,5},{2,6},{3,7},{4,0},{5,1},{6,2},{7,3},{8,12},{9,13},{10,... | collective-permute-start | bytes 98312 | tf_op jit(solution)/shard_map/ppermute | solution.py:320
